TPU v7x, 128 devices: a whole 4x4x4 slice. The times are simulated.
128 devices in a mesh: node: 8 (over x, z_lo), wide: 16 (over z_hi, y, core).
Axes of the slice: x: 4, y: 4, z: 4 (z_hi: 2, z_lo: 2; z = z_hi * 2 + z_lo), core: 2. Of those that a mesh axis runs over, the one named last changes fastest.
Arguments:
- grad_codes: int32 [16384, 12288], P(('node', 'wide')), may hold values from -8 to 7
- code_scales: float32 [16384, 96], P(('node', 'wide')), may hold values from 0.01 to 0.1
- requant_scales: int32 [8, 16, 16, 96], P('node', 'wide'), may hold values from 2 to 16
- params: float32 [128, 12288], P(('node', 'wide')), may hold values from -4 to 4
- first_moment: float32 [128, 12288], P(('node', 'wide')), may hold values from -3 to 3
- second_moment: float32 [128, 12288], P(('node', 'wide')), may hold values from 0.1 to 2
- step_count: int32 [1], replicated, may hold values from 1 to 32
Outputs:
- update: float32 [128, 12288], P(('node', 'wide'))
- new_first: float32 [128, 12288], P(('node', 'wide'))
- new_second: float32 [128, 12288], P(('node', 'wide'))
Inputs may be any that keep to these rules, and one draw needn't show every extreme that they name: `grad_codes`: 4-bit codes.
All inputs are finite; a program needn't handle non-finite values.
Results may differ from a plain program's by a relative error of at most 0.0035.
Values may be sent and summed in bfloat16 or wider, within the bound.
No kernel may reach another device: no remote copies, remote signals or barrier semaphores. Data moves between devices by JAX's collectives and lax.ppermute only.
A program may use at most 64 MiB of HBM per device.

v0:
```python
import jax
import jax.numpy as jnp
from jax import lax
from jax.sharding import PartitionSpec as P

decay_first = 0.9
decay_second = 0.95
epsilon = 1e-08
weight_decay = 0.1


def dequantize(codes, scales):
    row_count = codes.shape[0]
    blocks = scales.shape[1]
    values = (codes.astype(jnp.float32) + 0.5).reshape(row_count, blocks, 128) * scales[:, :, None]
    return values.reshape(row_count, blocks * 128).astype(jnp.bfloat16)


def requantize(partial_value, scale_two):
    shaped = partial_value.reshape(partial_value.shape[:-1] + (scale_two.shape[-1], 128))
    return jnp.clip(shaped / scale_two[..., None], -8.0, 8.0).astype(jnp.bfloat16)


def restore(requant, scale_two):
    return requant.astype(jnp.float32) * scale_two[..., None]


def adamw(gradient, params, first_moment, second_moment, step_count):
    steps = step_count[0].astype(jnp.float32)
    first = decay_first * first_moment + (1.0 - decay_first) * gradient
    second = decay_second * second_moment + (1.0 - decay_second) * gradient * gradient
    bias_first = 1.0 - jnp.power(jnp.float32(decay_first), steps)
    bias_second = 1.0 - jnp.power(jnp.float32(decay_second), steps)
    update = first / bias_first / (jnp.sqrt(second / bias_second) + epsilon) + weight_decay * params
    return (update, first, second)


def shards(
    grad_codes, code_scales, requant_scales, params, first_moment, second_moment, step_count
):
    node_count = lax.axis_size("node")
    wide_count = lax.axis_size("wide")
    row_count = grad_codes.shape[0]
    columns = grad_codes.shape[1]
    blocks = columns // 128
    owned = params.shape[0]
    block_rows = row_count // node_count
    dequantized = dequantize(grad_codes, code_scales)
    local_scales = requant_scales.reshape(block_rows, blocks).astype(jnp.float32) / 32.0
    received = lax.all_to_all(
        dequantized.reshape(node_count * wide_count, owned, columns),
        ("node", "wide"),
        split_axis=0,
        concat_axis=0,
        tiled=True,
    )
    partials = jnp.sum(
        received.reshape(node_count, wide_count, owned, columns).astype(jnp.float32), axis=0
    )
    their_scales = lax.all_to_all(
        local_scales.astype(jnp.bfloat16).reshape(wide_count, owned, blocks),
        "wide",
        split_axis=0,
        concat_axis=0,
        tiled=True,
    ).astype(jnp.float32)
    terms = restore(requantize(partials, their_scales), their_scales)
    gradient = jnp.sum(terms, axis=0).reshape(owned, columns)
    return adamw(gradient, params, first_moment, second_moment, step_count)


def solution(mesh):
    in_specs = (
        P(("node", "wide"), None),
        P(("node", "wide"), None),
        P("node", "wide", None, None),
        P(("node", "wide"), None),
        P(("node", "wide"), None),
        P(("node", "wide"), None),
        P(),
    )
    out_specs = (P(("node", "wide"), None), P(("node", "wide"), None), P(("node", "wide"), None))
    return jax.shard_map(shards, mesh=mesh, in_specs=in_specs, out_specs=out_specs, check_vma=False)
```

profile of v0, /device:TPU:0, one launch (start us, length us, event | category | flops | bytes accessed | tf_op | source)
XLA Modules:
  0.0 102.9 jit_solution(3383319202096640873)
XLA Ops:
  0.6 0.7 fusion.5
  1.3 0.6 copy.17
  1.9 8.0 %all-to-all-start.1 = ((bf16[16,1,96]{2,1,0:T(2,128)(2,1)}), bf16[16,1,96]{2,1,0:T(2,128)(2,1)S(1)}, u32[]{:S(2)}, u32[]{:S(2)}) async-start(bf16[16,1,96]{2,1,0:T(2,128)(2,1)} %copy.17), calls=%async_computation.1 | async-start | bytes 16384 | tf_op jit(solution)/shard_map/all_to_all | solution.py:60
  9.9 0.9 copy.15
  10.8 0.0 copy-start
  10.8 1.8 %mul.78 = f32[128,96,128]{2,1,0:T(8,128)S(1)} broadcast(f32[128,96]{1,0:T(8,128)S(1)} %copy.15), dimensions={0,1} | broadcast | bytes 6340608 | tf_op jit(solution)/shard_map/mul | solution.py:15
  12.6 1.0 copy-done
  13.6 5.5 %fusion.1 = bf16[128,1,12288]{2,0,1:T(8,128)(2,1)} fusion(f32[16,8,96,128]{3,2,1,0:T(8,128)S(1)} %bitcast.26, s32[128,12288]{1,0:T(8,128)S(1)} %copy-done), kind=kLoop, calls=%fused_computation.2 | loop fusion | flops 6291456 | bytes 15728640 | tf_op jit(solution)/shard_map/reshape | solution.py:51
  19.1 0.5 broadcast.62
  19.7 5.0 %reduce.7 = bf16[128,12288]{1,0:T(8,128)(2,1)S(1)} reduce(bf16[128,1,12288]{2,0,1:T(8,128)(2,1)} %fusion.1, bf16[]{:T(256)} %broadcast.62), dimensions={1}, to_apply=%copy.16.reduce_sub_computation | reduce | bytes 6291458 | tf_op jit(solution)/shard_map/reshape | solution.py:51
  24.7 3.5 %reshape.141 = bf16[128,2,6144]{2,1,0:T(2,128)(2,1)} reshape(bf16[128,12288]{1,0:T(8,128)(2,1)S(1)} %reduce.7) | data formatting | bytes 6291456
  28.2 0.0 all-to-all-done.1
  28.2 10.6 %all-to-all-start = ((bf16[128,2,6144]{2,1,0:T(2,128)(2,1)}), bf16[128,2,6144]{2,1,0:T(2,128)(2,1)S(1)}, u32[]{:S(2)}, u32[]{:S(2)}) async-start(bf16[128,2,6144]{2,1,0:T(2,128)(2,1)} %reshape.141), calls=%async_computation | async-start | bytes 6291456 | tf_op jit(solution)/shard_map/all_to_all | solution.py:50
  39.6 40.6 %all-to-all-done = bf16[128,2,6144]{2,1,0:T(2,128)(2,1)S(1)} async-done(((bf16[128,2,6144]{2,1,0:T(2,128)(2,1)}), bf16[128,2,6144]{2,1,0:T(2,128)(2,1)S(1)}, u32[]{:S(2)}, u32[]{:S(2)}) %all-to-all-start) | async-done | bytes 3145760 | tf_op jit(solution)/shard_map/all_to_all | solution.py:50
  80.2 7.7 %reshape.142 = bf16[128,1,12288]{2,1,0:T(2,128)(2,1)} reshape(bf16[128,2,6144]{2,1,0:T(2,128)(2,1)S(1)} %all-to-all-done) | data formatting | bytes 6291456
  87.9 10.4 %copy.18 = f32[128,1,12288]{2,0,1:T(8,128)} copy(bf16[128,1,12288]{2,1,0:T(2,128)(2,1)} %reshape.142) | data formatting | bytes 9437184
  98.3 0.0 copy-start.1
  98.3 0.0 copy-start.2
  98.3 0.0 copy-start.3
  98.3 3.2 %reduce_sum.22 = f32[16,12288]{1,0:T(8,128)S(1)} reduce(f32[8,16,12288]{2,1,0:T(8,128)} %bitcast.25, f32[]{:T(128)} %constant.8.clone.1), dimensions={0}, to_apply=%region_0.0 | reduce | flops 1376256 | bytes 7077892 | tf_op jit(solution)/shard_map/reduce_sum | solution.py:57
  101.5 0.2 copy.20
  101.6 0.3 multiply_reduce_fusion
  101.9 0.0 copy-done.1
  101.9 0.0 copy-done.2
  102.0 0.0 copy-done.3
  102.0 0.9 multiply_add_fusion
  (1 shorter events, 0.0 us)
Async XLA Ops:
  1.9 26.3 %all-to-all-start.1 = ((bf16[16,1,96]{2,1,0:T(2,128)(2,1)}), bf16[16,1,96]{2,1,0:T(2,128)(2,1)S(1)}, u32[]{:S(2)}, u32[]{:S(2)}) async-start(bf16[16,1,96]{2,1,0:T(2,128)(2,1)} %copy.17), calls=%async_computation.1 | async-start | bytes 16384 | tf_op jit(solution)/shard_map/all_to_all | solution.py:60
  10.8 2.8 %copy-start = (s32[128,12288]{1,0:T(8,128)S(1)}, s32[128,12288]{1,0:T(8,128)}, u32[]{:S(2)}) copy-start(s32[128,12288]{1,0:T(8,128)} %param.7) | copy-start | bytes 18874372
  28.2 51.9 %all-to-all-start = ((bf16[128,2,6144]{2,1,0:T(2,128)(2,1)}), bf16[128,2,6144]{2,1,0:T(2,128)(2,1)S(1)}, u32[]{:S(2)}, u32[]{:S(2)}) async-start(bf16[128,2,6144]{2,1,0:T(2,128)(2,1)} %reshape.141), calls=%async_computation | async-start | bytes 6291456 | tf_op jit(solution)/shard_map/all_to_all | solution.py:50
  98.3 3.6 %copy-start.1 = (f32[1,12288]{1,0:T(1,128)S(1)}, f32[1,12288]{1,0:T(1,128)}, u32[]{:S(2)}) copy-start(f32[1,12288]{1,0:T(1,128)} %param.10) | copy-start | bytes 147460
  98.3 3.7 %copy-start.2 = (f32[1,12288]{1,0:T(1,128)S(1)}, f32[1,12288]{1,0:T(1,128)}, u32[]{:S(2)}) copy-start(f32[1,12288]{1,0:T(1,128)} %param.12) | copy-start | bytes 147460
  98.3 3.7 %copy-start.3 = (f32[1,12288]{1,0:T(1,128)S(1)}, f32[1,12288]{1,0:T(1,128)}, u32[]{:S(2)}) copy-start(f32[1,12288]{1,0:T(1,128)} %param.11) | copy-start | bytes 147460
where the time goes:
time: 104 us; the launch traced here: 103 us
  waiting for transfers between devices  40.6 us (39%)
  local copies, waits for them, and re-layouts  26.6 us (26%)
  starting transfers between devices  18.5 us (18%)
  other arithmetic  15.7 us (15%)
  between operations  1.47 us (1%)
    all_to_all x1, waiting for transfers between devices, shards(): lax.all_to_all(dequantized.reshape(node_count * wide_count, owned, column...  40.6 us
    unnamed x13, local copies, waits for them, and re-layouts  23.7 us
    all_to_all x1, starting transfers between devices, shards(): lax.all_to_all(dequantized.reshape(node_count * wide_count, owned, column...  10.6 us
    reshape x2, other arithmetic, shards(): dequantized.reshape(node_count * wide_count, owned, columns)  10.6 us
    all_to_all x1, starting transfers between devices, shards(): lax.all_to_all(local_scales.astype(jnp.bfloat16).reshape(wide_count, owne...  7.97 us
    reduce_sum x1, other arithmetic, shards(): jnp.sum(received.reshape(node_count, wide_count, owned, columns).astype(j...  3.19 us
  transfers between devices with their start and end apart: 2, of which 1 were waited for; matrix products, arithmetic and copies ran while one was open for 17% of the time, Pallas kernels for 0%

commit v1 on v0

v1 whole, which is shorter than its diff:
```python
import jax
import jax.numpy as jnp
from jax import lax
from jax.experimental import pallas as pl
from jax.experimental.pallas import tpu as pltpu
from jax.sharding import PartitionSpec as P

decay_first = 0.9
decay_second = 0.95
epsilon = 1e-08
weight_decay = 0.1

BLOCKS = 96
LANES = 128
COLUMNS = BLOCKS * LANES
TILE = 16
PIECES = (
    (0, 32, "PQZ", "PQZ"),
    (32, 32, "QZP", "QZP"),
    (64, 32, "ZPQ", "ZPQ"),
)
AXES = ("node", "wide")
VMEM_LIMIT = 32 * 1024 * 1024


def bits(node):
    high = node >> 2
    return {"P": ((node >> 1) & 1) ^ high, "Q": high, "Z": node & 1}


def node_of(label):
    return (label["Q"] << 2) | ((label["P"] ^ label["Q"]) << 1) | label["Z"]


def pairs(dim0, dim1):
    result = []
    for node in range(8):
        for wide in range(16):
            label = bits(node)
            label[dim1 if wide & 1 else dim0] ^= 1
            result.append((node * 16 + wide, node_of(label) * 16 + wide))
    return result


def block_row(piece, relative):
    mine = bits(lax.axis_index("node"))
    core = lax.axis_index("wide") & 1
    label = {}
    for dim in "PQZ":
        flip0 = relative[piece[2].index(dim)]
        flip1 = relative[piece[3].index(dim)]
        label[dim] = mine[dim] ^ (flip0 + core * (flip1 - flip0))
    return pl.multiple_of(node_of(label) * TILE, TILE)


ORDER = ((1, 1), (1, 0), (0, 1), (0, 0))


def dequantize_kernel(parts, codes_ref, scales_ref, *rest):
    outs = rest[: len(parts)]
    scales_buf = rest[len(parts)]
    stage = rest[len(parts) + 1 : -1]
    sem = rest[-1]
    copies = []
    for n, (piece, first) in enumerate(parts):
        for j, tail in enumerate(ORDER):
            row = block_row(piece, (first,) + tail)
            copy = pltpu.make_async_copy(
                codes_ref.at[pl.ds(row, TILE), pl.ds(piece[0] * LANES, piece[1] * LANES)],
                stage[n].at[pl.ds(j * TILE, TILE), :],
                sem.at[n, j],
            )
            copy.start()
            copies.append((n, j, row, copy))
    scales_buf[:, :BLOCKS] = scales_ref[...].T
    for n, j, row, copy in copies:
        piece = parts[n][0]
        scale = scales_buf[pl.ds(row, TILE), :]
        copy.wait()
        for k in range(piece[1]):
            at = piece[0] + k
            codes = stage[n][j * TILE : (j + 1) * TILE, k * LANES : (k + 1) * LANES]
            values = (codes.astype(jnp.float32) + 0.5) * scale[:, at : at + 1]
            outs[n][j * TILE : (j + 1) * TILE, k * LANES : (k + 1) * LANES] = values.astype(jnp.bfloat16)


def dequantize(parts, codes, scales_t):
    shapes = [(4 * TILE, piece[1] * LANES) for piece, _ in parts]
    return pl.pallas_call(
        lambda *refs: dequantize_kernel(parts, *refs),
        out_shape=[jax.ShapeDtypeStruct(s, jnp.bfloat16) for s in shapes],
        in_specs=[pl.BlockSpec(memory_space=pl.ANY), pl.BlockSpec(memory_space=pltpu.VMEM)],
        out_specs=[pl.BlockSpec(memory_space=pltpu.VMEM) for _ in parts],
        scratch_shapes=[pltpu.VMEM((128, LANES), jnp.float32)]
        + [pltpu.VMEM(s, jnp.int32) for s in shapes]
        + [pltpu.SemaphoreType.DMA((len(parts), 4))],
        compiler_params=pltpu.CompilerParams(vmem_limit_bytes=VMEM_LIMIT),
        name="dequantize",
    )(codes, scales_t)


def finish_kernel(requant_ref, *refs):
    count = len(PIECES)
    keeps, firsts, seconds, thirds = (refs[i * count : (i + 1) * count] for i in range(4))
    send_ref, keep_ref, rows = refs[4 * count :]
    numerators = requant_ref[...].astype(jnp.float32)
    scale = numerators * (1.0 / 32.0)
    inverse = 32.0 / numerators
    for n, piece in enumerate(PIECES):
        for k in range(piece[1]):
            cut = pl.ds(k * LANES, LANES)
            at = piece[0] + k
            partial = (
                keeps[n][3 * TILE : 4 * TILE, cut].astype(jnp.float32)
                + firsts[n][3 * TILE : 4 * TILE, cut].astype(jnp.float32)
            ) + (seconds[n][TILE : 2 * TILE, cut].astype(jnp.float32) + thirds[n][:, cut].astype(jnp.float32))
            coded = jnp.clip(partial * inverse[:, at : at + 1], -8.0, 8.0).astype(jnp.bfloat16)
            rows[pl.ds(at, TILE, stride=BLOCKS), :] = coded.astype(jnp.float32) * scale[:, at : at + 1]
    core = lax.axis_index("wide") & 1
    for j in range(8):
        other = pl.multiple_of((2 * j + 1 - core) * BLOCKS, 8)
        own = pl.multiple_of((2 * j + core) * BLOCKS, 8)
        send_ref[j] = rows[pl.ds(other, BLOCKS), :].astype(jnp.bfloat16)
        keep_ref[j] = rows[pl.ds(own, BLOCKS), :]


def finish(requant, keeps, firsts, seconds, thirds):
    vmem = pl.BlockSpec(memory_space=pltpu.VMEM)
    return pl.pallas_call(
        finish_kernel,
        out_shape=[
            jax.ShapeDtypeStruct((8, BLOCKS, LANES), jnp.bfloat16),
            jax.ShapeDtypeStruct((8, BLOCKS, LANES), jnp.float32),
        ],
        in_specs=[vmem] * (1 + 4 * len(PIECES)),
        out_specs=[vmem, vmem],
        scratch_shapes=[pltpu.VMEM((TILE * BLOCKS, LANES), jnp.float32)],
        compiler_params=pltpu.CompilerParams(vmem_limit_bytes=VMEM_LIMIT),
        name="finish",
    )(requant, *keeps, *firsts, *seconds, *thirds)


def adamw_kernel(bias_ref, terms_ref, params_ref, first_ref, second_ref, update_out, first_out, second_out):
    gradient = terms_ref[0].astype(jnp.float32)
    for j in range(1, 8):
        gradient = gradient + terms_ref[j].astype(jnp.float32)
    first = decay_first * first_ref[...] + (1.0 - decay_first) * gradient
    second = decay_second * second_ref[...] + (1.0 - decay_second) * gradient * gradient
    update_out[...] = (
        first / bias_ref[0] / (jnp.sqrt(second / bias_ref[1]) + epsilon) + weight_decay * params_ref[...]
    )
    first_out[...] = first
    second_out[...] = second


def adamw(bias, terms, params, first_moment, second_moment):
    vmem = pl.BlockSpec(memory_space=pltpu.VMEM)
    return pl.pallas_call(
        adamw_kernel,
        out_shape=[jax.ShapeDtypeStruct((BLOCKS, LANES), jnp.float32)] * 3,
        in_specs=[pl.BlockSpec(memory_space=pltpu.SMEM)] + [vmem] * 4,
        out_specs=[vmem] * 3,
        name="adamw",
    )(bias, terms, params, first_moment, second_moment)


def shards(grad_codes, code_scales, requant_scales, params, first_moment, second_moment, step_count):
    scales_t = code_scales.T
    firsts, seconds, thirds = [], [], []
    for piece in PIECES:
        (send,) = dequantize([(piece, 1)], grad_codes, scales_t)
        firsts.append(lax.ppermute(send, AXES, pairs(piece[2][0], piece[3][0])))
    keeps = dequantize([(piece, 0) for piece in PIECES], grad_codes, scales_t)
    for n, piece in enumerate(PIECES):
        send = firsts[n][: 2 * TILE].astype(jnp.float32) + keeps[n][: 2 * TILE].astype(jnp.float32)
        seconds.append(lax.ppermute(send.astype(jnp.bfloat16), AXES, pairs(piece[2][1], piece[3][1])))
    for n, piece in enumerate(PIECES):
        send = (
            firsts[n][2 * TILE : 3 * TILE].astype(jnp.float32)
            + keeps[n][2 * TILE : 3 * TILE].astype(jnp.float32)
            + seconds[n][:TILE].astype(jnp.float32)
        )
        thirds.append(lax.ppermute(send.astype(jnp.bfloat16), AXES, pairs(piece[2][2], piece[3][2])))
    send, keep = finish(requant_scales.reshape(TILE, BLOCKS), keeps, firsts, seconds, thirds)
    other = lax.ppermute(send, "wide", [(b, b ^ 1) for b in range(16)])
    terms = (keep + other.astype(jnp.float32)).astype(jnp.bfloat16)
    groups = [[2 * j + core for j in range(8)] for core in range(2)]
    terms = lax.all_to_all(terms, "wide", 0, 0, tiled=True, axis_index_groups=groups)
    steps = step_count.astype(jnp.float32)
    bias = jnp.concatenate(
        [1.0 - jnp.power(jnp.float32(decay_first), steps), 1.0 - jnp.power(jnp.float32(decay_second), steps)]
    )
    tall = (BLOCKS, LANES)
    outs = adamw(bias, terms, params.reshape(tall), first_moment.reshape(tall), second_moment.reshape(tall))
    return tuple(out.reshape(1, COLUMNS) for out in outs)


def solution(mesh):
    in_specs = (
        P(("node", "wide"), None),
        P(("node", "wide"), None),
        P("node", "wide", None, None),
        P(("node", "wide"), None),
        P(("node", "wide"), None),
        P(("node", "wide"), None),
        P(),
    )
    out_specs = (P(("node", "wide"), None), P(("node", "wide"), None), P(("node", "wide"), None))
    return jax.shard_map(shards, mesh=mesh, in_specs=in_specs, out_specs=out_specs, check_vma=False)
```

time: 104 us -> 60.1 us (0.58)
  local copies, waits for them, and re-layouts: 26.6 us -> 4.27 us
  waiting for transfers between devices: 40.6 us -> 19.7 us
  other arithmetic: 15.7 us -> 1.69 us
  Pallas kernels: 0 us -> 7.89 us
  starting transfers between devices: 18.5 us -> 24.7 us
    all_to_all x2 -> x1, waiting for transfers between devices: 40.6 us -> 7.08 us  [shards(): lax.all_to_all(terms, 'wide', 0, 0, tiled=True, axis_index_groups=groups)]
    unnamed x13 -> x8, local copies, waits for them, and re-layouts: 23.7 us -> 4.27 us
    ppermute x0 -> x10, starting transfers between devices: none -> 17 us  [the longest x3 5.82 us: shards(): firsts.append(lax.ppermute(send, AXES, pairs(piece[2][0], piece[3][0])))]
    ppermute x0 -> x10, waiting for transfers between devices: none -> 12.6 us  [the longest x3 4.53 us: shards(): firsts.append(lax.ppermute(send, AXES, pairs(piece[2][0], piece[3][0])))]
    all_to_all x2 -> x1, starting transfers between devices: 18.5 us -> 7.74 us  [shards(): lax.all_to_all(terms, 'wide', 0, 0, tiled=True, axis_index_groups=groups)]
    reshape x2 -> x0, other arithmetic: 10.6 us -> none  [shards(): dequantized.reshape(node_count * wide_count, owned, columns)]
    pallas_call x0 -> x6, Pallas kernels: none -> 7.89 us  [the longest x4 5.26 us: dequantize(): pl.pallas_call(lambda *refs: dequantize_kernel(parts, *refs), out_shape=[...]
    reduce_sum x2 -> x0, other arithmetic: 3.46 us -> none  [the longest x1 3.19 us: shards(): jnp.sum(received.reshape(node_count, wide_count, owned, columns).astype(j...]
  transfers between devices with their start and end apart: 2 -> 11, of which waited for: 1 -> 8; matrix products, arithmetic and copies ran while one was open for 17% -> 2% of each run, Pallas kernels for 0% -> 7%
where the time goes in v1:
time: 60.1 us; the launch traced here: 59.8 us
  starting transfers between devices  24.7 us (41%)
  waiting for transfers between devices  19.7 us (33%)
  Pallas kernels  7.89 us (13%)
  local copies, waits for them, and re-layouts  4.27 us (7%)
  other arithmetic  1.69 us (3%)
  between operations  1.47 us (2%)
    all_to_all x1, starting transfers between devices, shards(): lax.all_to_all(terms, 'wide', 0, 0, tiled=True, axis_index_groups=groups)  7.74 us
    all_to_all x1, waiting for transfers between devices, shards(): lax.all_to_all(terms, 'wide', 0, 0, tiled=True, axis_index_groups=groups)  7.08 us
    ppermute x3, starting transfers between devices, shards(): firsts.append(lax.ppermute(send, AXES, pairs(piece[2][0], piece[3][0])))  5.82 us
    ppermute x3, starting transfers between devices, shards(): lax.ppermute(send.astype(jnp.bfloat16), AXES, pairs(piece[2][2], piece[3]...  5.57 us
    ppermute x3, starting transfers between devices, shards(): lax.ppermute(send.astype(jnp.bfloat16), AXES, pairs(piece[2][1], piece[3]...  5.53 us
    pallas_call x4, Pallas kernels, dequantize(): pl.pallas_call(lambda *refs: dequantize_kernel(parts, *refs), out_shape=[...  5.26 us
    ppermute x3, waiting for transfers between devices, shards(): firsts.append(lax.ppermute(send, AXES, pairs(piece[2][0], piece[3][0])))  4.53 us
    unnamed x8, local copies, waits for them, and re-layouts  4.27 us
  transfers between devices with their start and end apart: 11, of which 8 were waited for; matrix products, arithmetic and copies ran while one was open for 2% of the time, Pallas kernels for 7%

profile of v1, /device:TPU:0, one launch (start us, length us, event | category | flops | bytes accessed | tf_op | source)
XLA Modules:
  0.0 59.8 jit_solution(7469626643248024398)
XLA Ops:
  0.6 0.0 copy-start
  0.6 2.8 %copy-done = s32[128,12288]{1,0:T(8,128)S(1)} copy-done((s32[128,12288]{1,0:T(8,128)S(1)}, s32[128,12288]{1,0:T(8,128)}, u32[]{:S(2)}) %copy-start) | copy-done | bytes 6291480
  3.4 0.0 copy-start.1
  3.4 0.8 %copy-done.1 = f32[128,96]{0,1:T(8,128)S(1)} copy-done((f32[128,96]{0,1:T(8,128)S(1)}, f32[128,96]{0,1:T(8,128)}, u32[]{:S(2)}) %copy-start.1) | copy-done | bytes 49176
  4.2 0.9 %dequantize.5 = bf16[64,4096]{1,0:T(8,128)(2,1)S(1)} custom-call(s32[128,12288]{1,0:T(8,128)S(1)} %copy-done, f32[96,128]{1,0:T(8,128)S(1)} %bitcast.8), custom_call_target="tpu_custom_call" | custom-call | tf_op jit(solution)/shard_map/dequantize/pallas_call | solution.py:89
  5.1 1.7 %collective-permute-start = (bf16[64,4096]{1,0:T(8,128)(2,1)S(1)}, bf16[64,4096]{1,0:T(8,128)(2,1)S(1)}, u32[]{:S(2)}, u32[]{:S(2)}) collective-permute-start(bf16[64,4096]{1,0:T(8,128)(2,1)S(1)} %dequantize.5), channel_id=1, source_target_pairs={{0,32},{1,33},{2,34},{3,35},{4,36},{5,37},{6,38},{7,39},{8,40},{9,... | collective-permute-start | bytes 1572872 | tf_op jit(solution)/shard_map/ppermute | solution.py:172
  6.8 0.9 %dequantize.6 = bf16[64,4096]{1,0:T(8,128)(2,1)S(1)} custom-call(s32[128,12288]{1,0:T(8,128)S(1)} %copy-done, f32[96,128]{1,0:T(8,128)S(1)} %bitcast.9), custom_call_target="tpu_custom_call" | custom-call | tf_op jit(solution)/shard_map/dequantize/pallas_call | solution.py:89
  7.7 2.2 %collective-permute-start.1 = (bf16[64,4096]{1,0:T(8,128)(2,1)S(1)}, bf16[64,4096]{1,0:T(8,128)(2,1)S(1)}, u32[]{:S(2)}, u32[]{:S(2)}) collective-permute-start(bf16[64,4096]{1,0:T(8,128)(2,1)S(1)} %dequantize.6), channel_id=1, source_target_pairs={{0,96},{1,97},{2,98},{3,99},{4,100},{5,101},{6,102},{7,103},{8,104... | collective-permute-start | bytes 1572872 | tf_op jit(solution)/shard_map/ppermute | solution.py:172
  9.9 0.9 %dequantize.7 = bf16[64,4096]{1,0:T(8,128)(2,1)S(1)} custom-call(s32[128,12288]{1,0:T(8,128)S(1)} %copy-done, f32[96,128]{1,0:T(8,128)S(1)} %bitcast.10), custom_call_target="tpu_custom_call" | custom-call | tf_op jit(solution)/shard_map/dequantize/pallas_call | solution.py:89
  10.8 0.0 copy-start.2
  10.8 2.0 %collective-permute-start.2 = (bf16[64,4096]{1,0:T(8,128)(2,1)S(1)}, bf16[64,4096]{1,0:T(8,128)(2,1)S(1)}, u32[]{:S(2)}, u32[]{:S(2)}) collective-permute-start(bf16[64,4096]{1,0:T(8,128)(2,1)S(1)} %dequantize.7), channel_id=1, source_target_pairs={{0,16},{1,17},{2,18},{3,19},{4,20},{5,21},{6,22},{7,23},{8,24},{9,... | collective-permute-start | bytes 1572872 | tf_op jit(solution)/shard_map/ppermute | solution.py:172
  12.8 2.5 %dequantize.4 = (bf16[64,4096]{1,0:T(8,128)(2,1)S(1)}, bf16[64,4096]{1,0:T(8,128)(2,1)S(1)}, bf16[64,4096]{1,0:T(8,128)(2,1)S(1)}) custom-call(s32[128,12288]{1,0:T(8,128)S(1)} %copy-done, f32[96,128]{1,0:T(8,128)S(1)} %bitcast.11), custom_call_target="tpu_custom_call" | custom-call | tf_op jit(solution)/shard_map/dequantize/pallas_call | solution.py:89
  15.3 3.4 %collective-permute-done.refs_3_ = bf16[64,4096]{1,0:T(8,128)(2,1)S(1)} collective-permute-done((bf16[64,4096]{1,0:T(8,128)(2,1)S(1)}, bf16[64,4096]{1,0:T(8,128)(2,1)S(1)}, u32[]{:S(2)}, u32[]{:S(2)}) %collective-permute-start) | collective-permute-done | bytes 524320 | tf_op jit(solution)/shard_map/ppermute | solution.py:172
  18.7 0.1 add_convert_fusion.2
  18.8 3.1 %collective-permute-start.3 = (bf16[32,4096]{1,0:T(8,128)(2,1)S(1)}, bf16[32,4096]{1,0:T(8,128)(2,1)S(1)}, u32[]{:S(2)}, u32[]{:S(2)}) collective-permute-start(bf16[32,4096]{1,0:T(8,128)(2,1)S(1)} %add_convert_fusion.2), channel_id=1, source_target_pairs={{0,96},{1,97},{2,98},{3,99},{4,100},{5,101},{6,102},{7,103},{8,104... | collective-permute-start | bytes 786440 | tf_op jit(solution)/shard_map/ppermute | solution.py:176
  21.9 1.2 %collective-permute-done.1.refs_4_ = bf16[64,4096]{1,0:T(8,128)(2,1)S(1)} collective-permute-done((bf16[64,4096]{1,0:T(8,128)(2,1)S(1)}, bf16[64,4096]{1,0:T(8,128)(2,1)S(1)}, u32[]{:S(2)}, u32[]{:S(2)}) %collective-permute-start.1) | collective-permute-done | bytes 524320 | tf_op jit(solution)/shard_map/ppermute | solution.py:172
  23.0 0.1 add_convert_fusion.1
  23.1 1.8 %collective-permute-start.4 = (bf16[32,4096]{1,0:T(8,128)(2,1)S(1)}, bf16[32,4096]{1,0:T(8,128)(2,1)S(1)}, u32[]{:S(2)}, u32[]{:S(2)}) collective-permute-start(bf16[32,4096]{1,0:T(8,128)(2,1)S(1)} %add_convert_fusion.1), channel_id=1, source_target_pairs={{0,16},{1,17},{2,18},{3,19},{4,20},{5,21},{6,22},{7,23},{8,24},{9,... | collective-permute-start | bytes 786440 | tf_op jit(solution)/shard_map/ppermute | solution.py:176
  24.9 0.0 collective-permute-done.2.refs_5_
  24.9 0.1 add_convert_fusion
  24.9 0.7 %collective-permute-start.5 = (bf16[32,4096]{1,0:T(8,128)(2,1)S(1)}, bf16[32,4096]{1,0:T(8,128)(2,1)S(1)}, u32[]{:S(2)}, u32[]{:S(2)}) collective-permute-start(bf16[32,4096]{1,0:T(8,128)(2,1)S(1)} %add_convert_fusion), channel_id=1, source_target_pairs={{0,32},{1,33},{2,34},{3,35},{4,36},{5,37},{6,38},{7,39},{8,40},{9,... | collective-permute-start | bytes 786440 | tf_op jit(solution)/shard_map/ppermute | solution.py:176
  25.6 2.4 %collective-permute-done.3.refs_6_ = bf16[32,4096]{1,0:T(8,128)(2,1)S(1)} collective-permute-done((bf16[32,4096]{1,0:T(8,128)(2,1)S(1)}, bf16[32,4096]{1,0:T(8,128)(2,1)S(1)}, u32[]{:S(2)}, u32[]{:S(2)}) %collective-permute-start.3) | collective-permute-done | bytes 262176 | tf_op jit(solution)/shard_map/ppermute | solution.py:176
  28.0 0.1 add_convert_fusion.6
  28.1 2.0 %collective-permute-start.6 = (bf16[16,4096]{1,0:T(8,128)(2,1)S(1)}, bf16[16,4096]{1,0:T(8,128)(2,1)S(1)}, u32[]{:S(2)}, u32[]{:S(2)}) collective-permute-start(bf16[16,4096]{1,0:T(8,128)(2,1)S(1)} %add_convert_fusion.6), channel_id=1, source_target_pairs={{0,16},{1,17},{2,18},{3,19},{4,20},{5,21},{6,22},{7,23},{8,24},{9,... | collective-permute-start | bytes 393224 | tf_op jit(solution)/shard_map/ppermute | solution.py:183
  30.0 0.0 collective-permute-done.4.refs_7_
  30.0 0.1 add_convert_fusion.5
  30.1 1.5 %collective-permute-start.7 = (bf16[16,4096]{1,0:T(8,128)(2,1)S(1)}, bf16[16,4096]{1,0:T(8,128)(2,1)S(1)}, u32[]{:S(2)}, u32[]{:S(2)}) collective-permute-start(bf16[16,4096]{1,0:T(8,128)(2,1)S(1)} %add_convert_fusion.5), channel_id=1, source_target_pairs={{0,32},{1,33},{2,34},{3,35},{4,36},{5,37},{6,38},{7,39},{8,40},{9,... | collective-permute-start | bytes 393224 | tf_op jit(solution)/shard_map/ppermute | solution.py:183
  31.6 0.1 collective-permute-done.5.refs_8_
  31.7 0.1 add_convert_fusion.4
  31.7 2.0 %collective-permute-start.8 = (bf16[16,4096]{1,0:T(8,128)(2,1)S(1)}, bf16[16,4096]{1,0:T(8,128)(2,1)S(1)}, u32[]{:S(2)}, u32[]{:S(2)}) collective-permute-start(bf16[16,4096]{1,0:T(8,128)(2,1)S(1)} %add_convert_fusion.4), channel_id=1, source_target_pairs={{0,96},{1,97},{2,98},{3,99},{4,100},{5,101},{6,102},{7,103},{8,104... | collective-permute-start | bytes 393224 | tf_op jit(solution)/shard_map/ppermute | solution.py:183
  33.8 0.0 collective-permute-done.6.refs_9_
  33.8 1.4 %collective-permute-done.7.refs_10_ = bf16[16,4096]{1,0:T(8,128)(2,1)S(1)} collective-permute-done((bf16[16,4096]{1,0:T(8,128)(2,1)S(1)}, bf16[16,4096]{1,0:T(8,128)(2,1)S(1)}, u32[]{:S(2)}, u32[]{:S(2)}) %collective-permute-start.7) | collective-permute-done | bytes 131104 | tf_op jit(solution)/shard_map/ppermute | solution.py:183
  35.2 2.9 %collective-permute-done.8.refs_11_ = bf16[16,4096]{1,0:T(8,128)(2,1)S(1)} collective-permute-done((bf16[16,4096]{1,0:T(8,128)(2,1)S(1)}, bf16[16,4096]{1,0:T(8,128)(2,1)S(1)}, u32[]{:S(2)}, u32[]{:S(2)}) %collective-permute-start.8) | collective-permute-done | bytes 131104 | tf_op jit(solution)/shard_map/ppermute | solution.py:183
  38.0 0.0 copy-done.2
  38.0 1.0 %finish.1 = (bf16[8,96,128]{2,1,0:T(8,128)(2,1)S(1)}, f32[8,96,128]{2,1,0:T(8,128)S(1)}) custom-call(s32[16,96]{1,0:T(8,128)S(1)} %bitcast.12, bf16[64,4096]{1,0:T(8,128)(2,1)S(1)} %get-tuple-element.11.refs_0_, bf16[64,4096]{1,0:T(8,128)(2,1)S(1)} %get-tuple-element.12.refs_1_, bf16[64,4096]{1,0:T(8,128)(2,1)S(1)} %get-tuple-element.13.refs_2_, ...), custom_call_target="tpu_custom_call" | custom-call | tf_op jit(solution)/shard_map/finish/pallas_call | solution.py:129
  39.0 0.1 collective-permute-start.9
  39.1 1.4 %collective-permute-done.9 = bf16[8,96,128]{2,1,0:T(8,128)(2,1)S(1)} collective-permute-done((bf16[8,96,128]{2,1,0:T(8,128)(2,1)S(1)}, bf16[8,96,128]{2,1,0:T(8,128)(2,1)S(1)}, u32[]{:S(2)}, u32[]{:S(2)}) %collective-permute-start.9) | collective-permute-done | bytes 196640 | tf_op jit(solution)/shard_map/ppermute | solution.py:185
  40.5 0.7 %add_convert_fusion.3 = bf16[8,96,128]{2,1,0:T(8,128)(2,1)} fusion(f32[8,96,128]{2,1,0:T(8,128)S(1)} %get-tuple-element.14, bf16[8,96,128]{2,1,0:T(8,128)(2,1)S(1)} %collective-permute-done.9), kind=kLoop, calls=%fused_computation.3 | loop fusion | flops 294912 | bytes 786432 | tf_op jit(solution)/shard_map/convert_element_type | solution.py:186
  41.2 7.7 %all-to-all-start = ((bf16[8,96,128]{2,1,0:T(8,128)(2,1)}), bf16[8,96,128]{2,1,0:T(8,128)(2,1)S(1)}, u32[]{:S(2)}, u32[]{:S(2)}) async-start(bf16[8,96,128]{2,1,0:T(8,128)(2,1)} %add_convert_fusion.3), calls=%async_computation | async-start | bytes 393216 | tf_op jit(solution)/shard_map/all_to_all | solution.py:188
  49.7 0.6 %pad_maximum_fusion.bias_ref = f32[2]{0:T(128)} fusion(f32[1]{0:T(128)S(6)} %sub.7, f32[1]{0:T(128)S(6)} %sub.6), kind=kLoop, calls=%fused_computation.7 | loop fusion | flops 2 | bytes 16 | tf_op jit(solution)/shard_map/concatenate | solution.py:190
  50.3 7.1 %all-to-all-done.terms_ref = bf16[8,96,128]{2,1,0:T(8,128)(2,1)S(1)} async-done(((bf16[8,96,128]{2,1,0:T(8,128)(2,1)}), bf16[8,96,128]{2,1,0:T(8,128)(2,1)S(1)}, u32[]{:S(2)}, u32[]{:S(2)}) %all-to-all-start) | async-done | bytes 196640 | tf_op jit(solution)/shard_map/all_to_all | solution.py:188
  57.4 0.0 copy-start.3
  57.4 0.7 %copy-done.3 = bf16[8,96,128]{2,1,0:T(8,128)(2,1)} copy-done((bf16[8,96,128]{2,1,0:T(8,128)(2,1)}, bf16[8,96,128]{2,1,0:T(8,128)(2,1)S(1)}, u32[]{:S(2)}) %copy-start.3) | copy-done | bytes 196632
  58.1 1.7 %adamw.1 = (f32[96,128]{1,0:T(8,128)}, f32[96,128]{1,0:T(8,128)}, f32[96,128]{1,0:T(8,128)}) custom-call(f32[2]{0:T(128)} %pad_maximum_fusion.bias_ref, bf16[8,96,128]{2,1,0:T(8,128)(2,1)} %copy-done.3, f32[96,128]{1,0:T(8,128)} %bitcast.13, f32[96,128]{1,0:T(8,128)} %bitcast.14, f32[96,128]{1,0:T(8,128)} %bitcast.15), custom_call_target="tpu_custom_call" | custom-call | tf_op jit(solution)/shard_map/adamw/pallas_call | solution.py:158
Async XLA Ops:
  0.6 2.8 %copy-start = (s32[128,12288]{1,0:T(8,128)S(1)}, s32[128,12288]{1,0:T(8,128)}, u32[]{:S(2)}) copy-start(s32[128,12288]{1,0:T(8,128)} %refs_0_.7) | copy-start | bytes 18874372
  3.4 0.8 %copy-start.1 = (f32[128,96]{0,1:T(8,128)S(1)}, f32[128,96]{0,1:T(8,128)}, u32[]{:S(2)}) copy-start(f32[128,96]{0,1:T(8,128)} %param.8) | copy-start | bytes 147460
  5.1 13.6 %collective-permute-start = (bf16[64,4096]{1,0:T(8,128)(2,1)S(1)}, bf16[64,4096]{1,0:T(8,128)(2,1)S(1)}, u32[]{:S(2)}, u32[]{:S(2)}) collective-permute-start(bf16[64,4096]{1,0:T(8,128)(2,1)S(1)} %dequantize.5), channel_id=1, source_target_pairs={{0,32},{1,33},{2,34},{3,35},{4,36},{5,37},{6,38},{7,39},{8,40},{9,... | collective-permute-start | bytes 1572872 | tf_op jit(solution)/shard_map/ppermute | solution.py:172
  7.7 15.3 %collective-permute-start.1 = (bf16[64,4096]{1,0:T(8,128)(2,1)S(1)}, bf16[64,4096]{1,0:T(8,128)(2,1)S(1)}, u32[]{:S(2)}, u32[]{:S(2)}) collective-permute-start(bf16[64,4096]{1,0:T(8,128)(2,1)S(1)} %dequantize.6), channel_id=1, source_target_pairs={{0,96},{1,97},{2,98},{3,99},{4,100},{5,101},{6,102},{7,103},{8,104... | collective-permute-start | bytes 1572872 | tf_op jit(solution)/shard_map/ppermute | solution.py:172
  10.8 27.2 %copy-start.2 = (s32[1,1,16,96]{3,2,1,0:T(8,128)S(1)}, s32[1,1,16,96]{3,2,1,0:T(8,128)}, u32[]{:S(2)}) copy-start(s32[1,1,16,96]{3,2,1,0:T(8,128)} %param.9) | copy-start | bytes 18436
  10.8 14.1 %collective-permute-start.2 = (bf16[64,4096]{1,0:T(8,128)(2,1)S(1)}, bf16[64,4096]{1,0:T(8,128)(2,1)S(1)}, u32[]{:S(2)}, u32[]{:S(2)}) collective-permute-start(bf16[64,4096]{1,0:T(8,128)(2,1)S(1)} %dequantize.7), channel_id=1, source_target_pairs={{0,16},{1,17},{2,18},{3,19},{4,20},{5,21},{6,22},{7,23},{8,24},{9,... | collective-permute-start | bytes 1572872 | tf_op jit(solution)/shard_map/ppermute | solution.py:172
  18.8 9.2 %collective-permute-start.3 = (bf16[32,4096]{1,0:T(8,128)(2,1)S(1)}, bf16[32,4096]{1,0:T(8,128)(2,1)S(1)}, u32[]{:S(2)}, u32[]{:S(2)}) collective-permute-start(bf16[32,4096]{1,0:T(8,128)(2,1)S(1)} %add_convert_fusion.2), channel_id=1, source_target_pairs={{0,96},{1,97},{2,98},{3,99},{4,100},{5,101},{6,102},{7,103},{8,104... | collective-permute-start | bytes 786440 | tf_op jit(solution)/shard_map/ppermute | solution.py:176
  23.1 7.0 %collective-permute-start.4 = (bf16[32,4096]{1,0:T(8,128)(2,1)S(1)}, bf16[32,4096]{1,0:T(8,128)(2,1)S(1)}, u32[]{:S(2)}, u32[]{:S(2)}) collective-permute-start(bf16[32,4096]{1,0:T(8,128)(2,1)S(1)} %add_convert_fusion.1), channel_id=1, source_target_pairs={{0,16},{1,17},{2,18},{3,19},{4,20},{5,21},{6,22},{7,23},{8,24},{9,... | collective-permute-start | bytes 786440 | tf_op jit(solution)/shard_map/ppermute | solution.py:176
  24.9 6.7 %collective-permute-start.5 = (bf16[32,4096]{1,0:T(8,128)(2,1)S(1)}, bf16[32,4096]{1,0:T(8,128)(2,1)S(1)}, u32[]{:S(2)}, u32[]{:S(2)}) collective-permute-start(bf16[32,4096]{1,0:T(8,128)(2,1)S(1)} %add_convert_fusion), channel_id=1, source_target_pairs={{0,32},{1,33},{2,34},{3,35},{4,36},{5,37},{6,38},{7,39},{8,40},{9,... | collective-permute-start | bytes 786440 | tf_op jit(solution)/shard_map/ppermute | solution.py:176
  28.1 5.7 %collective-permute-start.6 = (bf16[16,4096]{1,0:T(8,128)(2,1)S(1)}, bf16[16,4096]{1,0:T(8,128)(2,1)S(1)}, u32[]{:S(2)}, u32[]{:S(2)}) collective-permute-start(bf16[16,4096]{1,0:T(8,128)(2,1)S(1)} %add_convert_fusion.6), channel_id=1, source_target_pairs={{0,16},{1,17},{2,18},{3,19},{4,20},{5,21},{6,22},{7,23},{8,24},{9,... | collective-permute-start | bytes 393224 | tf_op jit(solution)/shard_map/ppermute | solution.py:183
  30.1 5.0 %collective-permute-start.7 = (bf16[16,4096]{1,0:T(8,128)(2,1)S(1)}, bf16[16,4096]{1,0:T(8,128)(2,1)S(1)}, u32[]{:S(2)}, u32[]{:S(2)}) collective-permute-start(bf16[16,4096]{1,0:T(8,128)(2,1)S(1)} %add_convert_fusion.5), channel_id=1, source_target_pairs={{0,32},{1,33},{2,34},{3,35},{4,36},{5,37},{6,38},{7,39},{8,40},{9,... | collective-permute-start | bytes 393224 | tf_op jit(solution)/shard_map/ppermute | solution.py:183
  31.7 6.3 %collective-permute-start.8 = (bf16[16,4096]{1,0:T(8,128)(2,1)S(1)}, bf16[16,4096]{1,0:T(8,128)(2,1)S(1)}, u32[]{:S(2)}, u32[]{:S(2)}) collective-permute-start(bf16[16,4096]{1,0:T(8,128)(2,1)S(1)} %add_convert_fusion.4), channel_id=1, source_target_pairs={{0,96},{1,97},{2,98},{3,99},{4,100},{5,101},{6,102},{7,103},{8,104... | collective-permute-start | bytes 393224 | tf_op jit(solution)/shard_map/ppermute | solution.py:183
  39.0 1.5 %collective-permute-start.9 = (bf16[8,96,128]{2,1,0:T(8,128)(2,1)S(1)}, bf16[8,96,128]{2,1,0:T(8,128)(2,1)S(1)}, u32[]{:S(2)}, u32[]{:S(2)}) collective-permute-start(bf16[8,96,128]{2,1,0:T(8,128)(2,1)S(1)} %get-tuple-element.15), channel_id=1, source_target_pairs={{0,1},{1,0},{2,3},{3,2},{4,5},{5,4},{6,7},{7,6},{8,9},{9,8},{10,11... | collective-permute-start | bytes 589832 | tf_op jit(solution)/shard_map/ppermute | solution.py:185
  41.2 16.2 %all-to-all-start = ((bf16[8,96,128]{2,1,0:T(8,128)(2,1)}), bf16[8,96,128]{2,1,0:T(8,128)(2,1)S(1)}, u32[]{:S(2)}, u32[]{:S(2)}) async-start(bf16[8,96,128]{2,1,0:T(8,128)(2,1)} %add_convert_fusion.3), calls=%async_computation | async-start | bytes 393216 | tf_op jit(solution)/shard_map/all_to_all | solution.py:188
  57.4 0.7 %copy-start.3 = (bf16[8,96,128]{2,1,0:T(8,128)(2,1)}, bf16[8,96,128]{2,1,0:T(8,128)(2,1)S(1)}, u32[]{:S(2)}) copy-start(bf16[8,96,128]{2,1,0:T(8,128)(2,1)S(1)} %all-to-all-done.terms_ref) | copy-start | bytes 589828

commit v2 on v1

--- a/solution.py
+++ b/solution.py
@@ -1,3 +1,5 @@
+import itertools
+
 import jax
 import jax.numpy as jnp
 from jax import lax
@@ -15,9 +17,9 @@
 COLUMNS = BLOCKS * LANES
 TILE = 16
 PIECES = (
-    (0, 32, "PQZ", "PQZ"),
-    (32, 32, "QZP", "QZP"),
-    (64, 32, "ZPQ", "ZPQ"),
+    (0, 32, "PQZ", "QZP"),
+    (32, 32, "QZP", "ZPQ"),
+    (64, 32, "ZPQ", "PQZ"),
 )
 AXES = ("node", "wide")
 VMEM_LIMIT = 32 * 1024 * 1024
@@ -30,6 +32,12 @@
 
 def node_of(label):
     return (label["Q"] << 2) | ((label["P"] ^ label["Q"]) << 1) | label["Z"]
+
+
+def wide_near(wide, relative):
+    high, low, core = (wide >> 2) & 1, (wide >> 1) & 1, wide & 1
+    first, second, third = (low ^ high) ^ relative[0], high ^ relative[1], (wide >> 3) ^ relative[2]
+    return (third << 3) | (second << 2) | ((first ^ second) << 1) | core
 
 
 def pairs(dim0, dim1):
@@ -57,10 +65,10 @@
 
 
 def dequantize_kernel(parts, codes_ref, scales_ref, *rest):
-    outs = rest[: len(parts)]
-    scales_buf = rest[len(parts)]
-    stage = rest[len(parts) + 1 : -1]
-    sem = rest[-1]
+    outs, stage = rest[: len(parts)], rest[len(parts) : 2 * len(parts)]
+    scales_buf, scales, sem, scale_sem = rest[2 * len(parts) :]
+    scale_copy = pltpu.make_async_copy(scales_ref, scales_buf, scale_sem)
+    scale_copy.start()
     copies = []
     for n, (piece, first) in enumerate(parts):
         for j, tail in enumerate(ORDER):
@@ -72,10 +80,11 @@
             )
             copy.start()
             copies.append((n, j, row, copy))
-    scales_buf[:, :BLOCKS] = scales_ref[...].T
+    scale_copy.wait()
+    scales[:, :BLOCKS] = scales_buf[...].T
     for n, j, row, copy in copies:
         piece = parts[n][0]
-        scale = scales_buf[pl.ds(row, TILE), :]
+        scale = scales[pl.ds(row, TILE), :]
         copy.wait()
         for k in range(piece[1]):
             at = piece[0] + k
@@ -85,15 +94,20 @@
 
 
 def dequantize(parts, codes, scales_t):
+    hbm = pl.BlockSpec(memory_space=pltpu.HBM)
     shapes = [(4 * TILE, piece[1] * LANES) for piece, _ in parts]
     return pl.pallas_call(
         lambda *refs: dequantize_kernel(parts, *refs),
         out_shape=[jax.ShapeDtypeStruct(s, jnp.bfloat16) for s in shapes],
-        in_specs=[pl.BlockSpec(memory_space=pl.ANY), pl.BlockSpec(memory_space=pltpu.VMEM)],
+        in_specs=[hbm, hbm],
         out_specs=[pl.BlockSpec(memory_space=pltpu.VMEM) for _ in parts],
-        scratch_shapes=[pltpu.VMEM((128, LANES), jnp.float32)]
-        + [pltpu.VMEM(s, jnp.int32) for s in shapes]
-        + [pltpu.SemaphoreType.DMA((len(parts), 4))],
+        scratch_shapes=[pltpu.VMEM(s, jnp.int32) for s in shapes]
+        + [
+            pltpu.VMEM((BLOCKS, 128), jnp.float32),
+            pltpu.VMEM((128, LANES), jnp.float32),
+            pltpu.SemaphoreType.DMA((len(parts), 4)),
+            pltpu.SemaphoreType.DMA,
+        ],
         compiler_params=pltpu.CompilerParams(vmem_limit_bytes=VMEM_LIMIT),
         name="dequantize",
     )(codes, scales_t)
@@ -116,10 +130,11 @@
             ) + (seconds[n][TILE : 2 * TILE, cut].astype(jnp.float32) + thirds[n][:, cut].astype(jnp.float32))
             coded = jnp.clip(partial * inverse[:, at : at + 1], -8.0, 8.0).astype(jnp.bfloat16)
             rows[pl.ds(at, TILE, stride=BLOCKS), :] = coded.astype(jnp.float32) * scale[:, at : at + 1]
-    core = lax.axis_index("wide") & 1
-    for j in range(8):
-        other = pl.multiple_of((2 * j + 1 - core) * BLOCKS, 8)
-        own = pl.multiple_of((2 * j + core) * BLOCKS, 8)
+    wide = lax.axis_index("wide")
+    for j, relative in enumerate(itertools.product((1, 0), repeat=3)):
+        owner = wide_near(wide, relative)
+        own = pl.multiple_of(owner * BLOCKS, 8)
+        other = pl.multiple_of((owner ^ 1) * BLOCKS, 8)
         send_ref[j] = rows[pl.ds(other, BLOCKS), :].astype(jnp.bfloat16)
         keep_ref[j] = rows[pl.ds(own, BLOCKS), :]
 
@@ -140,37 +155,24 @@
     )(requant, *keeps, *firsts, *seconds, *thirds)
 
 
-def adamw_kernel(bias_ref, terms_ref, params_ref, first_ref, second_ref, update_out, first_out, second_out):
-    gradient = terms_ref[0].astype(jnp.float32)
-    for j in range(1, 8):
-        gradient = gradient + terms_ref[j].astype(jnp.float32)
-    first = decay_first * first_ref[...] + (1.0 - decay_first) * gradient
-    second = decay_second * second_ref[...] + (1.0 - decay_second) * gradient * gradient
-    update_out[...] = (
-        first / bias_ref[0] / (jnp.sqrt(second / bias_ref[1]) + epsilon) + weight_decay * params_ref[...]
-    )
-    first_out[...] = first
-    second_out[...] = second
-
-
-def adamw(bias, terms, params, first_moment, second_moment):
-    vmem = pl.BlockSpec(memory_space=pltpu.VMEM)
-    return pl.pallas_call(
-        adamw_kernel,
-        out_shape=[jax.ShapeDtypeStruct((BLOCKS, LANES), jnp.float32)] * 3,
-        in_specs=[pl.BlockSpec(memory_space=pltpu.SMEM)] + [vmem] * 4,
-        out_specs=[vmem] * 3,
-        name="adamw",
-    )(bias, terms, params, first_moment, second_moment)
+def adamw(gradient, params, first_moment, second_moment, step_count):
+    steps = step_count[0].astype(jnp.float32)
+    first = decay_first * first_moment + (1.0 - decay_first) * gradient
+    second = decay_second * second_moment + (1.0 - decay_second) * gradient * gradient
+    bias_first = 1.0 - jnp.power(jnp.float32(decay_first), steps)
+    bias_second = 1.0 - jnp.power(jnp.float32(decay_second), steps)
+    update = first / bias_first / (jnp.sqrt(second / bias_second) + epsilon) + weight_decay * params
+    return (update, first, second)
 
 
 def shards(grad_codes, code_scales, requant_scales, params, first_moment, second_moment, step_count):
-    scales_t = code_scales.T
     firsts, seconds, thirds = [], [], []
+    codes = pltpu.with_memory_space_constraint(grad_codes, pltpu.HBM)
+    scales = pltpu.with_memory_space_constraint(code_scales.T, pltpu.HBM)
     for piece in PIECES:
-        (send,) = dequantize([(piece, 1)], grad_codes, scales_t)
+        (send,) = dequantize([(piece, 1)], codes, scales)
         firsts.append(lax.ppermute(send, AXES, pairs(piece[2][0], piece[3][0])))
-    keeps = dequantize([(piece, 0) for piece in PIECES], grad_codes, scales_t)
+    keeps = dequantize([(piece, 0) for piece in PIECES], codes, scales)
     for n, piece in enumerate(PIECES):
         send = firsts[n][: 2 * TILE].astype(jnp.float32) + keeps[n][: 2 * TILE].astype(jnp.float32)
         seconds.append(lax.ppermute(send.astype(jnp.bfloat16), AXES, pairs(piece[2][1], piece[3][1])))
@@ -182,16 +184,18 @@
         )
         thirds.append(lax.ppermute(send.astype(jnp.bfloat16), AXES, pairs(piece[2][2], piece[3][2])))
     send, keep = finish(requant_scales.reshape(TILE, BLOCKS), keeps, firsts, seconds, thirds)
-    other = lax.ppermute(send, "wide", [(b, b ^ 1) for b in range(16)])
-    terms = (keep + other.astype(jnp.float32)).astype(jnp.bfloat16)
-    groups = [[2 * j + core for j in range(8)] for core in range(2)]
-    terms = lax.all_to_all(terms, "wide", 0, 0, tiled=True, axis_index_groups=groups)
-    steps = step_count.astype(jnp.float32)
-    bias = jnp.concatenate(
-        [1.0 - jnp.power(jnp.float32(decay_first), steps), 1.0 - jnp.power(jnp.float32(decay_second), steps)]
+    from_core = lax.ppermute(send, "wide", [(b, b ^ 1) for b in range(16)]).astype(jnp.float32)
+    near = keep + from_core
+    hops = []
+    for step, count in enumerate((4, 2, 1)):
+        relative = tuple(int(step == n) for n in range(3))
+        route = [(b, wide_near(b, relative)) for b in range(16)]
+        hops.append(lax.ppermute(near[:count].astype(jnp.bfloat16), "wide", route).astype(jnp.float32))
+        near = near[count:] + hops[-1]
+    tall = (BLOCKS, LANES)
+    outs = adamw(
+        near[0], params.reshape(tall), first_moment.reshape(tall), second_moment.reshape(tall), step_count
     )
-    tall = (BLOCKS, LANES)
-    outs = adamw(bias, terms, params.reshape(tall), first_moment.reshape(tall), second_moment.reshape(tall))
     return tuple(out.reshape(1, COLUMNS) for out in outs)
 
 

time: 60.1 us -> 55.9 us (0.930)
  local copies, waits for them, and re-layouts: 4.27 us -> 0.06 us
  starting transfers between devices: 24.7 us -> 21.3 us
  Pallas kernels: 7.89 us -> 10.2 us
  waiting for transfers between devices: 19.7 us -> 21.3 us
    ppermute x1 -> x4, starting transfers between devices: 0.09 us -> 8.61 us  [the longest x3 8.53 us: shards(): lax.ppermute(near[:count].astype(jnp.bfloat16), 'wide', route)]
    all_to_all x1 -> x0, starting transfers between devices: 7.74 us -> none  [shards(): lax.all_to_all(terms, 'wide', 0, 0, tiled=True, axis_index_groups=groups)]
    all_to_all x1 -> x0, waiting for transfers between devices: 7.08 us -> none  [shards(): lax.all_to_all(terms, 'wide', 0, 0, tiled=True, axis_index_groups=groups)]
    ppermute x1 -> x4, waiting for transfers between devices: 1.43 us -> 8.05 us  [the longest x3 6.62 us: shards(): lax.ppermute(near[:count].astype(jnp.bfloat16), 'wide', route)]
    unnamed x8, local copies, waits for them, and re-layouts: 4.27 us -> 0.03 us
    pallas_call x4, Pallas kernels: 5.26 us -> 9.29 us  [dequantize(): pl.pallas_call(lambda *refs: dequantize_kernel(parts, *refs), out_shape=[...]
    ppermute x3, starting transfers between devices: 5.57 us -> 3.28 us  [shards(): lax.ppermute(send.astype(jnp.bfloat16), AXES, pairs(piece[2][2], piece[3]...]
    ppermute x3, starting transfers between devices: 5.53 us -> 3.57 us  [shards(): lax.ppermute(send.astype(jnp.bfloat16), AXES, pairs(piece[2][1], piece[3]...]
  transfers between devices with their start and end apart: 11 -> 13, of which waited for: 8 -> 10; matrix products, arithmetic and copies ran while one was open for 2% -> 1% of each run, Pallas kernels for 7% -> 14%
where the time goes in v2:
time: 55.9 us; the launch traced here: 55.7 us
  starting transfers between devices  21.3 us (38%)
  waiting for transfers between devices  21.3 us (38%)
  Pallas kernels  10.2 us (18%)
  between operations  1.55 us (3%)
  other arithmetic  1.35 us (2%)
    pallas_call x4, Pallas kernels, dequantize(): pl.pallas_call(lambda *refs: dequantize_kernel(parts, *refs), out_shape=[...  9.29 us
    ppermute x3, starting transfers between devices, shards(): lax.ppermute(near[:count].astype(jnp.bfloat16), 'wide', route)  8.53 us
    ppermute x3, waiting for transfers between devices, shards(): lax.ppermute(near[:count].astype(jnp.bfloat16), 'wide', route)  6.62 us
    ppermute x3, starting transfers between devices, shards(): firsts.append(lax.ppermute(send, AXES, pairs(piece[2][0], piece[3][0])))  5.83 us
    ppermute x3, waiting for transfers between devices, shards(): lax.ppermute(send.astype(jnp.bfloat16), AXES, pairs(piece[2][2], piece[3]...  5.4 us
    ppermute x3, waiting for transfers between devices, shards(): firsts.append(lax.ppermute(send, AXES, pairs(piece[2][0], piece[3][0])))  4 us
    ppermute x3, waiting for transfers between devices, shards(): lax.ppermute(send.astype(jnp.bfloat16), AXES, pairs(piece[2][1], piece[3]...  3.82 us
    ppermute x3, starting transfers between devices, shards(): lax.ppermute(send.astype(jnp.bfloat16), AXES, pairs(piece[2][1], piece[3]...  3.57 us
  transfers between devices with their start and end apart: 13, of which 10 were waited for; matrix products, arithmetic and copies ran while one was open for 1% of the time, Pallas kernels for 14%

profile of v2, /device:TPU:0, one launch (start us, length us, event | category | flops | bytes accessed | tf_op | source)
XLA Modules:
  0.0 55.7 jit_solution(17345425445906825698)
XLA Ops:
  0.6 1.7 %dequantize.5 = bf16[64,4096]{1,0:T(8,128)(2,1)S(1)} custom-call(s32[128,12288]{1,0:T(8,128)} %refs_0_.7, f32[96,128]{1,0:T(8,128)} %bitcast.6), custom_call_target="tpu_custom_call" | custom-call | tf_op jit(solution)/shard_map/dequantize/pallas_call | solution.py:99
  2.4 1.7 %collective-permute-start = (bf16[64,4096]{1,0:T(8,128)(2,1)S(1)}, bf16[64,4096]{1,0:T(8,128)(2,1)S(1)}, u32[]{:S(2)}, u32[]{:S(2)}) collective-permute-start(bf16[64,4096]{1,0:T(8,128)(2,1)S(1)} %dequantize.5), channel_id=1, source_target_pairs={{0,32},{1,97},{2,34},{3,99},{4,36},{5,101},{6,38},{7,103},{8,40},{... | collective-permute-start | bytes 1572872 | tf_op jit(solution)/shard_map/ppermute | solution.py:174
  4.0 1.7 %dequantize.6 = bf16[64,4096]{1,0:T(8,128)(2,1)S(1)} custom-call(s32[128,12288]{1,0:T(8,128)} %refs_0_.7, f32[96,128]{1,0:T(8,128)} %bitcast.7), custom_call_target="tpu_custom_call" | custom-call | tf_op jit(solution)/shard_map/dequantize/pallas_call | solution.py:99
  5.7 2.2 %collective-permute-start.1 = (bf16[64,4096]{1,0:T(8,128)(2,1)S(1)}, bf16[64,4096]{1,0:T(8,128)(2,1)S(1)}, u32[]{:S(2)}, u32[]{:S(2)}) collective-permute-start(bf16[64,4096]{1,0:T(8,128)(2,1)S(1)} %dequantize.6), channel_id=1, source_target_pairs={{0,96},{1,17},{2,98},{3,19},{4,100},{5,21},{6,102},{7,23},{8,104},... | collective-permute-start | bytes 1572872 | tf_op jit(solution)/shard_map/ppermute | solution.py:174
  7.9 1.9 %dequantize.7 = bf16[64,4096]{1,0:T(8,128)(2,1)S(1)} custom-call(s32[128,12288]{1,0:T(8,128)} %refs_0_.7, f32[96,128]{1,0:T(8,128)} %bitcast.8), custom_call_target="tpu_custom_call" | custom-call | tf_op jit(solution)/shard_map/dequantize/pallas_call | solution.py:99
  9.8 0.0 copy-start
  9.8 2.0 %collective-permute-start.2 = (bf16[64,4096]{1,0:T(8,128)(2,1)S(1)}, bf16[64,4096]{1,0:T(8,128)(2,1)S(1)}, u32[]{:S(2)}, u32[]{:S(2)}) collective-permute-start(bf16[64,4096]{1,0:T(8,128)(2,1)S(1)} %dequantize.7), channel_id=1, source_target_pairs={{0,16},{1,33},{2,18},{3,35},{4,20},{5,37},{6,22},{7,39},{8,24},{9,... | collective-permute-start | bytes 1572872 | tf_op jit(solution)/shard_map/ppermute | solution.py:174
  11.8 4.0 %dequantize.4 = (bf16[64,4096]{1,0:T(8,128)(2,1)S(1)}, bf16[64,4096]{1,0:T(8,128)(2,1)S(1)}, bf16[64,4096]{1,0:T(8,128)(2,1)S(1)}) custom-call(s32[128,12288]{1,0:T(8,128)} %refs_0_.7, f32[96,128]{1,0:T(8,128)} %bitcast.9), custom_call_target="tpu_custom_call" | custom-call | tf_op jit(solution)/shard_map/dequantize/pallas_call | solution.py:99
  15.8 0.0 copy-start.1
  15.8 0.0 copy-start.2
  15.8 0.0 copy-start.3
  15.8 0.0 collective-permute-done.refs_3_
  15.8 0.1 add_convert_fusion.2
  15.9 1.3 %collective-permute-start.3 = (bf16[32,4096]{1,0:T(8,128)(2,1)S(1)}, bf16[32,4096]{1,0:T(8,128)(2,1)S(1)}, u32[]{:S(2)}, u32[]{:S(2)}) collective-permute-start(bf16[32,4096]{1,0:T(8,128)(2,1)S(1)} %add_convert_fusion.2), channel_id=1, source_target_pairs={{0,96},{1,17},{2,98},{3,19},{4,100},{5,21},{6,102},{7,23},{8,104},... | collective-permute-start | bytes 786440 | tf_op jit(solution)/shard_map/ppermute | solution.py:178
  17.2 0.0 collective-permute-done.1.refs_4_
  17.2 0.1 add_convert_fusion.1
  17.3 2.2 %collective-permute-start.4 = (bf16[32,4096]{1,0:T(8,128)(2,1)S(1)}, bf16[32,4096]{1,0:T(8,128)(2,1)S(1)}, u32[]{:S(2)}, u32[]{:S(2)}) collective-permute-start(bf16[32,4096]{1,0:T(8,128)(2,1)S(1)} %add_convert_fusion.1), channel_id=1, source_target_pairs={{0,16},{1,33},{2,18},{3,35},{4,20},{5,37},{6,22},{7,39},{8,24},{9,... | collective-permute-start | bytes 786440 | tf_op jit(solution)/shard_map/ppermute | solution.py:178
  19.5 4.0 %collective-permute-done.2.refs_5_ = bf16[64,4096]{1,0:T(8,128)(2,1)S(1)} collective-permute-done((bf16[64,4096]{1,0:T(8,128)(2,1)S(1)}, bf16[64,4096]{1,0:T(8,128)(2,1)S(1)}, u32[]{:S(2)}, u32[]{:S(2)}) %collective-permute-start.2) | collective-permute-done | bytes 524320 | tf_op jit(solution)/shard_map/ppermute | solution.py:174
  23.4 0.1 add_convert_fusion
  23.5 0.1 collective-permute-start.5
  23.6 0.9 %collective-permute-done.3.refs_6_ = bf16[32,4096]{1,0:T(8,128)(2,1)S(1)} collective-permute-done((bf16[32,4096]{1,0:T(8,128)(2,1)S(1)}, bf16[32,4096]{1,0:T(8,128)(2,1)S(1)}, u32[]{:S(2)}, u32[]{:S(2)}) %collective-permute-start.3) | collective-permute-done | bytes 262176 | tf_op jit(solution)/shard_map/ppermute | solution.py:178
  24.5 0.1 add_convert_fusion.5
  24.6 1.1 %collective-permute-start.6 = (bf16[16,4096]{1,0:T(8,128)(2,1)S(1)}, bf16[16,4096]{1,0:T(8,128)(2,1)S(1)}, u32[]{:S(2)}, u32[]{:S(2)}) collective-permute-start(bf16[16,4096]{1,0:T(8,128)(2,1)S(1)} %add_convert_fusion.5), channel_id=1, source_target_pairs={{0,16},{1,33},{2,18},{3,35},{4,20},{5,37},{6,22},{7,39},{8,24},{9,... | collective-permute-start | bytes 393224 | tf_op jit(solution)/shard_map/ppermute | solution.py:185
  25.7 0.6 %collective-permute-done.4.refs_7_ = bf16[32,4096]{1,0:T(8,128)(2,1)S(1)} collective-permute-done((bf16[32,4096]{1,0:T(8,128)(2,1)S(1)}, bf16[32,4096]{1,0:T(8,128)(2,1)S(1)}, u32[]{:S(2)}, u32[]{:S(2)}) %collective-permute-start.4) | collective-permute-done | bytes 262176 | tf_op jit(solution)/shard_map/ppermute | solution.py:178
  26.3 0.1 add_convert_fusion.4
  26.3 1.3 %collective-permute-start.7 = (bf16[16,4096]{1,0:T(8,128)(2,1)S(1)}, bf16[16,4096]{1,0:T(8,128)(2,1)S(1)}, u32[]{:S(2)}, u32[]{:S(2)}) collective-permute-start(bf16[16,4096]{1,0:T(8,128)(2,1)S(1)} %add_convert_fusion.4), channel_id=1, source_target_pairs={{0,32},{1,97},{2,34},{3,99},{4,36},{5,101},{6,38},{7,103},{8,40},{... | collective-permute-start | bytes 393224 | tf_op jit(solution)/shard_map/ppermute | solution.py:185
  27.6 2.3 %collective-permute-done.5.refs_8_ = bf16[32,4096]{1,0:T(8,128)(2,1)S(1)} collective-permute-done((bf16[32,4096]{1,0:T(8,128)(2,1)S(1)}, bf16[32,4096]{1,0:T(8,128)(2,1)S(1)}, u32[]{:S(2)}, u32[]{:S(2)}) %collective-permute-start.5) | collective-permute-done | bytes 262176 | tf_op jit(solution)/shard_map/ppermute | solution.py:178
  30.0 0.1 add_convert_fusion.3
  30.0 0.9 %collective-permute-start.8 = (bf16[16,4096]{1,0:T(8,128)(2,1)S(1)}, bf16[16,4096]{1,0:T(8,128)(2,1)S(1)}, u32[]{:S(2)}, u32[]{:S(2)}) collective-permute-start(bf16[16,4096]{1,0:T(8,128)(2,1)S(1)} %add_convert_fusion.3), channel_id=1, source_target_pairs={{0,96},{1,17},{2,98},{3,19},{4,100},{5,21},{6,102},{7,23},{8,104},... | collective-permute-start | bytes 393224 | tf_op jit(solution)/shard_map/ppermute | solution.py:185
  30.9 0.0 collective-permute-done.6.refs_9_
  30.9 0.5 collective-permute-done.7.refs_10_
  31.4 4.9 %collective-permute-done.8.refs_11_ = bf16[16,4096]{1,0:T(8,128)(2,1)S(1)} collective-permute-done((bf16[16,4096]{1,0:T(8,128)(2,1)S(1)}, bf16[16,4096]{1,0:T(8,128)(2,1)S(1)}, u32[]{:S(2)}, u32[]{:S(2)}) %collective-permute-start.8) | collective-permute-done | bytes 131104 | tf_op jit(solution)/shard_map/ppermute | solution.py:185
  36.3 0.0 copy-done
  36.3 0.9 %finish.1 = (bf16[8,96,128]{2,1,0:T(8,128)(2,1)S(1)}, f32[8,96,128]{2,1,0:T(8,128)S(1)}) custom-call(s32[16,96]{1,0:T(8,128)S(1)} %bitcast.5, bf16[64,4096]{1,0:T(8,128)(2,1)S(1)} %get-tuple-element.8.refs_0_, bf16[64,4096]{1,0:T(8,128)(2,1)S(1)} %get-tuple-element.9.refs_1_, bf16[64,4096]{1,0:T(8,128)(2,1)S(1)} %get-tuple-element.10.refs_2_, ...), custom_call_target="tpu_custom_call" | custom-call | tf_op jit(solution)/shard_map/finish/pallas_call | solution.py:144
  37.2 0.1 collective-permute-start.9
  37.3 1.4 %collective-permute-done.9 = bf16[8,96,128]{2,1,0:T(8,128)(2,1)S(1)} collective-permute-done((bf16[8,96,128]{2,1,0:T(8,128)(2,1)S(1)}, bf16[8,96,128]{2,1,0:T(8,128)(2,1)S(1)}, u32[]{:S(2)}, u32[]{:S(2)}) %collective-permute-start.9) | collective-permute-done | bytes 196640 | tf_op jit(solution)/shard_map/ppermute | solution.py:187
  38.8 1.7 %collective-permute-start.10 = (bf16[4,96,128]{2,1,0:T(8,128)(2,1)S(1)}, bf16[4,96,128]{2,1,0:T(8,128)(2,1)S(1)}, u32[]{:S(2)}, u32[]{:S(2)}) collective-permute-start(bf16[4,96,128]{2,1,0:T(8,128)(2,1)S(1)} %slice.123), channel_id=1, source_target_pairs={{0,2},{1,3},{2,0},{3,1},{4,6},{5,7},{6,4},{7,5},{8,10},{9,11},{10,... | collective-permute-start | bytes 294920 | tf_op jit(solution)/shard_map/ppermute | solution.py:193
  40.4 3.3 %collective-permute-done.10 = bf16[4,96,128]{2,1,0:T(8,128)(2,1)S(1)} collective-permute-done((bf16[4,96,128]{2,1,0:T(8,128)(2,1)S(1)}, bf16[4,96,128]{2,1,0:T(8,128)(2,1)S(1)}, u32[]{:S(2)}, u32[]{:S(2)}) %collective-permute-start.10) | collective-permute-done | bytes 98336 | tf_op jit(solution)/shard_map/ppermute | solution.py:193
  43.7 3.1 %collective-permute-start.11 = (bf16[2,96,128]{2,1,0:T(8,128)(2,1)S(1)}, bf16[2,96,128]{2,1,0:T(8,128)(2,1)S(1)}, u32[]{:S(2)}, u32[]{:S(2)}) collective-permute-start(bf16[2,96,128]{2,1,0:T(8,128)(2,1)S(1)} %slice.124), channel_id=1, source_target_pairs={{0,6},{1,7},{2,4},{3,5},{4,2},{5,3},{6,0},{7,1},{8,14},{9,15},{10,... | collective-permute-start | bytes 147464 | tf_op jit(solution)/shard_map/ppermute | solution.py:193
  46.8 2.3 %collective-permute-done.11 = bf16[2,96,128]{2,1,0:T(8,128)(2,1)S(1)} collective-permute-done((bf16[2,96,128]{2,1,0:T(8,128)(2,1)S(1)}, bf16[2,96,128]{2,1,0:T(8,128)(2,1)S(1)}, u32[]{:S(2)}, u32[]{:S(2)}) %collective-permute-start.11) | collective-permute-done | bytes 49184 | tf_op jit(solution)/shard_map/ppermute | solution.py:193
  49.2 3.8 %collective-permute-start.12 = (bf16[1,96,128]{2,1,0:T(8,128)(2,1)S(1)}, bf16[1,96,128]{2,1,0:T(8,128)(2,1)S(1)}, u32[]{:S(2)}, u32[]{:S(2)}) collective-permute-start(bf16[1,96,128]{2,1,0:T(8,128)(2,1)S(1)} %slice.125), channel_id=1, source_target_pairs={{0,8},{1,9},{2,10},{3,11},{4,12},{5,13},{6,14},{7,15},{8,0},{9,1},... | collective-permute-start | bytes 73736 | tf_op jit(solution)/shard_map/ppermute | solution.py:193
  53.7 1.1 %collective-permute-done.12 = bf16[1,96,128]{2,1,0:T(8,128)(2,1)S(1)} collective-permute-done((bf16[1,96,128]{2,1,0:T(8,128)(2,1)S(1)}, bf16[1,96,128]{2,1,0:T(8,128)(2,1)S(1)}, u32[]{:S(2)}, u32[]{:S(2)}) %collective-permute-start.12) | collective-permute-done | bytes 24608 | tf_op jit(solution)/shard_map/ppermute | solution.py:193
  54.7 0.0 copy-done.1
  54.8 0.0 copy-done.2
  54.8 0.0 copy-done.3
  54.8 0.9 %multiply_add_fusion = (f32[1,12288]{1,0:T(1,128)}, f32[1,12288]{1,0:T(1,128)}, f32[1,12288]{1,0:T(1,128)}) fusion(f32[1,12288]{1,0:T(1,128)S(1)} %copy-done.1, f32[]{:T(128)} %bitcast.4, f32[]{:T(128)} %bitcast.3, f32[1,12288]{1,0:T(1,128)S(1)} %bitcast.10, f32[1,12288]{1,0:T(1,128)S(1)} %copy-done.2, f32[1,12288]{1,0:T(1,128)S(1)} %copy-done.3), kind=kLoop, calls=%fused_computation.15 | loop fusion | flops 159744 | bytes 344072 | tf_op jit(solution)/shard_map/add | solution.py:164
  (7 shorter events, 0.1 us)
Async XLA Ops:
  2.4 13.5 %collective-permute-start = (bf16[64,4096]{1,0:T(8,128)(2,1)S(1)}, bf16[64,4096]{1,0:T(8,128)(2,1)S(1)}, u32[]{:S(2)}, u32[]{:S(2)}) collective-permute-start(bf16[64,4096]{1,0:T(8,128)(2,1)S(1)} %dequantize.5), channel_id=1, source_target_pairs={{0,32},{1,97},{2,34},{3,99},{4,36},{5,101},{6,38},{7,103},{8,40},{... | collective-permute-start | bytes 1572872 | tf_op jit(solution)/shard_map/ppermute | solution.py:174
  5.7 11.5 %collective-permute-start.1 = (bf16[64,4096]{1,0:T(8,128)(2,1)S(1)}, bf16[64,4096]{1,0:T(8,128)(2,1)S(1)}, u32[]{:S(2)}, u32[]{:S(2)}) collective-permute-start(bf16[64,4096]{1,0:T(8,128)(2,1)S(1)} %dequantize.6), channel_id=1, source_target_pairs={{0,96},{1,17},{2,98},{3,19},{4,100},{5,21},{6,102},{7,23},{8,104},... | collective-permute-start | bytes 1572872 | tf_op jit(solution)/shard_map/ppermute | solution.py:174
  9.8 26.5 %copy-start = (s32[1,1,16,96]{3,2,1,0:T(8,128)S(1)}, s32[1,1,16,96]{3,2,1,0:T(8,128)}, u32[]{:S(2)}) copy-start(s32[1,1,16,96]{3,2,1,0:T(8,128)} %param.9) | copy-start | bytes 18436
  9.8 13.7 %collective-permute-start.2 = (bf16[64,4096]{1,0:T(8,128)(2,1)S(1)}, bf16[64,4096]{1,0:T(8,128)(2,1)S(1)}, u32[]{:S(2)}, u32[]{:S(2)}) collective-permute-start(bf16[64,4096]{1,0:T(8,128)(2,1)S(1)} %dequantize.7), channel_id=1, source_target_pairs={{0,16},{1,33},{2,18},{3,35},{4,20},{5,37},{6,22},{7,39},{8,24},{9,... | collective-permute-start | bytes 1572872 | tf_op jit(solution)/shard_map/ppermute | solution.py:174
  15.8 39.0 %copy-start.1 = (f32[1,12288]{1,0:T(1,128)S(1)}, f32[1,12288]{1,0:T(1,128)}, u32[]{:S(2)}) copy-start(f32[1,12288]{1,0:T(1,128)} %param.10) | copy-start | bytes 147460
  15.8 39.0 %copy-start.2 = (f32[1,12288]{1,0:T(1,128)S(1)}, f32[1,12288]{1,0:T(1,128)}, u32[]{:S(2)}) copy-start(f32[1,12288]{1,0:T(1,128)} %param.12) | copy-start | bytes 147460
  15.8 39.0 %copy-start.3 = (f32[1,12288]{1,0:T(1,128)S(1)}, f32[1,12288]{1,0:T(1,128)}, u32[]{:S(2)}) copy-start(f32[1,12288]{1,0:T(1,128)} %param.11) | copy-start | bytes 147460
  15.9 8.6 %collective-permute-start.3 = (bf16[32,4096]{1,0:T(8,128)(2,1)S(1)}, bf16[32,4096]{1,0:T(8,128)(2,1)S(1)}, u32[]{:S(2)}, u32[]{:S(2)}) collective-permute-start(bf16[32,4096]{1,0:T(8,128)(2,1)S(1)} %add_convert_fusion.2), channel_id=1, source_target_pairs={{0,96},{1,17},{2,98},{3,19},{4,100},{5,21},{6,102},{7,23},{8,104},... | collective-permute-start | bytes 786440 | tf_op jit(solution)/shard_map/ppermute | solution.py:178
  17.3 9.0 %collective-permute-start.4 = (bf16[32,4096]{1,0:T(8,128)(2,1)S(1)}, bf16[32,4096]{1,0:T(8,128)(2,1)S(1)}, u32[]{:S(2)}, u32[]{:S(2)}) collective-permute-start(bf16[32,4096]{1,0:T(8,128)(2,1)S(1)} %add_convert_fusion.1), channel_id=1, source_target_pairs={{0,16},{1,33},{2,18},{3,35},{4,20},{5,37},{6,22},{7,39},{8,24},{9,... | collective-permute-start | bytes 786440 | tf_op jit(solution)/shard_map/ppermute | solution.py:178
  23.5 6.5 %collective-permute-start.5 = (bf16[32,4096]{1,0:T(8,128)(2,1)S(1)}, bf16[32,4096]{1,0:T(8,128)(2,1)S(1)}, u32[]{:S(2)}, u32[]{:S(2)}) collective-permute-start(bf16[32,4096]{1,0:T(8,128)(2,1)S(1)} %add_convert_fusion), channel_id=1, source_target_pairs={{0,32},{1,97},{2,34},{3,99},{4,36},{5,101},{6,38},{7,103},{8,40},{... | collective-permute-start | bytes 786440 | tf_op jit(solution)/shard_map/ppermute | solution.py:178
  24.6 6.3 %collective-permute-start.6 = (bf16[16,4096]{1,0:T(8,128)(2,1)S(1)}, bf16[16,4096]{1,0:T(8,128)(2,1)S(1)}, u32[]{:S(2)}, u32[]{:S(2)}) collective-permute-start(bf16[16,4096]{1,0:T(8,128)(2,1)S(1)} %add_convert_fusion.5), channel_id=1, source_target_pairs={{0,16},{1,33},{2,18},{3,35},{4,20},{5,37},{6,22},{7,39},{8,24},{9,... | collective-permute-start | bytes 393224 | tf_op jit(solution)/shard_map/ppermute | solution.py:185
  26.3 5.1 %collective-permute-start.7 = (bf16[16,4096]{1,0:T(8,128)(2,1)S(1)}, bf16[16,4096]{1,0:T(8,128)(2,1)S(1)}, u32[]{:S(2)}, u32[]{:S(2)}) collective-permute-start(bf16[16,4096]{1,0:T(8,128)(2,1)S(1)} %add_convert_fusion.4), channel_id=1, source_target_pairs={{0,32},{1,97},{2,34},{3,99},{4,36},{5,101},{6,38},{7,103},{8,40},{... | collective-permute-start | bytes 393224 | tf_op jit(solution)/shard_map/ppermute | solution.py:185
  30.0 6.3 %collective-permute-start.8 = (bf16[16,4096]{1,0:T(8,128)(2,1)S(1)}, bf16[16,4096]{1,0:T(8,128)(2,1)S(1)}, u32[]{:S(2)}, u32[]{:S(2)}) collective-permute-start(bf16[16,4096]{1,0:T(8,128)(2,1)S(1)} %add_convert_fusion.3), channel_id=1, source_target_pairs={{0,96},{1,17},{2,98},{3,19},{4,100},{5,21},{6,102},{7,23},{8,104},... | collective-permute-start | bytes 393224 | tf_op jit(solution)/shard_map/ppermute | solution.py:185
  37.2 1.5 %collective-permute-start.9 = (bf16[8,96,128]{2,1,0:T(8,128)(2,1)S(1)}, bf16[8,96,128]{2,1,0:T(8,128)(2,1)S(1)}, u32[]{:S(2)}, u32[]{:S(2)}) collective-permute-start(bf16[8,96,128]{2,1,0:T(8,128)(2,1)S(1)} %get-tuple-element.12), channel_id=1, source_target_pairs={{0,1},{1,0},{2,3},{3,2},{4,5},{5,4},{6,7},{7,6},{8,9},{9,8},{10,11... | collective-permute-start | bytes 589832 | tf_op jit(solution)/shard_map/ppermute | solution.py:187
  38.8 4.9 %collective-permute-start.10 = (bf16[4,96,128]{2,1,0:T(8,128)(2,1)S(1)}, bf16[4,96,128]{2,1,0:T(8,128)(2,1)S(1)}, u32[]{:S(2)}, u32[]{:S(2)}) collective-permute-start(bf16[4,96,128]{2,1,0:T(8,128)(2,1)S(1)} %slice.123), channel_id=1, source_target_pairs={{0,2},{1,3},{2,0},{3,1},{4,6},{5,7},{6,4},{7,5},{8,10},{9,11},{10,... | collective-permute-start | bytes 294920 | tf_op jit(solution)/shard_map/ppermute | solution.py:193
  43.7 5.4 %collective-permute-start.11 = (bf16[2,96,128]{2,1,0:T(8,128)(2,1)S(1)}, bf16[2,96,128]{2,1,0:T(8,128)(2,1)S(1)}, u32[]{:S(2)}, u32[]{:S(2)}) collective-permute-start(bf16[2,96,128]{2,1,0:T(8,128)(2,1)S(1)} %slice.124), channel_id=1, source_target_pairs={{0,6},{1,7},{2,4},{3,5},{4,2},{5,3},{6,0},{7,1},{8,14},{9,15},{10,... | collective-permute-start | bytes 147464 | tf_op jit(solution)/shard_map/ppermute | solution.py:193
  49.2 5.6 %collective-permute-start.12 = (bf16[1,96,128]{2,1,0:T(8,128)(2,1)S(1)}, bf16[1,96,128]{2,1,0:T(8,128)(2,1)S(1)}, u32[]{:S(2)}, u32[]{:S(2)}) collective-permute-start(bf16[1,96,128]{2,1,0:T(8,128)(2,1)S(1)} %slice.125), channel_id=1, source_target_pairs={{0,8},{1,9},{2,10},{3,11},{4,12},{5,13},{6,14},{7,15},{8,0},{9,1},... | collective-permute-start | bytes 73736 | tf_op jit(solution)/shard_map/ppermute | solution.py:193

commit v3 on v2

v3 whole, which is shorter than its diff:
```python
import itertools

import jax
import jax.numpy as jnp
from jax import lax
from jax.experimental import pallas as pl
from jax.experimental.pallas import tpu as pltpu
from jax.sharding import PartitionSpec as P

decay_first = 0.9
decay_second = 0.95
epsilon = 1e-08
weight_decay = 0.1

BLOCKS = 96
LANES = 128
COLUMNS = BLOCKS * LANES
TILE = 16
PIECES = (
    (0, 34, "PQZ", "PQZ", False),
    (34, 32, "QZP", "QZP", False),
    (66, 30, "ZPQ", "ZPQ", False),
)
FIRST = 0
AXES = ("node", "wide")
VMEM_LIMIT = 32 * 1024 * 1024


def bits(node):
    high = node >> 2
    return {"P": ((node >> 1) & 1) ^ high, "Q": high, "Z": node & 1}


def node_of(label):
    return (label["Q"] << 2) | ((label["P"] ^ label["Q"]) << 1) | label["Z"]


Y_FLIPS = ((3, 0), (2, 1))


def wide_at(wide, z_flip, y_flip, core):
    high = ((wide >> 2) & 1) ^ (y_flip >> 1)
    low = (((wide >> 1) ^ (wide >> 2)) & 1) ^ (y_flip & 1)
    return ((wide >> 3) ^ z_flip) << 3 | high << 2 | (high ^ low) << 1 | core


def y_route(slot):
    return [(b, wide_at(b, 0, Y_FLIPS[b & 1][slot], b & 1)) for b in range(16) if Y_FLIPS[b & 1][slot]]


def pairs(piece, *steps):
    result = []
    for node in range(8):
        for wide in range(16):
            label = bits(node)
            for step in steps:
                label[piece[2 + (wide & 1)][step]] ^= 1
            result.append((node * 16 + wide, node_of(label) * 16 + wide))
    return result


def block_row(piece, relative):
    mine = bits(lax.axis_index("node"))
    core = lax.axis_index("wide") & 1
    label = {}
    for dim in "PQZ":
        flip0 = relative[piece[2].index(dim)]
        flip1 = relative[piece[3].index(dim)]
        label[dim] = mine[dim] ^ (flip0 + core * (flip1 - flip0))
    return pl.multiple_of(node_of(label) * TILE, TILE)


ORDER = ((1, 1), (1, 0), (0, 1), (0, 0))


def dequantize_rows(piece, row, scale, codes, out):
    for k in range(piece[1]):
        at = piece[0] + k
        values = (codes(k).astype(jnp.float32) + 0.5) * scale[:, at : at + 1]
        out[:, k * LANES : (k + 1) * LANES] = values.astype(jnp.bfloat16)


def first_kernel(piece, codes_ref, scales_ref, out_ref, scales, stage, scales_buf, sem, scale_sem):
    scale_copy = pltpu.make_async_copy(scales_ref, scales_buf, scale_sem)
    scale_copy.start()
    copies = []
    for j, tail in enumerate(ORDER):
        row = block_row(piece, (1,) + tail)
        copy = pltpu.make_async_copy(
            codes_ref.at[pl.ds(row, TILE), pl.ds(piece[0] * LANES, piece[1] * LANES)],
            stage.at[pl.ds(j * TILE, TILE), :],
            sem.at[j],
        )
        copy.start()
        copies.append((row, copy))
    scale_copy.wait()
    scales[:, :BLOCKS] = scales_buf[...].T
    for j, (row, copy) in enumerate(copies):
        copy.wait()
        rows = slice(j * TILE, (j + 1) * TILE)
        dequantize_rows(
            piece,
            row,
            scales[pl.ds(row, TILE), :],
            lambda k: stage[rows, k * LANES : (k + 1) * LANES],
            out_ref.at[rows],
        )


def first_rows(piece, codes, scales_t):
    hbm = pl.BlockSpec(memory_space=pltpu.HBM)
    vmem = pl.BlockSpec(memory_space=pltpu.VMEM)
    shape = (4 * TILE, piece[1] * LANES)
    return pl.pallas_call(
        lambda *refs: first_kernel(piece, *refs),
        out_shape=jax.ShapeDtypeStruct(shape, jnp.bfloat16),
        in_specs=[hbm, hbm],
        out_specs=vmem,
        scratch_shapes=[
            pltpu.VMEM((128, LANES), jnp.float32),
            pltpu.VMEM(shape, jnp.int32),
            pltpu.VMEM((BLOCKS, 128), jnp.float32),
            pltpu.SemaphoreType.DMA((4,)),
            pltpu.SemaphoreType.DMA,
        ],
        compiler_params=pltpu.CompilerParams(vmem_limit_bytes=VMEM_LIMIT),
        name="first_rows",
    )(codes, scales_t)


def dequantize_kernel(parts, codes_ref, scales_ref, *rest):
    *outs, scales = rest
    scales[:, :BLOCKS] = scales_ref[...].T
    for (piece, first), out in zip(parts, outs):
        for j, tail in enumerate(ORDER):
            row = block_row(piece, (first,) + tail)
            dequantize_rows(
                piece,
                row,
                scales[pl.ds(row, TILE), :],
                lambda k: codes_ref[pl.ds(row, TILE), pl.ds((piece[0] + k) * LANES, LANES)],
                out.at[j * TILE : (j + 1) * TILE],
            )


def dequantize(parts, codes, scales):
    vmem = pl.BlockSpec(memory_space=pltpu.VMEM)
    return pl.pallas_call(
        lambda *refs: dequantize_kernel(parts, *refs),
        out_shape=[jax.ShapeDtypeStruct((4 * TILE, piece[1] * LANES), jnp.bfloat16) for piece, _ in parts],
        in_specs=[vmem, vmem],
        out_specs=[vmem for _ in parts],
        scratch_shapes=[pltpu.VMEM((128, LANES), jnp.float32)],
        compiler_params=pltpu.CompilerParams(vmem_limit_bytes=VMEM_LIMIT),
        name="dequantize",
    )(codes, scales)


def finish_kernel(counts, requant_ref, *refs):
    parts, (send_ref, keep_ref, rows) = refs[: sum(counts)], refs[sum(counts) :]
    numerators = requant_ref[...].astype(jnp.float32)
    scale = numerators * (1.0 / 32.0)
    inverse = 32.0 / numerators
    for n, piece in enumerate(PIECES):
        arrays = parts[sum(counts[:n]) : sum(counts[: n + 1])]
        for k in range(piece[1]):
            cut = pl.ds(k * LANES, LANES)
            at = piece[0] + k
            partial = arrays[0][arrays[0].shape[0] - TILE :, cut].astype(jnp.float32)
            for array in arrays[1:]:
                partial = partial + array[array.shape[0] - TILE :, cut].astype(jnp.float32)
            coded = jnp.clip(partial * inverse[:, at : at + 1], -8.0, 8.0).astype(jnp.bfloat16)
            rows[pl.ds(at, TILE, stride=BLOCKS), :] = coded.astype(jnp.float32) * scale[:, at : at + 1]
    wide = lax.axis_index("wide")
    core = wide & 1
    for slot in range(2):
        first, second = Y_FLIPS[0][slot], Y_FLIPS[1][slot]
        for ref, server in ((send_ref, 1 - core), (keep_ref, core)):
            y_flip = first + server * (second - first)
            for at, flip in enumerate((1, 0)):
                for owner in range(2):
                    row = pl.multiple_of(wide_at(wide, flip, y_flip, (server + owner + 1) & 1) * BLOCKS, 8)
                    ref[slot, at, owner] = rows[pl.ds(row, BLOCKS), :].astype(ref.dtype)


def finish(requant, parts):
    vmem = pl.BlockSpec(memory_space=pltpu.VMEM)
    shape = (2, 2, 2, BLOCKS, LANES)
    counts = [len(arrays) for arrays in parts]
    return pl.pallas_call(
        lambda *refs: finish_kernel(counts, *refs),
        out_shape=[jax.ShapeDtypeStruct(shape, jnp.bfloat16), jax.ShapeDtypeStruct(shape, jnp.float32)],
        in_specs=[vmem] * (1 + sum(counts)),
        out_specs=[vmem, vmem],
        scratch_shapes=[pltpu.VMEM((TILE * BLOCKS, LANES), jnp.float32)],
        compiler_params=pltpu.CompilerParams(vmem_limit_bytes=VMEM_LIMIT),
        name="finish",
    )(requant, *[array for arrays in parts for array in arrays])


def adamw(gradient, params, first_moment, second_moment, step_count):
    steps = step_count[0].astype(jnp.float32)
    first = decay_first * first_moment + (1.0 - decay_first) * gradient
    second = decay_second * second_moment + (1.0 - decay_second) * gradient * gradient
    bias_first = 1.0 - jnp.power(jnp.float32(decay_first), steps)
    bias_second = 1.0 - jnp.power(jnp.float32(decay_second), steps)
    update = first / bias_first / (jnp.sqrt(second / bias_second) + epsilon) + weight_decay * params
    return (update, first, second)


def send(array, axes, route):
    return lax.ppermute(array.astype(jnp.bfloat16), axes, route)


def total(*arrays):
    result = arrays[0].astype(jnp.float32)
    for array in arrays[1:]:
        result = result + array.astype(jnp.float32)
    return result


def shards(grad_codes, code_scales, requant_scales, params, first_moment, second_moment, step_count):
    codes = pltpu.with_memory_space_constraint(grad_codes, pltpu.HBM)
    scales = code_scales.T
    scales_hbm = pltpu.with_memory_space_constraint(scales, pltpu.HBM)
    firsts, parts = [], []
    for n, piece in enumerate(PIECES):
        if n == FIRST:
            rows = first_rows(piece, codes, scales_hbm)
        else:
            (rows,) = dequantize([(piece, 1)], grad_codes, scales)
        firsts.append(send(rows, AXES, pairs(piece, 0)))
    keeps = dequantize([(piece, 0) for piece in PIECES], grad_codes, scales)
    last = None
    for piece, first, keep in zip(PIECES, firsts, keeps):
        if last is not None:
            first, last = lax.optimization_barrier((first, last))
        parts.append([keep, first])
        if piece[4]:
            for n, steps in enumerate(((1, 2), (1,), (2,))):
                cut = slice(n * TILE, (n + 1) * TILE)
                last = total(keep[cut], first[cut]).astype(jnp.bfloat16)
                parts[-1].append(send(last, AXES, pairs(piece, *steps)))
        else:
            cut = slice(0, 2 * TILE)
            last = total(keep[cut], first[cut]).astype(jnp.bfloat16)
            parts[-1].append(send(last, AXES, pairs(piece, 1)))
    for piece, arrays in zip(PIECES, parts):
        if not piece[4]:
            arrays[2], last = lax.optimization_barrier((arrays[2], last))
            keep, first, second = arrays
            cut = slice(2 * TILE, 3 * TILE)
            last = total(keep[cut], first[cut], second[:TILE]).astype(jnp.bfloat16)
            arrays.append(send(last, AXES, pairs(piece, 2)))
    other_core = [(b, b ^ 1) for b in range(16)]
    away, near = finish(requant_scales.reshape(TILE, BLOCKS), parts)
    near = total(near, send(away, "wide", other_core))
    flipped = [send(near[slot], "wide", y_route(slot)) for slot in range(2)]
    stays = jnp.where((lax.axis_index("wide") & 1) == 0, near[1], 0.0)
    chip = total(stays, *flipped)
    chip = total(chip[1], send(chip[0], "wide", [(b, b ^ 8) for b in range(16)]))
    gradient = total(chip[1], lax.ppermute(chip[0], "wide", other_core))
    tall = (BLOCKS, LANES)
    outs = adamw(gradient, params.reshape(tall), first_moment.reshape(tall), second_moment.reshape(tall), step_count)
    return tuple(out.reshape(1, COLUMNS) for out in outs)


def solution(mesh):
    in_specs = (
        P(("node", "wide"), None),
        P(("node", "wide"), None),
        P("node", "wide", None, None),
        P(("node", "wide"), None),
        P(("node", "wide"), None),
        P(("node", "wide"), None),
        P(),
    )
    out_specs = (P(("node", "wide"), None), P(("node", "wide"), None), P(("node", "wide"), None))
    return jax.shard_map(shards, mesh=mesh, in_specs=in_specs, out_specs=out_specs, check_vma=False)
```

time: 55.9 us -> 53.5 us (0.957)
  the two profiles are of different devices: /device:TPU:0 before, /device:TPU:1 now
where the time goes in v3:
time: 53.5 us; the launch traced here: 53.4 us
  starting transfers between devices  28.1 us (53%)
  waiting for transfers between devices  16.9 us (32%)
  Pallas kernels  5.49 us (10%)
  between operations  1.58 us (3%)
  other arithmetic  1.25 us (2%)
    ppermute x13, starting transfers between devices, send(): return lax.ppermute(array.astype(jnp.bfloat16), axes, route)  28 us
    ppermute x13, waiting for transfers between devices, send(): return lax.ppermute(array.astype(jnp.bfloat16), axes, route)  16.5 us
    pallas_call x3, Pallas kernels, dequantize(): pl.pallas_call(lambda *refs: dequantize_kernel(parts, *refs), out_shape=[...  2.67 us
    pallas_call x1, Pallas kernels, first_rows(): pl.pallas_call(lambda *refs: first_kernel(piece, *refs), out_shape=jax.Sh...  1.89 us
  transfers between devices with their start and end apart: 14, of which 7 were waited for; matrix products, arithmetic and copies ran while one was open for 1% of the time, Pallas kernels for 5%

profile of v3, /device:TPU:1, one launch (start us, length us, event | category | flops | bytes accessed | tf_op | source)
XLA Modules:
  0.0 53.4 jit_solution(13776305026752373642)
XLA Ops:
  0.6 0.0 copy-start.1
  0.6 0.0 copy-start
  0.6 1.9 %first_rows.1 = bf16[64,4352]{1,0:T(8,128)(2,1)S(1)} custom-call(s32[128,12288]{1,0:T(8,128)} %refs_0_.7, f32[96,128]{1,0:T(8,128)} %bitcast.36), custom_call_target="tpu_custom_call" | custom-call | tf_op jit(solution)/shard_map/first_rows/pallas_call | solution.py:114
  2.6 2.1 %collective-permute-start = (bf16[64,4352]{1,0:T(8,128)(2,1)S(1)}, bf16[64,4352]{1,0:T(8,128)(2,1)S(1)}, u32[]{:S(2)}, u32[]{:S(2)}) collective-permute-start(bf16[64,4352]{1,0:T(8,128)(2,1)S(1)} %first_rows.1), channel_id=1, source_target_pairs={{0,32},{1,33},{2,34},{3,35},{4,36},{5,37},{6,38},{7,39},{8,40},{9,... | collective-permute-start | bytes 1671176 | tf_op jit(solution)/shard_map/ppermute | solution.py:212
  4.7 0.6 %dequantize.5 = bf16[64,4096]{1,0:T(8,128)(2,1)S(1)} custom-call(s32[128,12288]{1,0:T(8,128)S(1)} %copy-done, f32[96,128]{1,0:T(8,128)S(1)} %bitcast.37), custom_call_target="tpu_custom_call" | custom-call | tf_op jit(solution)/shard_map/dequantize/pallas_call | solution.py:148
  5.3 2.5 %collective-permute-start.3 = (bf16[64,4096]{1,0:T(8,128)(2,1)S(1)}, bf16[64,4096]{1,0:T(8,128)(2,1)S(1)}, u32[]{:S(2)}, u32[]{:S(2)}) collective-permute-start(bf16[64,4096]{1,0:T(8,128)(2,1)S(1)} %dequantize.5), channel_id=1, source_target_pairs={{0,96},{1,97},{2,98},{3,99},{4,100},{5,101},{6,102},{7,103},{8,104... | collective-permute-start | bytes 1572872 | tf_op jit(solution)/shard_map/ppermute | solution.py:212
  7.8 0.6 %dequantize.4 = bf16[64,3840]{1,0:T(8,128)(2,1)S(1)} custom-call(s32[128,12288]{1,0:T(8,128)S(1)} %copy-done, f32[96,128]{1,0:T(8,128)S(1)} %bitcast.38), custom_call_target="tpu_custom_call" | custom-call | tf_op jit(solution)/shard_map/dequantize/pallas_call | solution.py:148
  8.4 0.0 copy-start.2
  8.4 1.7 %collective-permute-start.2 = (bf16[64,3840]{1,0:T(8,128)(2,1)S(1)}, bf16[64,3840]{1,0:T(8,128)(2,1)S(1)}, u32[]{:S(2)}, u32[]{:S(2)}) collective-permute-start(bf16[64,3840]{1,0:T(8,128)(2,1)S(1)} %dequantize.4), channel_id=1, source_target_pairs={{0,16},{1,17},{2,18},{3,19},{4,20},{5,21},{6,22},{7,23},{8,24},{9,... | collective-permute-start | bytes 1474568 | tf_op jit(solution)/shard_map/ppermute | solution.py:212
  10.1 1.5 %dequantize.3 = (bf16[64,4352]{1,0:T(8,128)(2,1)S(1)}, bf16[64,4096]{1,0:T(8,128)(2,1)S(1)}, bf16[64,3840]{1,0:T(8,128)(2,1)S(1)}) custom-call(s32[128,12288]{1,0:T(8,128)S(1)} %copy-done, f32[96,128]{1,0:T(8,128)S(1)} %bitcast.39), custom_call_target="tpu_custom_call" | custom-call | tf_op jit(solution)/shard_map/dequantize/pallas_call | solution.py:148
  11.6 0.0 copy-start.3
  11.6 0.0 copy-start.4
  11.6 0.0 copy-start.5
  11.6 4.9 %collective-permute-done.refs_2_ = bf16[64,4352]{1,0:T(8,128)(2,1)S(1)} collective-permute-done((bf16[64,4352]{1,0:T(8,128)(2,1)S(1)}, bf16[64,4352]{1,0:T(8,128)(2,1)S(1)}, u32[]{:S(2)}, u32[]{:S(2)}) %collective-permute-start) | collective-permute-done | bytes 557088 | tf_op jit(solution)/shard_map/ppermute | solution.py:212
  16.5 0.1 add_convert_fusion
  16.6 3.0 %collective-permute-start.1 = (bf16[32,4352]{1,0:T(8,128)(2,1)S(1)}, bf16[32,4352]{1,0:T(8,128)(2,1)S(1)}, u32[]{:S(2)}, u32[]{:S(2)}) collective-permute-start(bf16[32,4352]{1,0:T(8,128)(2,1)S(1)} %add_convert_fusion), channel_id=1, source_target_pairs={{0,96},{1,97},{2,98},{3,99},{4,100},{5,101},{6,102},{7,103},{8,104... | collective-permute-start | bytes 835592 | tf_op jit(solution)/shard_map/ppermute | solution.py:212
  19.6 0.0 collective-permute-done.3.refs_6_
  19.6 0.1 add_convert_fusion.1
  19.7 1.7 %collective-permute-start.5 = (bf16[32,4096]{1,0:T(8,128)(2,1)S(1)}, bf16[32,4096]{1,0:T(8,128)(2,1)S(1)}, u32[]{:S(2)}, u32[]{:S(2)}) collective-permute-start(bf16[32,4096]{1,0:T(8,128)(2,1)S(1)} %add_convert_fusion.1), channel_id=1, source_target_pairs={{0,16},{1,17},{2,18},{3,19},{4,20},{5,21},{6,22},{7,23},{8,24},{9,... | collective-permute-start | bytes 786440 | tf_op jit(solution)/shard_map/ppermute | solution.py:212
  21.4 0.0 collective-permute-done.2.refs_10_
  21.4 0.1 add_convert_fusion.2
  21.4 0.1 collective-permute-start.7
  21.5 3.3 %collective-permute-done.1.refs_3_ = bf16[32,4352]{1,0:T(8,128)(2,1)S(1)} collective-permute-done((bf16[32,4352]{1,0:T(8,128)(2,1)S(1)}, bf16[32,4352]{1,0:T(8,128)(2,1)S(1)}, u32[]{:S(2)}, u32[]{:S(2)}) %collective-permute-start.1) | collective-permute-done | bytes 278560 | tf_op jit(solution)/shard_map/ppermute | solution.py:212
  24.8 0.1 add_convert_fusion.3
  24.8 1.9 %collective-permute-start.4 = (bf16[16,4352]{1,0:T(8,128)(2,1)S(1)}, bf16[16,4352]{1,0:T(8,128)(2,1)S(1)}, u32[]{:S(2)}, u32[]{:S(2)}) collective-permute-start(bf16[16,4352]{1,0:T(8,128)(2,1)S(1)} %add_convert_fusion.3), channel_id=1, source_target_pairs={{0,16},{1,17},{2,18},{3,19},{4,20},{5,21},{6,22},{7,23},{8,24},{9,... | collective-permute-start | bytes 417800 | tf_op jit(solution)/shard_map/ppermute | solution.py:212
  26.7 0.0 collective-permute-done.5.refs_7_
  26.7 0.1 add_convert_fusion.4
  26.8 0.1 collective-permute-start.6
  26.8 0.0 collective-permute-done.7.refs_11_
  26.9 2.6 %collective-permute-start.8 = (bf16[16,3840]{1,0:T(8,128)(2,1)S(1)}, bf16[16,3840]{1,0:T(8,128)(2,1)S(1)}, u32[]{:S(2)}, u32[]{:S(2)}) collective-permute-start(bf16[16,3840]{1,0:T(8,128)(2,1)S(1)} %add_convert_fusion.5), channel_id=1, source_target_pairs={{0,96},{1,97},{2,98},{3,99},{4,100},{5,101},{6,102},{7,103},{8,104... | collective-permute-start | bytes 368648 | tf_op jit(solution)/shard_map/ppermute | solution.py:212
  29.5 2.4 %collective-permute-done.8.refs_12_ = bf16[16,3840]{1,0:T(8,128)(2,1)S(1)} collective-permute-done((bf16[16,3840]{1,0:T(8,128)(2,1)S(1)}, bf16[16,3840]{1,0:T(8,128)(2,1)S(1)}, u32[]{:S(2)}, u32[]{:S(2)}) %collective-permute-start.8) | collective-permute-done | bytes 122912 | tf_op jit(solution)/shard_map/ppermute | solution.py:212
  31.9 0.0 collective-permute-done.6.refs_8_
  31.9 0.0 collective-permute-done.4.refs_4_
  31.9 0.9 %finish.1 = (bf16[2,2,2,96,128]{4,3,2,1,0:T(8,128)(2,1)S(1)}, f32[2,2,2,96,128]{4,3,2,1,0:T(8,128)S(1)}) custom-call(s32[16,96]{1,0:T(8,128)S(1)} %bitcast.40, bf16[64,4352]{1,0:T(8,128)(2,1)S(1)} %get-tuple-element.13.refs_1_, bf16[64,4352]{1,0:T(8,128)(2,1)S(1)} %collective-permute-done.refs_2_, bf16[32,4352]{1,0:T(8,128)(2,1)S(1)} %collective-permute-done.1.refs_3_, ...), custom_call_target="tpu_custom_call" | custom-call | tf_op jit(solution)/shard_map/finish/pallas_call | solution.py:190
  32.9 4.3 %collective-permute-start.9 = (bf16[2,2,2,96,128]{4,3,2,1,0:T(8,128)(2,1)S(1)}, bf16[2,2,2,96,128]{4,3,2,1,0:T(8,128)(2,1)S(1)}, u32[]{:S(2)}, u32[]{:S(2)}) collective-permute-start(bf16[2,2,2,96,128]{4,3,2,1,0:T(8,128)(2,1)S(1)} %get-tuple-element.22), channel_id=1, source_target_pairs={{0,1},{1,0},{2,3},{3,2},{4,5},{5,4},{6,7},{7,6},{8,9},{9,8},{10,11... | collective-permute-start | bytes 589832 | tf_op jit(solution)/shard_map/ppermute | solution.py:212
  37.1 1.1 %collective-permute-done.9 = bf16[2,2,2,96,128]{4,3,2,1,0:T(8,128)(2,1)S(1)} collective-permute-done((bf16[2,2,2,96,128]{4,3,2,1,0:T(8,128)(2,1)S(1)}, bf16[2,2,2,96,128]{4,3,2,1,0:T(8,128)(2,1)S(1)}, u32[]{:S(2)}, u32[]{:S(2)}) %collective-permute-start.9) | collective-permute-done | bytes 196640 | tf_op jit(solution)/shard_map/ppermute | solution.py:212
  38.3 2.8 %collective-permute-start.10 = (bf16[2,2,96,128]{3,2,1,0:T(8,128)(2,1)S(1)}, bf16[2,2,96,128]{3,2,1,0:T(8,128)(2,1)S(1)}, u32[]{:S(2)}, u32[]{:S(2)}) collective-permute-start(bf16[2,2,96,128]{3,2,1,0:T(8,128)(2,1)S(1)} %get-tuple-element.26), channel_id=1, source_target_pairs={{0,4},{1,7},{2,6},{3,5},{4,0},{5,3},{6,2},{7,1},{8,12},{9,15},{10,... | collective-permute-start | bytes 294920 | tf_op jit(solution)/shard_map/ppermute | solution.py:212
  41.1 1.9 %collective-permute-start.11 = (bf16[2,2,96,128]{3,2,1,0:T(8,128)(2,1)S(1)}, bf16[2,2,96,128]{3,2,1,0:T(8,128)(2,1)S(1)}, u32[]{:S(2)}, u32[]{:S(2)}) collective-permute-start(bf16[2,2,96,128]{3,2,1,0:T(8,128)(2,1)S(1)} %get-tuple-element.27), channel_id=1, source_target_pairs={{1,3},{3,1},{5,7},{7,5},{9,11},{11,9},{13,15},{15,13},{17,19},{19,... | collective-permute-start | bytes 294920 | tf_op jit(solution)/shard_map/ppermute | solution.py:212
  43.0 0.1 broadcast_multiply_fusion.2
  43.1 0.0 collective-permute-done.10
  43.1 3.3 %collective-permute-done.11 = bf16[2,2,96,128]{3,2,1,0:T(8,128)(2,1)S(1)} collective-permute-done((bf16[2,2,96,128]{3,2,1,0:T(8,128)(2,1)S(1)}, bf16[2,2,96,128]{3,2,1,0:T(8,128)(2,1)S(1)}, u32[]{:S(2)}, u32[]{:S(2)}) %collective-permute-start.11) | collective-permute-done | bytes 98336 | tf_op jit(solution)/shard_map/ppermute | solution.py:212
  46.5 3.4 %collective-permute-start.12 = (bf16[2,96,128]{2,1,0:T(8,128)(2,1)S(1)}, bf16[2,96,128]{2,1,0:T(8,128)(2,1)S(1)}, u32[]{:S(2)}, u32[]{:S(2)}) collective-permute-start(bf16[2,96,128]{2,1,0:T(8,128)(2,1)S(1)} %fusion.5), channel_id=1, source_target_pairs={{0,8},{1,9},{2,10},{3,11},{4,12},{5,13},{6,14},{7,15},{8,0},{9,1},... | collective-permute-start | bytes 147464 | tf_op jit(solution)/shard_map/ppermute | solution.py:212
  49.9 0.1 broadcast_multiply_fusion.1
  49.9 1.4 %collective-permute-done.12 = bf16[2,96,128]{2,1,0:T(8,128)(2,1)S(1)} collective-permute-done((bf16[2,96,128]{2,1,0:T(8,128)(2,1)S(1)}, bf16[2,96,128]{2,1,0:T(8,128)(2,1)S(1)}, u32[]{:S(2)}, u32[]{:S(2)}) %collective-permute-start.12) | collective-permute-done | bytes 49184 | tf_op jit(solution)/shard_map/ppermute | solution.py:212
  51.4 0.1 collective-permute-start.13
  51.5 0.1 broadcast_multiply_fusion
  52.3 0.4 collective-permute-done.13
  52.7 0.7 %divide_add_fusion = (f32[96,128]{1,0:T(8,128)}, f32[96,128]{1,0:T(8,128)}, f32[96,128]{1,0:T(8,128)}) fusion(f32[96,128]{1,0:T(8,128)S(1)} %bitcast.43, f32[]{:T(128)} %bitcast.12, f32[]{:T(128)} %bitcast.10, f32[96,128]{1,0:T(8,128)S(1)} %bitcast.42, f32[96,128]{1,0:T(8,128)S(1)} %collective-permute-done.13, f32[2,96,128]{2,1,0:T(8,128)S(1)} %fusion.3, ...), kind=kLoop, calls=%fused_computation.22 | loop fusion | flops 135168 | bytes 393224 | tf_op jit(solution)/shard_map/add | solution.py:207
  (13 shorter events, 0.2 us)
Async XLA Ops:
  0.6 4.0 %copy-start.1 = (f32[128,96]{0,1:T(8,128)S(1)}, f32[128,96]{0,1:T(8,128)}, u32[]{:S(2)}) copy-start(f32[128,96]{0,1:T(8,128)} %param.8) | copy-start | bytes 147460
  0.6 4.0 %copy-start = (s32[128,12288]{1,0:T(8,128)S(1)}, s32[128,12288]{1,0:T(8,128)}, u32[]{:S(2)}) copy-start(s32[128,12288]{1,0:T(8,128)} %refs_0_.7) | copy-start | bytes 18874372
  2.6 14.0 %collective-permute-start = (bf16[64,4352]{1,0:T(8,128)(2,1)S(1)}, bf16[64,4352]{1,0:T(8,128)(2,1)S(1)}, u32[]{:S(2)}, u32[]{:S(2)}) collective-permute-start(bf16[64,4352]{1,0:T(8,128)(2,1)S(1)} %first_rows.1), channel_id=1, source_target_pairs={{0,32},{1,33},{2,34},{3,35},{4,36},{5,37},{6,38},{7,39},{8,40},{9,... | collective-permute-start | bytes 1671176 | tf_op jit(solution)/shard_map/ppermute | solution.py:212
  5.3 14.3 %collective-permute-start.3 = (bf16[64,4096]{1,0:T(8,128)(2,1)S(1)}, bf16[64,4096]{1,0:T(8,128)(2,1)S(1)}, u32[]{:S(2)}, u32[]{:S(2)}) collective-permute-start(bf16[64,4096]{1,0:T(8,128)(2,1)S(1)} %dequantize.5), channel_id=1, source_target_pairs={{0,96},{1,97},{2,98},{3,99},{4,100},{5,101},{6,102},{7,103},{8,104... | collective-permute-start | bytes 1572872 | tf_op jit(solution)/shard_map/ppermute | solution.py:212
  8.4 23.6 %copy-start.2 = (s32[1,1,16,96]{3,2,1,0:T(8,128)S(1)}, s32[1,1,16,96]{3,2,1,0:T(8,128)}, u32[]{:S(2)}) copy-start(s32[1,1,16,96]{3,2,1,0:T(8,128)} %param.9) | copy-start | bytes 18436
  8.4 13.0 %collective-permute-start.2 = (bf16[64,3840]{1,0:T(8,128)(2,1)S(1)}, bf16[64,3840]{1,0:T(8,128)(2,1)S(1)}, u32[]{:S(2)}, u32[]{:S(2)}) collective-permute-start(bf16[64,3840]{1,0:T(8,128)(2,1)S(1)} %dequantize.4), channel_id=1, source_target_pairs={{0,16},{1,17},{2,18},{3,19},{4,20},{5,21},{6,22},{7,23},{8,24},{9,... | collective-permute-start | bytes 1474568 | tf_op jit(solution)/shard_map/ppermute | solution.py:212
  11.6 31.4 %copy-start.3 = (f32[1,12288]{1,0:T(1,128)S(1)}, f32[1,12288]{1,0:T(1,128)}, u32[]{:S(2)}) copy-start(f32[1,12288]{1,0:T(1,128)} %param.11) | copy-start | bytes 147460
  11.6 38.3 %copy-start.4 = (f32[1,12288]{1,0:T(1,128)S(1)}, f32[1,12288]{1,0:T(1,128)}, u32[]{:S(2)}) copy-start(f32[1,12288]{1,0:T(1,128)} %param.12) | copy-start | bytes 147460
  11.6 39.9 %copy-start.5 = (f32[1,12288]{1,0:T(1,128)S(1)}, f32[1,12288]{1,0:T(1,128)}, u32[]{:S(2)}) copy-start(f32[1,12288]{1,0:T(1,128)} %param.10) | copy-start | bytes 147460
  16.6 8.2 %collective-permute-start.1 = (bf16[32,4352]{1,0:T(8,128)(2,1)S(1)}, bf16[32,4352]{1,0:T(8,128)(2,1)S(1)}, u32[]{:S(2)}, u32[]{:S(2)}) collective-permute-start(bf16[32,4352]{1,0:T(8,128)(2,1)S(1)} %add_convert_fusion), channel_id=1, source_target_pairs={{0,96},{1,97},{2,98},{3,99},{4,100},{5,101},{6,102},{7,103},{8,104... | collective-permute-start | bytes 835592 | tf_op jit(solution)/shard_map/ppermute | solution.py:212
  19.7 7.0 %collective-permute-start.5 = (bf16[32,4096]{1,0:T(8,128)(2,1)S(1)}, bf16[32,4096]{1,0:T(8,128)(2,1)S(1)}, u32[]{:S(2)}, u32[]{:S(2)}) collective-permute-start(bf16[32,4096]{1,0:T(8,128)(2,1)S(1)} %add_convert_fusion.1), channel_id=1, source_target_pairs={{0,16},{1,17},{2,18},{3,19},{4,20},{5,21},{6,22},{7,23},{8,24},{9,... | collective-permute-start | bytes 786440 | tf_op jit(solution)/shard_map/ppermute | solution.py:212
  21.4 5.4 %collective-permute-start.7 = (bf16[32,3840]{1,0:T(8,128)(2,1)S(1)}, bf16[32,3840]{1,0:T(8,128)(2,1)S(1)}, u32[]{:S(2)}, u32[]{:S(2)}) collective-permute-start(bf16[32,3840]{1,0:T(8,128)(2,1)S(1)} %add_convert_fusion.2), channel_id=1, source_target_pairs={{0,32},{1,33},{2,34},{3,35},{4,36},{5,37},{6,38},{7,39},{8,40},{9,... | collective-permute-start | bytes 737288 | tf_op jit(solution)/shard_map/ppermute | solution.py:212
  24.8 7.1 %collective-permute-start.4 = (bf16[16,4352]{1,0:T(8,128)(2,1)S(1)}, bf16[16,4352]{1,0:T(8,128)(2,1)S(1)}, u32[]{:S(2)}, u32[]{:S(2)}) collective-permute-start(bf16[16,4352]{1,0:T(8,128)(2,1)S(1)} %add_convert_fusion.3), channel_id=1, source_target_pairs={{0,16},{1,17},{2,18},{3,19},{4,20},{5,21},{6,22},{7,23},{8,24},{9,... | collective-permute-start | bytes 417800 | tf_op jit(solution)/shard_map/ppermute | solution.py:212
  26.8 5.2 %collective-permute-start.6 = (bf16[16,4096]{1,0:T(8,128)(2,1)S(1)}, bf16[16,4096]{1,0:T(8,128)(2,1)S(1)}, u32[]{:S(2)}, u32[]{:S(2)}) collective-permute-start(bf16[16,4096]{1,0:T(8,128)(2,1)S(1)} %add_convert_fusion.4), channel_id=1, source_target_pairs={{0,32},{1,33},{2,34},{3,35},{4,36},{5,37},{6,38},{7,39},{8,40},{9,... | collective-permute-start | bytes 393224 | tf_op jit(solution)/shard_map/ppermute | solution.py:212
  26.9 5.0 %collective-permute-start.8 = (bf16[16,3840]{1,0:T(8,128)(2,1)S(1)}, bf16[16,3840]{1,0:T(8,128)(2,1)S(1)}, u32[]{:S(2)}, u32[]{:S(2)}) collective-permute-start(bf16[16,3840]{1,0:T(8,128)(2,1)S(1)} %add_convert_fusion.5), channel_id=1, source_target_pairs={{0,96},{1,97},{2,98},{3,99},{4,100},{5,101},{6,102},{7,103},{8,104... | collective-permute-start | bytes 368648 | tf_op jit(solution)/shard_map/ppermute | solution.py:212
  32.9 5.3 %collective-permute-start.9 = (bf16[2,2,2,96,128]{4,3,2,1,0:T(8,128)(2,1)S(1)}, bf16[2,2,2,96,128]{4,3,2,1,0:T(8,128)(2,1)S(1)}, u32[]{:S(2)}, u32[]{:S(2)}) collective-permute-start(bf16[2,2,2,96,128]{4,3,2,1,0:T(8,128)(2,1)S(1)} %get-tuple-element.22), channel_id=1, source_target_pairs={{0,1},{1,0},{2,3},{3,2},{4,5},{5,4},{6,7},{7,6},{8,9},{9,8},{10,11... | collective-permute-start | bytes 589832 | tf_op jit(solution)/shard_map/ppermute | solution.py:212
  38.3 4.8 %collective-permute-start.10 = (bf16[2,2,96,128]{3,2,1,0:T(8,128)(2,1)S(1)}, bf16[2,2,96,128]{3,2,1,0:T(8,128)(2,1)S(1)}, u32[]{:S(2)}, u32[]{:S(2)}) collective-permute-start(bf16[2,2,96,128]{3,2,1,0:T(8,128)(2,1)S(1)} %get-tuple-element.26), channel_id=1, source_target_pairs={{0,4},{1,7},{2,6},{3,5},{4,0},{5,3},{6,2},{7,1},{8,12},{9,15},{10,... | collective-permute-start | bytes 294920 | tf_op jit(solution)/shard_map/ppermute | solution.py:212
  41.1 5.3 %collective-permute-start.11 = (bf16[2,2,96,128]{3,2,1,0:T(8,128)(2,1)S(1)}, bf16[2,2,96,128]{3,2,1,0:T(8,128)(2,1)S(1)}, u32[]{:S(2)}, u32[]{:S(2)}) collective-permute-start(bf16[2,2,96,128]{3,2,1,0:T(8,128)(2,1)S(1)} %get-tuple-element.27), channel_id=1, source_target_pairs={{1,3},{3,1},{5,7},{7,5},{9,11},{11,9},{13,15},{15,13},{17,19},{19,... | collective-permute-start | bytes 294920 | tf_op jit(solution)/shard_map/ppermute | solution.py:212
  46.5 4.9 %collective-permute-start.12 = (bf16[2,96,128]{2,1,0:T(8,128)(2,1)S(1)}, bf16[2,96,128]{2,1,0:T(8,128)(2,1)S(1)}, u32[]{:S(2)}, u32[]{:S(2)}) collective-permute-start(bf16[2,96,128]{2,1,0:T(8,128)(2,1)S(1)} %fusion.5), channel_id=1, source_target_pairs={{0,8},{1,9},{2,10},{3,11},{4,12},{5,13},{6,14},{7,15},{8,0},{9,1},... | collective-permute-start | bytes 147464 | tf_op jit(solution)/shard_map/ppermute | solution.py:212
  51.4 1.3 %collective-permute-start.13 = (f32[96,128]{1,0:T(8,128)S(1)}, f32[96,128]{1,0:T(8,128)S(1)}, u32[]{:S(2)}, u32[]{:S(2)}) collective-permute-start(f32[96,128]{1,0:T(8,128)S(1)} %slice_bitcast_fusion.1), channel_id=1, source_target_pairs={{0,1},{1,0},{2,3},{3,2},{4,5},{5,4},{6,7},{7,6},{8,9},{9,8},{10,11... | collective-permute-start | bytes 147464 | tf_op jit(solution)/shard_map/ppermute | solution.py:262

commit v4 on v3

--- a/solution.py
+++ b/solution.py
@@ -17,10 +17,11 @@
 COLUMNS = BLOCKS * LANES
 TILE = 16
 PIECES = (
-    (0, 34, "PQZ", "PQZ", False),
-    (34, 32, "QZP", "QZP", False),
-    (66, 30, "ZPQ", "ZPQ", False),
+    (0, 34, "PZQ"),
+    (34, 32, "ZQP"),
+    (66, 30, "QPZ"),
 )
+SUMS = ((0, 1), (1, 1), (2, 1), (0, 2), (1, 2), (2, 2))
 FIRST = 0
 AXES = ("node", "wide")
 VMEM_LIMIT = 32 * 1024 * 1024
@@ -35,17 +36,13 @@
     return (label["Q"] << 2) | ((label["P"] ^ label["Q"]) << 1) | label["Z"]
 
 
-Y_FLIPS = ((3, 0), (2, 1))
+Y_FLIPS = (3, 1, 2, 0)
 
 
 def wide_at(wide, z_flip, y_flip, core):
     high = ((wide >> 2) & 1) ^ (y_flip >> 1)
     low = (((wide >> 1) ^ (wide >> 2)) & 1) ^ (y_flip & 1)
     return ((wide >> 3) ^ z_flip) << 3 | high << 2 | (high ^ low) << 1 | core
-
-
-def y_route(slot):
-    return [(b, wide_at(b, 0, Y_FLIPS[b & 1][slot], b & 1)) for b in range(16) if Y_FLIPS[b & 1][slot]]
 
 
 def pairs(piece, *steps):
@@ -54,19 +51,14 @@
         for wide in range(16):
             label = bits(node)
             for step in steps:
-                label[piece[2 + (wide & 1)][step]] ^= 1
+                label[piece[2][step]] ^= 1
             result.append((node * 16 + wide, node_of(label) * 16 + wide))
     return result
 
 
 def block_row(piece, relative):
     mine = bits(lax.axis_index("node"))
-    core = lax.axis_index("wide") & 1
-    label = {}
-    for dim in "PQZ":
-        flip0 = relative[piece[2].index(dim)]
-        flip1 = relative[piece[3].index(dim)]
-        label[dim] = mine[dim] ^ (flip0 + core * (flip1 - flip0))
+    label = {dim: mine[dim] ^ relative[piece[2].index(dim)] for dim in "PQZ"}
     return pl.multiple_of(node_of(label) * TILE, TILE)
 
 
@@ -173,19 +165,16 @@
             rows[pl.ds(at, TILE, stride=BLOCKS), :] = coded.astype(jnp.float32) * scale[:, at : at + 1]
     wide = lax.axis_index("wide")
     core = wide & 1
-    for slot in range(2):
-        first, second = Y_FLIPS[0][slot], Y_FLIPS[1][slot]
-        for ref, server in ((send_ref, 1 - core), (keep_ref, core)):
-            y_flip = first + server * (second - first)
-            for at, flip in enumerate((1, 0)):
-                for owner in range(2):
-                    row = pl.multiple_of(wide_at(wide, flip, y_flip, (server + owner + 1) & 1) * BLOCKS, 8)
-                    ref[slot, at, owner] = rows[pl.ds(row, BLOCKS), :].astype(ref.dtype)
+    for slot, y_flip in enumerate(Y_FLIPS):
+        for z_slot, z_flip in enumerate((1, 0)):
+            for ref, owner in ((send_ref, 1 - core), (keep_ref, core)):
+                row = pl.multiple_of(wide_at(wide, z_flip, y_flip, owner) * BLOCKS, 8)
+                ref[slot, z_slot] = rows[pl.ds(row, BLOCKS), :].astype(ref.dtype)
 
 
 def finish(requant, parts):
     vmem = pl.BlockSpec(memory_space=pltpu.VMEM)
-    shape = (2, 2, 2, BLOCKS, LANES)
+    shape = (4, 2, BLOCKS, LANES)
     counts = [len(arrays) for arrays in parts]
     return pl.pallas_call(
         lambda *refs: finish_kernel(counts, *refs),
@@ -223,7 +212,7 @@
     codes = pltpu.with_memory_space_constraint(grad_codes, pltpu.HBM)
     scales = code_scales.T
     scales_hbm = pltpu.with_memory_space_constraint(scales, pltpu.HBM)
-    firsts, parts = [], []
+    firsts = []
     for n, piece in enumerate(PIECES):
         if n == FIRST:
             rows = first_rows(piece, codes, scales_hbm)
@@ -231,35 +220,21 @@
             (rows,) = dequantize([(piece, 1)], grad_codes, scales)
         firsts.append(send(rows, AXES, pairs(piece, 0)))
     keeps = dequantize([(piece, 0) for piece in PIECES], grad_codes, scales)
+    parts = [[keep, first] for keep, first in zip(keeps, firsts)]
     last = None
-    for piece, first, keep in zip(PIECES, firsts, keeps):
+    for n, step in SUMS:
         if last is not None:
-            first, last = lax.optimization_barrier((first, last))
-        parts.append([keep, first])
-        if piece[4]:
-            for n, steps in enumerate(((1, 2), (1,), (2,))):
-                cut = slice(n * TILE, (n + 1) * TILE)
-                last = total(keep[cut], first[cut]).astype(jnp.bfloat16)
-                parts[-1].append(send(last, AXES, pairs(piece, *steps)))
-        else:
-            cut = slice(0, 2 * TILE)
-            last = total(keep[cut], first[cut]).astype(jnp.bfloat16)
-            parts[-1].append(send(last, AXES, pairs(piece, 1)))
-    for piece, arrays in zip(PIECES, parts):
-        if not piece[4]:
-            arrays[2], last = lax.optimization_barrier((arrays[2], last))
-            keep, first, second = arrays
-            cut = slice(2 * TILE, 3 * TILE)
-            last = total(keep[cut], first[cut], second[:TILE]).astype(jnp.bfloat16)
-            arrays.append(send(last, AXES, pairs(piece, 2)))
+            parts[n][step], last = lax.optimization_barrier((parts[n][step], last))
+        cut = slice(0, 2 * TILE) if step == 1 else slice(2 * TILE, 3 * TILE)
+        last = total(*[array[cut] for array in parts[n][:2]], *[array[:TILE] for array in parts[n][2:]])
+        last = last.astype(jnp.bfloat16)
+        parts[n].append(send(last, AXES, pairs(PIECES[n], step)))
     other_core = [(b, b ^ 1) for b in range(16)]
     away, near = finish(requant_scales.reshape(TILE, BLOCKS), parts)
     near = total(near, send(away, "wide", other_core))
-    flipped = [send(near[slot], "wide", y_route(slot)) for slot in range(2)]
-    stays = jnp.where((lax.axis_index("wide") & 1) == 0, near[1], 0.0)
-    chip = total(stays, *flipped)
-    chip = total(chip[1], send(chip[0], "wide", [(b, b ^ 8) for b in range(16)]))
-    gradient = total(chip[1], lax.ppermute(chip[0], "wide", other_core))
+    routes = [[(b, wide_at(b, 0, y_flip, b & 1)) for b in range(16)] for y_flip in Y_FLIPS[:3]]
+    chip = total(near[3], *[send(near[slot], "wide", route) for slot, route in enumerate(routes)])
+    gradient = total(chip[1], send(chip[0], "wide", [(b, b ^ 8) for b in range(16)]))
     tall = (BLOCKS, LANES)
     outs = adamw(gradient, params.reshape(tall), first_moment.reshape(tall), second_moment.reshape(tall), step_count)
     return tuple(out.reshape(1, COLUMNS) for out in outs)

time: 53.5 us -> 52.1 us (0.974)
  the two profiles are of different devices: /device:TPU:1 before, /device:TPU:0 now
where the time goes in v4:
time: 52.1 us; the launch traced here: 51.5 us
  starting transfers between devices  24.3 us (47%)
  waiting for transfers between devices  18.8 us (36%)
  Pallas kernels  5.49 us (11%)
  between operations  1.53 us (3%)
  other arithmetic  1.25 us (2%)
    ppermute x14, starting transfers between devices, send(): return lax.ppermute(array.astype(jnp.bfloat16), axes, route)  24.3 us
    ppermute x14, waiting for transfers between devices, send(): return lax.ppermute(array.astype(jnp.bfloat16), axes, route)  18.8 us
    pallas_call x3, Pallas kernels, dequantize(): pl.pallas_call(lambda *refs: dequantize_kernel(parts, *refs), out_shape=[...  2.67 us
    pallas_call x1, Pallas kernels, first_rows(): pl.pallas_call(lambda *refs: first_kernel(piece, *refs), out_shape=jax.Sh...  1.89 us
  transfers between devices with their start and end apart: 14, of which 9 were waited for; matrix products, arithmetic and copies ran while one was open for 1% of the time, Pallas kernels for 5%

profile of v4, /device:TPU:0, one launch (start us, length us, event | category | flops | bytes accessed | tf_op | source)
XLA Modules:
  0.0 51.5 jit_solution(16973982635161697723)
XLA Ops:
  0.6 1.9 %first_rows.1 = bf16[64,4352]{1,0:T(8,128)(2,1)S(1)} custom-call(s32[128,12288]{1,0:T(8,128)} %refs_0_.7, f32[96,128]{1,0:T(8,128)} %bitcast.36), custom_call_target="tpu_custom_call" | custom-call | tf_op jit(solution)/shard_map/first_rows/pallas_call | solution.py:106
  2.6 1.7 %collective-permute-start = (bf16[64,4352]{1,0:T(8,128)(2,1)S(1)}, bf16[64,4352]{1,0:T(8,128)(2,1)S(1)}, u32[]{:S(2)}, u32[]{:S(2)}) collective-permute-start(bf16[64,4352]{1,0:T(8,128)(2,1)S(1)} %first_rows.1), channel_id=1, source_target_pairs={{0,32},{1,33},{2,34},{3,35},{4,36},{5,37},{6,38},{7,39},{8,40},{9,... | collective-permute-start | bytes 1671176 | tf_op jit(solution)/shard_map/ppermute | solution.py:201
  4.2 0.6 %dequantize.5 = bf16[64,4096]{1,0:T(8,128)(2,1)S(1)} custom-call(s32[128,12288]{1,0:T(8,128)S(1)} %copy-done, f32[96,128]{1,0:T(8,128)S(1)} %bitcast.37), custom_call_target="tpu_custom_call" | custom-call | tf_op jit(solution)/shard_map/dequantize/pallas_call | solution.py:140
  4.8 2.0 %collective-permute-start.3 = (bf16[64,4096]{1,0:T(8,128)(2,1)S(1)}, bf16[64,4096]{1,0:T(8,128)(2,1)S(1)}, u32[]{:S(2)}, u32[]{:S(2)}) collective-permute-start(bf16[64,4096]{1,0:T(8,128)(2,1)S(1)} %dequantize.5), channel_id=1, source_target_pairs={{0,16},{1,17},{2,18},{3,19},{4,20},{5,21},{6,22},{7,23},{8,24},{9,... | collective-permute-start | bytes 1572872 | tf_op jit(solution)/shard_map/ppermute | solution.py:201
  6.8 0.6 %dequantize.4 = bf16[64,3840]{1,0:T(8,128)(2,1)S(1)} custom-call(s32[128,12288]{1,0:T(8,128)S(1)} %copy-done, f32[96,128]{1,0:T(8,128)S(1)} %bitcast.38), custom_call_target="tpu_custom_call" | custom-call | tf_op jit(solution)/shard_map/dequantize/pallas_call | solution.py:140
  7.4 0.0 copy-start.2
  7.4 0.0 copy-start.3
  7.4 2.5 %collective-permute-start.2 = (bf16[64,3840]{1,0:T(8,128)(2,1)S(1)}, bf16[64,3840]{1,0:T(8,128)(2,1)S(1)}, u32[]{:S(2)}, u32[]{:S(2)}) collective-permute-start(bf16[64,3840]{1,0:T(8,128)(2,1)S(1)} %dequantize.4), channel_id=1, source_target_pairs={{0,96},{1,97},{2,98},{3,99},{4,100},{5,101},{6,102},{7,103},{8,104... | collective-permute-start | bytes 1474568 | tf_op jit(solution)/shard_map/ppermute | solution.py:201
  9.9 1.5 %dequantize.3 = (bf16[64,4352]{1,0:T(8,128)(2,1)S(1)}, bf16[64,4096]{1,0:T(8,128)(2,1)S(1)}, bf16[64,3840]{1,0:T(8,128)(2,1)S(1)}) custom-call(s32[128,12288]{1,0:T(8,128)S(1)} %copy-done, f32[96,128]{1,0:T(8,128)S(1)} %bitcast.39), custom_call_target="tpu_custom_call" | custom-call | tf_op jit(solution)/shard_map/dequantize/pallas_call | solution.py:140
  11.4 0.0 copy-start.4
  11.4 0.0 copy-start.5
  11.4 5.4 %collective-permute-done.refs_2_ = bf16[64,4352]{1,0:T(8,128)(2,1)S(1)} collective-permute-done((bf16[64,4352]{1,0:T(8,128)(2,1)S(1)}, bf16[64,4352]{1,0:T(8,128)(2,1)S(1)}, u32[]{:S(2)}, u32[]{:S(2)}) %collective-permute-start) | collective-permute-done | bytes 557088 | tf_op jit(solution)/shard_map/ppermute | solution.py:201
  16.8 0.1 add_convert_fusion
  16.9 2.2 %collective-permute-start.1 = (bf16[32,4352]{1,0:T(8,128)(2,1)S(1)}, bf16[32,4352]{1,0:T(8,128)(2,1)S(1)}, u32[]{:S(2)}, u32[]{:S(2)}) collective-permute-start(bf16[32,4352]{1,0:T(8,128)(2,1)S(1)} %add_convert_fusion), channel_id=1, source_target_pairs={{0,16},{1,17},{2,18},{3,19},{4,20},{5,21},{6,22},{7,23},{8,24},{9,... | collective-permute-start | bytes 835592 | tf_op jit(solution)/shard_map/ppermute | solution.py:201
  19.1 0.0 collective-permute-done.3.refs_6_
  19.2 0.1 add_convert_fusion.1
  19.2 2.8 %collective-permute-start.5 = (bf16[32,4096]{1,0:T(8,128)(2,1)S(1)}, bf16[32,4096]{1,0:T(8,128)(2,1)S(1)}, u32[]{:S(2)}, u32[]{:S(2)}) collective-permute-start(bf16[32,4096]{1,0:T(8,128)(2,1)S(1)} %add_convert_fusion.1), channel_id=1, source_target_pairs={{0,96},{1,97},{2,98},{3,99},{4,100},{5,101},{6,102},{7,103},{8,104... | collective-permute-start | bytes 786440 | tf_op jit(solution)/shard_map/ppermute | solution.py:201
  22.1 0.0 collective-permute-done.2.refs_10_
  22.1 0.1 add_convert_fusion.2
  22.1 0.3 collective-permute-start.7
  22.4 2.5 %collective-permute-done.1.refs_3_ = bf16[32,4352]{1,0:T(8,128)(2,1)S(1)} collective-permute-done((bf16[32,4352]{1,0:T(8,128)(2,1)S(1)}, bf16[32,4352]{1,0:T(8,128)(2,1)S(1)}, u32[]{:S(2)}, u32[]{:S(2)}) %collective-permute-start.1) | collective-permute-done | bytes 278560 | tf_op jit(solution)/shard_map/ppermute | solution.py:201
  24.9 0.1 add_convert_fusion.3
  25.0 2.8 %collective-permute-start.4 = (bf16[16,4352]{1,0:T(8,128)(2,1)S(1)}, bf16[16,4352]{1,0:T(8,128)(2,1)S(1)}, u32[]{:S(2)}, u32[]{:S(2)}) collective-permute-start(bf16[16,4352]{1,0:T(8,128)(2,1)S(1)} %add_convert_fusion.3), channel_id=1, source_target_pairs={{0,96},{1,97},{2,98},{3,99},{4,100},{5,101},{6,102},{7,103},{8,104... | collective-permute-start | bytes 417800 | tf_op jit(solution)/shard_map/ppermute | solution.py:201
  27.8 0.0 collective-permute-done.5.refs_7_
  27.8 0.1 add_convert_fusion.4
  27.9 0.3 collective-permute-start.6
  28.2 0.3 collective-permute-done.7.refs_11_
  28.5 1.5 %collective-permute-start.8 = (bf16[16,3840]{1,0:T(8,128)(2,1)S(1)}, bf16[16,3840]{1,0:T(8,128)(2,1)S(1)}, u32[]{:S(2)}, u32[]{:S(2)}) collective-permute-start(bf16[16,3840]{1,0:T(8,128)(2,1)S(1)} %add_convert_fusion.5), channel_id=1, source_target_pairs={{0,16},{1,17},{2,18},{3,19},{4,20},{5,21},{6,22},{7,23},{8,24},{9,... | collective-permute-start | bytes 368648 | tf_op jit(solution)/shard_map/ppermute | solution.py:201
  30.1 3.4 %collective-permute-done.8.refs_12_ = bf16[16,3840]{1,0:T(8,128)(2,1)S(1)} collective-permute-done((bf16[16,3840]{1,0:T(8,128)(2,1)S(1)}, bf16[16,3840]{1,0:T(8,128)(2,1)S(1)}, u32[]{:S(2)}, u32[]{:S(2)}) %collective-permute-start.8) | collective-permute-done | bytes 122912 | tf_op jit(solution)/shard_map/ppermute | solution.py:201
  33.5 0.0 collective-permute-done.6.refs_8_
  33.5 0.0 collective-permute-done.4.refs_4_
  33.5 0.9 %finish.1 = (bf16[4,2,96,128]{3,2,1,0:T(8,128)(2,1)S(1)}, f32[4,2,96,128]{3,2,1,0:T(8,128)S(1)}) custom-call(s32[16,96]{1,0:T(8,128)S(1)} %bitcast.40, bf16[64,4352]{1,0:T(8,128)(2,1)S(1)} %get-tuple-element.13.refs_1_, bf16[64,4352]{1,0:T(8,128)(2,1)S(1)} %collective-permute-done.refs_2_, bf16[32,4352]{1,0:T(8,128)(2,1)S(1)} %collective-permute-done.1.refs_3_, ...), custom_call_target="tpu_custom_call" | custom-call | tf_op jit(solution)/shard_map/finish/pallas_call | solution.py:179
  34.4 0.1 collective-permute-start.9
  34.5 0.0 copy-done.3
  34.5 0.1 broadcast_multiply_fusion.2
  34.6 1.4 %collective-permute-done.9 = bf16[4,2,96,128]{3,2,1,0:T(8,128)(2,1)S(1)} collective-permute-done((bf16[4,2,96,128]{3,2,1,0:T(8,128)(2,1)S(1)}, bf16[4,2,96,128]{3,2,1,0:T(8,128)(2,1)S(1)}, u32[]{:S(2)}, u32[]{:S(2)}) %collective-permute-start.9) | collective-permute-done | bytes 196640 | tf_op jit(solution)/shard_map/ppermute | solution.py:201
  35.9 0.1 fusion.7
  36.0 3.3 %collective-permute-start.10 = (bf16[2,96,128]{2,1,0:T(8,128)(2,1)S(1)}, bf16[2,96,128]{2,1,0:T(8,128)(2,1)S(1)}, u32[]{:S(2)}, u32[]{:S(2)}) collective-permute-start(bf16[2,96,128]{2,1,0:T(8,128)(2,1)S(1)} %get-tuple-element.28), channel_id=1, source_target_pairs={{0,4},{1,5},{2,6},{3,7},{4,0},{5,1},{6,2},{7,3},{8,12},{9,13},{10,... | collective-permute-start | bytes 147464 | tf_op jit(solution)/shard_map/ppermute | solution.py:201
  39.3 0.7 %collective-permute-start.11 = (bf16[2,96,128]{2,1,0:T(8,128)(2,1)S(1)}, bf16[2,96,128]{2,1,0:T(8,128)(2,1)S(1)}, u32[]{:S(2)}, u32[]{:S(2)}) collective-permute-start(bf16[2,96,128]{2,1,0:T(8,128)(2,1)S(1)} %get-tuple-element.30), channel_id=1, source_target_pairs={{0,2},{1,3},{2,0},{3,1},{4,6},{5,7},{6,4},{7,5},{8,10},{9,11},{10,... | collective-permute-start | bytes 147464 | tf_op jit(solution)/shard_map/ppermute | solution.py:201
  40.0 0.4 collective-permute-start.12
  40.4 0.1 broadcast_multiply_fusion.1
  40.4 1.3 %collective-permute-done.10 = bf16[2,96,128]{2,1,0:T(8,128)(2,1)S(1)} collective-permute-done((bf16[2,96,128]{2,1,0:T(8,128)(2,1)S(1)}, bf16[2,96,128]{2,1,0:T(8,128)(2,1)S(1)}, u32[]{:S(2)}, u32[]{:S(2)}) %collective-permute-start.10) | collective-permute-done | bytes 49184 | tf_op jit(solution)/shard_map/ppermute | solution.py:201
  41.7 1.7 %collective-permute-done.11 = bf16[2,96,128]{2,1,0:T(8,128)(2,1)S(1)} collective-permute-done((bf16[2,96,128]{2,1,0:T(8,128)(2,1)S(1)}, bf16[2,96,128]{2,1,0:T(8,128)(2,1)S(1)}, u32[]{:S(2)}, u32[]{:S(2)}) %collective-permute-start.11) | collective-permute-done | bytes 49184 | tf_op jit(solution)/shard_map/ppermute | solution.py:201
  43.4 1.9 %collective-permute-done.12 = bf16[2,96,128]{2,1,0:T(8,128)(2,1)S(1)} collective-permute-done((bf16[2,96,128]{2,1,0:T(8,128)(2,1)S(1)}, bf16[2,96,128]{2,1,0:T(8,128)(2,1)S(1)}, u32[]{:S(2)}, u32[]{:S(2)}) %collective-permute-start.12) | collective-permute-done | bytes 49184 | tf_op jit(solution)/shard_map/ppermute | solution.py:201
  45.3 3.7 %collective-permute-start.13 = (bf16[96,128]{1,0:T(8,128)(2,1)S(1)}, bf16[96,128]{1,0:T(8,128)(2,1)S(1)}, u32[]{:S(2)}, u32[]{:S(2)}) collective-permute-start(bf16[96,128]{1,0:T(8,128)(2,1)S(1)} %fusion.5), channel_id=1, source_target_pairs={{0,8},{1,9},{2,10},{3,11},{4,12},{5,13},{6,14},{7,15},{8,0},{9,1},... | collective-permute-start | bytes 73736 | tf_op jit(solution)/shard_map/ppermute | solution.py:201
  49.0 0.1 broadcast_multiply_fusion
  49.8 1.0 %collective-permute-done.13 = bf16[96,128]{1,0:T(8,128)(2,1)S(1)} collective-permute-done((bf16[96,128]{1,0:T(8,128)(2,1)S(1)}, bf16[96,128]{1,0:T(8,128)(2,1)S(1)}, u32[]{:S(2)}, u32[]{:S(2)}) %collective-permute-start.13) | collective-permute-done | bytes 24608 | tf_op jit(solution)/shard_map/ppermute | solution.py:201
  50.8 0.7 %divide_add_fusion = (f32[96,128]{1,0:T(8,128)}, f32[96,128]{1,0:T(8,128)}, f32[96,128]{1,0:T(8,128)}) fusion(f32[96,128]{1,0:T(8,128)S(1)} %bitcast.43, f32[]{:T(128)} %bitcast.11, f32[]{:T(128)} %bitcast.9, f32[96,128]{1,0:T(8,128)S(1)} %bitcast.42, bf16[96,128]{1,0:T(8,128)(2,1)S(1)} %collective-permute-done.13, f32[2,96,128]{2,1,0:T(8,128)S(1)} %fusion.2, ...), kind=kLoop, calls=%fused_computation.19 | loop fusion | flops 147456 | bytes 368648 | tf_op jit(solution)/shard_map/add | solution.py:196
  (11 shorter events, 0.1 us)
Async XLA Ops:
  0.6 3.6 %copy-start.1 = (f32[128,96]{0,1:T(8,128)S(1)}, f32[128,96]{0,1:T(8,128)}, u32[]{:S(2)}) copy-start(f32[128,96]{0,1:T(8,128)} %param.8) | copy-start | bytes 147460
  0.6 3.6 %copy-start = (s32[128,12288]{1,0:T(8,128)S(1)}, s32[128,12288]{1,0:T(8,128)}, u32[]{:S(2)}) copy-start(s32[128,12288]{1,0:T(8,128)} %refs_0_.7) | copy-start | bytes 18874372
  2.6 14.3 %collective-permute-start = (bf16[64,4352]{1,0:T(8,128)(2,1)S(1)}, bf16[64,4352]{1,0:T(8,128)(2,1)S(1)}, u32[]{:S(2)}, u32[]{:S(2)}) collective-permute-start(bf16[64,4352]{1,0:T(8,128)(2,1)S(1)} %first_rows.1), channel_id=1, source_target_pairs={{0,32},{1,33},{2,34},{3,35},{4,36},{5,37},{6,38},{7,39},{8,40},{9,... | collective-permute-start | bytes 1671176 | tf_op jit(solution)/shard_map/ppermute | solution.py:201
  4.8 14.3 %collective-permute-start.3 = (bf16[64,4096]{1,0:T(8,128)(2,1)S(1)}, bf16[64,4096]{1,0:T(8,128)(2,1)S(1)}, u32[]{:S(2)}, u32[]{:S(2)}) collective-permute-start(bf16[64,4096]{1,0:T(8,128)(2,1)S(1)} %dequantize.5), channel_id=1, source_target_pairs={{0,16},{1,17},{2,18},{3,19},{4,20},{5,21},{6,22},{7,23},{8,24},{9,... | collective-permute-start | bytes 1572872 | tf_op jit(solution)/shard_map/ppermute | solution.py:201
  7.4 26.1 %copy-start.2 = (s32[1,1,16,96]{3,2,1,0:T(8,128)S(1)}, s32[1,1,16,96]{3,2,1,0:T(8,128)}, u32[]{:S(2)}) copy-start(s32[1,1,16,96]{3,2,1,0:T(8,128)} %param.9) | copy-start | bytes 18436
  7.4 27.1 %copy-start.3 = (f32[1,12288]{1,0:T(1,128)S(1)}, f32[1,12288]{1,0:T(1,128)}, u32[]{:S(2)}) copy-start(f32[1,12288]{1,0:T(1,128)} %param.11) | copy-start | bytes 147460
  7.4 14.6 %collective-permute-start.2 = (bf16[64,3840]{1,0:T(8,128)(2,1)S(1)}, bf16[64,3840]{1,0:T(8,128)(2,1)S(1)}, u32[]{:S(2)}, u32[]{:S(2)}) collective-permute-start(bf16[64,3840]{1,0:T(8,128)(2,1)S(1)} %dequantize.4), channel_id=1, source_target_pairs={{0,96},{1,97},{2,98},{3,99},{4,100},{5,101},{6,102},{7,103},{8,104... | collective-permute-start | bytes 1474568 | tf_op jit(solution)/shard_map/ppermute | solution.py:201
  11.4 29.0 %copy-start.4 = (f32[1,12288]{1,0:T(1,128)S(1)}, f32[1,12288]{1,0:T(1,128)}, u32[]{:S(2)}) copy-start(f32[1,12288]{1,0:T(1,128)} %param.12) | copy-start | bytes 147460
  11.4 37.6 %copy-start.5 = (f32[1,12288]{1,0:T(1,128)S(1)}, f32[1,12288]{1,0:T(1,128)}, u32[]{:S(2)}) copy-start(f32[1,12288]{1,0:T(1,128)} %param.10) | copy-start | bytes 147460
  16.9 8.0 %collective-permute-start.1 = (bf16[32,4352]{1,0:T(8,128)(2,1)S(1)}, bf16[32,4352]{1,0:T(8,128)(2,1)S(1)}, u32[]{:S(2)}, u32[]{:S(2)}) collective-permute-start(bf16[32,4352]{1,0:T(8,128)(2,1)S(1)} %add_convert_fusion), channel_id=1, source_target_pairs={{0,16},{1,17},{2,18},{3,19},{4,20},{5,21},{6,22},{7,23},{8,24},{9,... | collective-permute-start | bytes 835592 | tf_op jit(solution)/shard_map/ppermute | solution.py:201
  19.2 8.6 %collective-permute-start.5 = (bf16[32,4096]{1,0:T(8,128)(2,1)S(1)}, bf16[32,4096]{1,0:T(8,128)(2,1)S(1)}, u32[]{:S(2)}, u32[]{:S(2)}) collective-permute-start(bf16[32,4096]{1,0:T(8,128)(2,1)S(1)} %add_convert_fusion.1), channel_id=1, source_target_pairs={{0,96},{1,97},{2,98},{3,99},{4,100},{5,101},{6,102},{7,103},{8,104... | collective-permute-start | bytes 786440 | tf_op jit(solution)/shard_map/ppermute | solution.py:201
  22.1 6.3 %collective-permute-start.7 = (bf16[32,3840]{1,0:T(8,128)(2,1)S(1)}, bf16[32,3840]{1,0:T(8,128)(2,1)S(1)}, u32[]{:S(2)}, u32[]{:S(2)}) collective-permute-start(bf16[32,3840]{1,0:T(8,128)(2,1)S(1)} %add_convert_fusion.2), channel_id=1, source_target_pairs={{0,32},{1,33},{2,34},{3,35},{4,36},{5,37},{6,38},{7,39},{8,40},{9,... | collective-permute-start | bytes 737288 | tf_op jit(solution)/shard_map/ppermute | solution.py:201
  25.0 8.5 %collective-permute-start.4 = (bf16[16,4352]{1,0:T(8,128)(2,1)S(1)}, bf16[16,4352]{1,0:T(8,128)(2,1)S(1)}, u32[]{:S(2)}, u32[]{:S(2)}) collective-permute-start(bf16[16,4352]{1,0:T(8,128)(2,1)S(1)} %add_convert_fusion.3), channel_id=1, source_target_pairs={{0,96},{1,97},{2,98},{3,99},{4,100},{5,101},{6,102},{7,103},{8,104... | collective-permute-start | bytes 417800 | tf_op jit(solution)/shard_map/ppermute | solution.py:201
  27.9 5.6 %collective-permute-start.6 = (bf16[16,4096]{1,0:T(8,128)(2,1)S(1)}, bf16[16,4096]{1,0:T(8,128)(2,1)S(1)}, u32[]{:S(2)}, u32[]{:S(2)}) collective-permute-start(bf16[16,4096]{1,0:T(8,128)(2,1)S(1)} %add_convert_fusion.4), channel_id=1, source_target_pairs={{0,32},{1,33},{2,34},{3,35},{4,36},{5,37},{6,38},{7,39},{8,40},{9,... | collective-permute-start | bytes 393224 | tf_op jit(solution)/shard_map/ppermute | solution.py:201
  28.5 5.0 %collective-permute-start.8 = (bf16[16,3840]{1,0:T(8,128)(2,1)S(1)}, bf16[16,3840]{1,0:T(8,128)(2,1)S(1)}, u32[]{:S(2)}, u32[]{:S(2)}) collective-permute-start(bf16[16,3840]{1,0:T(8,128)(2,1)S(1)} %add_convert_fusion.5), channel_id=1, source_target_pairs={{0,16},{1,17},{2,18},{3,19},{4,20},{5,21},{6,22},{7,23},{8,24},{9,... | collective-permute-start | bytes 368648 | tf_op jit(solution)/shard_map/ppermute | solution.py:201
  34.4 1.5 %collective-permute-start.9 = (bf16[4,2,96,128]{3,2,1,0:T(8,128)(2,1)S(1)}, bf16[4,2,96,128]{3,2,1,0:T(8,128)(2,1)S(1)}, u32[]{:S(2)}, u32[]{:S(2)}) collective-permute-start(bf16[4,2,96,128]{3,2,1,0:T(8,128)(2,1)S(1)} %get-tuple-element.22), channel_id=1, source_target_pairs={{0,1},{1,0},{2,3},{3,2},{4,5},{5,4},{6,7},{7,6},{8,9},{9,8},{10,11... | collective-permute-start | bytes 589832 | tf_op jit(solution)/shard_map/ppermute | solution.py:201
  36.0 5.7 %collective-permute-start.10 = (bf16[2,96,128]{2,1,0:T(8,128)(2,1)S(1)}, bf16[2,96,128]{2,1,0:T(8,128)(2,1)S(1)}, u32[]{:S(2)}, u32[]{:S(2)}) collective-permute-start(bf16[2,96,128]{2,1,0:T(8,128)(2,1)S(1)} %get-tuple-element.28), channel_id=1, source_target_pairs={{0,4},{1,5},{2,6},{3,7},{4,0},{5,1},{6,2},{7,3},{8,12},{9,13},{10,... | collective-permute-start | bytes 147464 | tf_op jit(solution)/shard_map/ppermute | solution.py:201
  39.3 4.1 %collective-permute-start.11 = (bf16[2,96,128]{2,1,0:T(8,128)(2,1)S(1)}, bf16[2,96,128]{2,1,0:T(8,128)(2,1)S(1)}, u32[]{:S(2)}, u32[]{:S(2)}) collective-permute-start(bf16[2,96,128]{2,1,0:T(8,128)(2,1)S(1)} %get-tuple-element.30), channel_id=1, source_target_pairs={{0,2},{1,3},{2,0},{3,1},{4,6},{5,7},{6,4},{7,5},{8,10},{9,11},{10,... | collective-permute-start | bytes 147464 | tf_op jit(solution)/shard_map/ppermute | solution.py:201
  40.0 5.3 %collective-permute-start.12 = (bf16[2,96,128]{2,1,0:T(8,128)(2,1)S(1)}, bf16[2,96,128]{2,1,0:T(8,128)(2,1)S(1)}, u32[]{:S(2)}, u32[]{:S(2)}) collective-permute-start(bf16[2,96,128]{2,1,0:T(8,128)(2,1)S(1)} %get-tuple-element.29), channel_id=1, source_target_pairs={{0,6},{1,7},{2,4},{3,5},{4,2},{5,3},{6,0},{7,1},{8,14},{9,15},{10,... | collective-permute-start | bytes 147464 | tf_op jit(solution)/shard_map/ppermute | solution.py:201
  45.3 5.5 %collective-permute-start.13 = (bf16[96,128]{1,0:T(8,128)(2,1)S(1)}, bf16[96,128]{1,0:T(8,128)(2,1)S(1)}, u32[]{:S(2)}, u32[]{:S(2)}) collective-permute-start(bf16[96,128]{1,0:T(8,128)(2,1)S(1)} %fusion.5), channel_id=1, source_target_pairs={{0,8},{1,9},{2,10},{3,11},{4,12},{5,13},{6,14},{7,15},{8,0},{9,1},... | collective-permute-start | bytes 73736 | tf_op jit(solution)/shard_map/ppermute | solution.py:201

commit v5 on v4

--- a/solution.py
+++ b/solution.py
@@ -22,6 +22,7 @@
     (66, 30, "QPZ"),
 )
 SUMS = ((0, 1), (1, 1), (2, 1), (0, 2), (1, 2), (2, 2))
+EARLY = 1
 FIRST = 0
 AXES = ("node", "wide")
 VMEM_LIMIT = 32 * 1024 * 1024
@@ -65,15 +66,20 @@
 ORDER = ((1, 1), (1, 0), (0, 1), (0, 0))
 
 
+def block_range(pieces):
+    return pieces[0][0] // 8 * 8, pl.cdiv(pieces[-1][0] + pieces[-1][1], 8) * 8
+
+
 def dequantize_rows(piece, row, scale, codes, out):
     for k in range(piece[1]):
-        at = piece[0] + k
-        values = (codes(k).astype(jnp.float32) + 0.5) * scale[:, at : at + 1]
+        at = piece[0] + k - scale[1]
+        values = (codes(k).astype(jnp.float32) + 0.5) * scale[0][:, at : at + 1]
         out[:, k * LANES : (k + 1) * LANES] = values.astype(jnp.bfloat16)
 
 
 def first_kernel(piece, codes_ref, scales_ref, out_ref, scales, stage, scales_buf, sem, scale_sem):
-    scale_copy = pltpu.make_async_copy(scales_ref, scales_buf, scale_sem)
+    low, high = block_range([piece])
+    scale_copy = pltpu.make_async_copy(scales_ref.at[low:high], scales_buf, scale_sem)
     scale_copy.start()
     copies = []
     for j, tail in enumerate(ORDER):
@@ -86,20 +92,21 @@
         copy.start()
         copies.append((row, copy))
     scale_copy.wait()
-    scales[:, :BLOCKS] = scales_buf[...].T
+    scales[:, : high - low] = scales_buf[...].T
     for j, (row, copy) in enumerate(copies):
         copy.wait()
         rows = slice(j * TILE, (j + 1) * TILE)
         dequantize_rows(
             piece,
             row,
-            scales[pl.ds(row, TILE), :],
+            (scales[pl.ds(row, TILE), :], low),
             lambda k: stage[rows, k * LANES : (k + 1) * LANES],
             out_ref.at[rows],
         )
 
 
 def first_rows(piece, codes, scales_t):
+    low, high = block_range([piece])
     hbm = pl.BlockSpec(memory_space=pltpu.HBM)
     vmem = pl.BlockSpec(memory_space=pltpu.VMEM)
     shape = (4 * TILE, piece[1] * LANES)
@@ -111,7 +118,7 @@
         scratch_shapes=[
             pltpu.VMEM((128, LANES), jnp.float32),
             pltpu.VMEM(shape, jnp.int32),
-            pltpu.VMEM((BLOCKS, 128), jnp.float32),
+            pltpu.VMEM((high - low, 128), jnp.float32),
             pltpu.SemaphoreType.DMA((4,)),
             pltpu.SemaphoreType.DMA,
         ],
@@ -122,14 +129,15 @@
 
 def dequantize_kernel(parts, codes_ref, scales_ref, *rest):
     *outs, scales = rest
-    scales[:, :BLOCKS] = scales_ref[...].T
+    low, high = block_range([piece for piece, _ in parts])
+    scales[:, : high - low] = scales_ref[low:high].T
     for (piece, first), out in zip(parts, outs):
         for j, tail in enumerate(ORDER):
             row = block_row(piece, (first,) + tail)
             dequantize_rows(
                 piece,
                 row,
-                scales[pl.ds(row, TILE), :],
+                (scales[pl.ds(row, TILE), :], low),
                 lambda k: codes_ref[pl.ds(row, TILE), pl.ds((piece[0] + k) * LANES, LANES)],
                 out.at[j * TILE : (j + 1) * TILE],
             )
@@ -148,12 +156,14 @@
     )(codes, scales)
 
 
-def finish_kernel(counts, requant_ref, *refs):
-    parts, (send_ref, keep_ref, rows) = refs[: sum(counts)], refs[sum(counts) :]
+def finish_kernel(pieces, counts, requant_ref, *refs):
+    parts, (send_ref, keep_ref, rows) = refs[: sum(counts)], refs[-3:]
     numerators = requant_ref[...].astype(jnp.float32)
     scale = numerators * (1.0 / 32.0)
     inverse = 32.0 / numerators
-    for n, piece in enumerate(PIECES):
+    start, blocks = pieces[0][0], sum(piece[1] for piece in pieces)
+    stride = rows.shape[0] // TILE
+    for n, piece in enumerate(pieces):
         arrays = parts[sum(counts[:n]) : sum(counts[: n + 1])]
         for k in range(piece[1]):
             cut = pl.ds(k * LANES, LANES)
@@ -162,29 +172,31 @@
             for array in arrays[1:]:
                 partial = partial + array[array.shape[0] - TILE :, cut].astype(jnp.float32)
             coded = jnp.clip(partial * inverse[:, at : at + 1], -8.0, 8.0).astype(jnp.bfloat16)
-            rows[pl.ds(at, TILE, stride=BLOCKS), :] = coded.astype(jnp.float32) * scale[:, at : at + 1]
+            rows[pl.ds(at - start, TILE, stride=stride), :] = coded.astype(jnp.float32) * scale[:, at : at + 1]
     wide = lax.axis_index("wide")
     core = wide & 1
     for slot, y_flip in enumerate(Y_FLIPS):
         for z_slot, z_flip in enumerate((1, 0)):
             for ref, owner in ((send_ref, 1 - core), (keep_ref, core)):
-                row = pl.multiple_of(wide_at(wide, z_flip, y_flip, owner) * BLOCKS, 8)
-                ref[slot, z_slot] = rows[pl.ds(row, BLOCKS), :].astype(ref.dtype)
-
-
-def finish(requant, parts):
+                row = pl.multiple_of(wide_at(wide, z_flip, y_flip, owner) * stride, 8)
+                ref[slot, z_slot] = rows[pl.ds(row, blocks), :].astype(ref.dtype)
+
+
+def finish(requant, pieces, parts):
     vmem = pl.BlockSpec(memory_space=pltpu.VMEM)
-    shape = (4, 2, BLOCKS, LANES)
+    blocks = sum(piece[1] for piece in pieces)
+    shape = (4, 2, blocks, LANES)
     counts = [len(arrays) for arrays in parts]
+    inputs = [requant, *[array for arrays in parts for array in arrays]]
     return pl.pallas_call(
-        lambda *refs: finish_kernel(counts, *refs),
+        lambda *refs: finish_kernel(pieces, counts, *refs),
         out_shape=[jax.ShapeDtypeStruct(shape, jnp.bfloat16), jax.ShapeDtypeStruct(shape, jnp.float32)],
-        in_specs=[vmem] * (1 + sum(counts)),
+        in_specs=[vmem] * len(inputs),
         out_specs=[vmem, vmem],
-        scratch_shapes=[pltpu.VMEM((TILE * BLOCKS, LANES), jnp.float32)],
+        scratch_shapes=[pltpu.VMEM((TILE * pl.cdiv(blocks, 8) * 8, LANES), jnp.float32)],
         compiler_params=pltpu.CompilerParams(vmem_limit_bytes=VMEM_LIMIT),
         name="finish",
-    )(requant, *[array for arrays in parts for array in arrays])
+    )(*inputs)
 
 
 def adamw(gradient, params, first_moment, second_moment, step_count):
@@ -230,8 +242,13 @@
         last = last.astype(jnp.bfloat16)
         parts[n].append(send(last, AXES, pairs(PIECES[n], step)))
     other_core = [(b, b ^ 1) for b in range(16)]
-    away, near = finish(requant_scales.reshape(TILE, BLOCKS), parts)
-    near = total(near, send(away, "wide", other_core))
+    requant = requant_scales.reshape(TILE, BLOCKS)
+    near = []
+    for cut in (slice(0, EARLY), slice(EARLY, None)):
+        away, keep = finish(requant, PIECES[cut], parts[cut])
+        requant, away = lax.optimization_barrier((requant, away))
+        near.append(total(keep, send(away, "wide", [(b, b ^ 1) for b in range(16)])))
+    near = jnp.concatenate(near, axis=2)
     routes = [[(b, wide_at(b, 0, y_flip, b & 1)) for b in range(16)] for y_flip in Y_FLIPS[:3]]
     chip = total(near[3], *[send(near[slot], "wide", route) for slot, route in enumerate(routes)])
     gradient = total(chip[1], send(chip[0], "wide", [(b, b ^ 8) for b in range(16)]))

time: 52.1 us -> 51.7 us (level)
    ppermute x14 -> x15, waiting for transfers between devices: 18.8 us -> 18.3 us  [send(): return lax.ppermute(array.astype(jnp.bfloat16), axes, route)]
    ppermute x14 -> x15, starting transfers between devices: 24.3 us -> 24.4 us  [send(): return lax.ppermute(array.astype(jnp.bfloat16), axes, route)]
  transfers between devices with their start and end apart: 14 -> 15, of which waited for: 9 -> 10; matrix products, arithmetic and copies ran while one was open for 1% -> 1% of each run, Pallas kernels for 5% -> 7%
where the time goes in v5:
time: 51.7 us; the launch traced here: 51.1 us
  starting transfers between devices  24.4 us (47%)
  waiting for transfers between devices  18.3 us (35%)
  Pallas kernels  5.47 us (11%)
  between operations  1.56 us (3%)
  other arithmetic  1.3 us (3%)
    ppermute x15, starting transfers between devices, send(): return lax.ppermute(array.astype(jnp.bfloat16), axes, route)  24.4 us
    ppermute x15, waiting for transfers between devices, send(): return lax.ppermute(array.astype(jnp.bfloat16), axes, route)  18.3 us
    pallas_call x3, Pallas kernels, dequantize(): pl.pallas_call(lambda *refs: dequantize_kernel(parts, *refs), out_shape=[...  2.67 us
    pallas_call x1, Pallas kernels, first_rows(): pl.pallas_call(lambda *refs: first_kernel(piece, *refs), out_shape=jax.Sh...  1.89 us
  transfers between devices with their start and end apart: 15, of which 10 were waited for; matrix products, arithmetic and copies ran while one was open for 1% of the time, Pallas kernels for 7%

profile of v5, /device:TPU:0, one launch (start us, length us, event | category | flops | bytes accessed | tf_op | source)
XLA Modules:
  0.0 51.1 jit_solution(7873321612603763982)
XLA Ops:
  0.6 1.9 %first_rows.1 = bf16[64,4352]{1,0:T(8,128)(2,1)S(1)} custom-call(s32[128,12288]{1,0:T(8,128)} %refs_0_.7, f32[96,128]{1,0:T(8,128)} %bitcast.36), custom_call_target="tpu_custom_call" | custom-call | tf_op jit(solution)/shard_map/first_rows/pallas_call | solution.py:113
  2.5 1.7 %collective-permute-start = (bf16[64,4352]{1,0:T(8,128)(2,1)S(1)}, bf16[64,4352]{1,0:T(8,128)(2,1)S(1)}, u32[]{:S(2)}, u32[]{:S(2)}) collective-permute-start(bf16[64,4352]{1,0:T(8,128)(2,1)S(1)} %first_rows.1), channel_id=1, source_target_pairs={{0,32},{1,33},{2,34},{3,35},{4,36},{5,37},{6,38},{7,39},{8,40},{9,... | collective-permute-start | bytes 1671176 | tf_op jit(solution)/shard_map/ppermute | solution.py:213
  4.2 0.6 %dequantize.5 = bf16[64,4096]{1,0:T(8,128)(2,1)S(1)} custom-call(s32[128,12288]{1,0:T(8,128)S(1)} %copy-done, f32[96,128]{1,0:T(8,128)S(1)} %bitcast.37), custom_call_target="tpu_custom_call" | custom-call | tf_op jit(solution)/shard_map/dequantize/pallas_call | solution.py:148
  4.8 2.0 %collective-permute-start.3 = (bf16[64,4096]{1,0:T(8,128)(2,1)S(1)}, bf16[64,4096]{1,0:T(8,128)(2,1)S(1)}, u32[]{:S(2)}, u32[]{:S(2)}) collective-permute-start(bf16[64,4096]{1,0:T(8,128)(2,1)S(1)} %dequantize.5), channel_id=1, source_target_pairs={{0,16},{1,17},{2,18},{3,19},{4,20},{5,21},{6,22},{7,23},{8,24},{9,... | collective-permute-start | bytes 1572872 | tf_op jit(solution)/shard_map/ppermute | solution.py:213
  6.8 0.6 %dequantize.4 = bf16[64,3840]{1,0:T(8,128)(2,1)S(1)} custom-call(s32[128,12288]{1,0:T(8,128)S(1)} %copy-done, f32[96,128]{1,0:T(8,128)S(1)} %bitcast.38), custom_call_target="tpu_custom_call" | custom-call | tf_op jit(solution)/shard_map/dequantize/pallas_call | solution.py:148
  7.4 0.0 copy-start.2
  7.4 0.0 copy-start.3
  7.4 2.5 %collective-permute-start.2 = (bf16[64,3840]{1,0:T(8,128)(2,1)S(1)}, bf16[64,3840]{1,0:T(8,128)(2,1)S(1)}, u32[]{:S(2)}, u32[]{:S(2)}) collective-permute-start(bf16[64,3840]{1,0:T(8,128)(2,1)S(1)} %dequantize.4), channel_id=1, source_target_pairs={{0,96},{1,97},{2,98},{3,99},{4,100},{5,101},{6,102},{7,103},{8,104... | collective-permute-start | bytes 1474568 | tf_op jit(solution)/shard_map/ppermute | solution.py:213
  9.9 1.5 %dequantize.3 = (bf16[64,4352]{1,0:T(8,128)(2,1)S(1)}, bf16[64,4096]{1,0:T(8,128)(2,1)S(1)}, bf16[64,3840]{1,0:T(8,128)(2,1)S(1)}) custom-call(s32[128,12288]{1,0:T(8,128)S(1)} %copy-done, f32[96,128]{1,0:T(8,128)S(1)} %bitcast.39), custom_call_target="tpu_custom_call" | custom-call | tf_op jit(solution)/shard_map/dequantize/pallas_call | solution.py:148
  11.4 0.0 copy-start.4
  11.4 0.0 copy-start.5
  11.4 5.4 %collective-permute-done.refs_2_ = bf16[64,4352]{1,0:T(8,128)(2,1)S(1)} collective-permute-done((bf16[64,4352]{1,0:T(8,128)(2,1)S(1)}, bf16[64,4352]{1,0:T(8,128)(2,1)S(1)}, u32[]{:S(2)}, u32[]{:S(2)}) %collective-permute-start) | collective-permute-done | bytes 557088 | tf_op jit(solution)/shard_map/ppermute | solution.py:213
  16.8 0.1 add_convert_fusion
  16.9 2.2 %collective-permute-start.1 = (bf16[32,4352]{1,0:T(8,128)(2,1)S(1)}, bf16[32,4352]{1,0:T(8,128)(2,1)S(1)}, u32[]{:S(2)}, u32[]{:S(2)}) collective-permute-start(bf16[32,4352]{1,0:T(8,128)(2,1)S(1)} %add_convert_fusion), channel_id=1, source_target_pairs={{0,16},{1,17},{2,18},{3,19},{4,20},{5,21},{6,22},{7,23},{8,24},{9,... | collective-permute-start | bytes 835592 | tf_op jit(solution)/shard_map/ppermute | solution.py:213
  19.2 0.0 collective-permute-done.3.refs_2_
  19.2 0.1 add_convert_fusion.1
  19.2 2.8 %collective-permute-start.6 = (bf16[32,4096]{1,0:T(8,128)(2,1)S(1)}, bf16[32,4096]{1,0:T(8,128)(2,1)S(1)}, u32[]{:S(2)}, u32[]{:S(2)}) collective-permute-start(bf16[32,4096]{1,0:T(8,128)(2,1)S(1)} %add_convert_fusion.1), channel_id=1, source_target_pairs={{0,96},{1,97},{2,98},{3,99},{4,100},{5,101},{6,102},{7,103},{8,104... | collective-permute-start | bytes 786440 | tf_op jit(solution)/shard_map/ppermute | solution.py:213
  22.1 0.0 collective-permute-done.2.refs_6_
  22.1 0.1 add_convert_fusion.2
  22.1 0.3 collective-permute-start.8
  22.4 2.5 %collective-permute-done.1.refs_3_ = bf16[32,4352]{1,0:T(8,128)(2,1)S(1)} collective-permute-done((bf16[32,4352]{1,0:T(8,128)(2,1)S(1)}, bf16[32,4352]{1,0:T(8,128)(2,1)S(1)}, u32[]{:S(2)}, u32[]{:S(2)}) %collective-permute-start.1) | collective-permute-done | bytes 278560 | tf_op jit(solution)/shard_map/ppermute | solution.py:213
  24.9 0.1 add_convert_fusion.3
  25.0 2.8 %collective-permute-start.4 = (bf16[16,4352]{1,0:T(8,128)(2,1)S(1)}, bf16[16,4352]{1,0:T(8,128)(2,1)S(1)}, u32[]{:S(2)}, u32[]{:S(2)}) collective-permute-start(bf16[16,4352]{1,0:T(8,128)(2,1)S(1)} %add_convert_fusion.3), channel_id=1, source_target_pairs={{0,96},{1,97},{2,98},{3,99},{4,100},{5,101},{6,102},{7,103},{8,104... | collective-permute-start | bytes 417800 | tf_op jit(solution)/shard_map/ppermute | solution.py:213
  27.8 0.0 collective-permute-done.6.refs_3_
  27.8 0.1 add_convert_fusion.4
  27.9 0.3 collective-permute-start.7
  28.2 0.3 collective-permute-done.8.refs_7_
  28.5 1.5 %collective-permute-start.9 = (bf16[16,3840]{1,0:T(8,128)(2,1)S(1)}, bf16[16,3840]{1,0:T(8,128)(2,1)S(1)}, u32[]{:S(2)}, u32[]{:S(2)}) collective-permute-start(bf16[16,3840]{1,0:T(8,128)(2,1)S(1)} %add_convert_fusion.5), channel_id=1, source_target_pairs={{0,16},{1,17},{2,18},{3,19},{4,20},{5,21},{6,22},{7,23},{8,24},{9,... | collective-permute-start | bytes 368648 | tf_op jit(solution)/shard_map/ppermute | solution.py:213
  30.1 1.3 %collective-permute-done.4.refs_4_ = bf16[16,4352]{1,0:T(8,128)(2,1)S(1)} collective-permute-done((bf16[16,4352]{1,0:T(8,128)(2,1)S(1)}, bf16[16,4352]{1,0:T(8,128)(2,1)S(1)}, u32[]{:S(2)}, u32[]{:S(2)}) %collective-permute-start.4) | collective-permute-done | bytes 139296 | tf_op jit(solution)/shard_map/ppermute | solution.py:213
  31.3 0.3 finish.2
  31.6 0.1 collective-permute-start.5
  31.8 0.1 broadcast_multiply_fusion.2
  31.8 1.7 %collective-permute-done.9.refs_8_ = bf16[16,3840]{1,0:T(8,128)(2,1)S(1)} collective-permute-done((bf16[16,3840]{1,0:T(8,128)(2,1)S(1)}, bf16[16,3840]{1,0:T(8,128)(2,1)S(1)}, u32[]{:S(2)}, u32[]{:S(2)}) %collective-permute-start.9) | collective-permute-done | bytes 122912 | tf_op jit(solution)/shard_map/ppermute | solution.py:213
  33.5 0.6 %finish.3 = (bf16[4,2,62,128]{3,2,1,0:T(8,128)(2,1)S(1)}, f32[4,2,62,128]{3,2,1,0:T(8,128)S(1)}) custom-call(s32[16,96]{1,0:T(8,128)S(1)} %bitcast.41, bf16[64,4096]{1,0:T(8,128)(2,1)S(1)} %get-tuple-element.20.refs_1_, bf16[64,4096]{1,0:T(8,128)(2,1)S(1)} %collective-permute-done.3.refs_2_, bf16[32,4096]{1,0:T(8,128)(2,1)S(1)} %collective-permute-done.6.refs_3_, ...), custom_call_target="tpu_custom_call" | custom-call | tf_op jit(solution)/shard_map/finish/pallas_call | solution.py:191
  34.1 0.1 collective-permute-start.10
  34.2 0.0 collective-permute-done.5
  34.2 1.3 %collective-permute-done.10 = bf16[4,2,62,128]{3,2,1,0:T(8,128)(2,1)S(1)} collective-permute-done((bf16[4,2,62,128]{3,2,1,0:T(8,128)(2,1)S(1)}, bf16[4,2,62,128]{3,2,1,0:T(8,128)(2,1)S(1)}, u32[]{:S(2)}, u32[]{:S(2)}) %collective-permute-start.10) | collective-permute-done | bytes 127008 | tf_op jit(solution)/shard_map/ppermute | solution.py:213
  35.6 3.3 %collective-permute-start.11 = (bf16[2,96,128]{2,1,0:T(8,128)(2,1)S(1)}, bf16[2,96,128]{2,1,0:T(8,128)(2,1)S(1)}, u32[]{:S(2)}, u32[]{:S(2)}) collective-permute-start(bf16[2,96,128]{2,1,0:T(8,128)(2,1)S(1)} %get-tuple-element.36), channel_id=1, source_target_pairs={{0,4},{1,5},{2,6},{3,7},{4,0},{5,1},{6,2},{7,3},{8,12},{9,13},{10,... | collective-permute-start | bytes 147464 | tf_op jit(solution)/shard_map/ppermute | solution.py:213
  38.9 0.7 %collective-permute-start.12 = (bf16[2,96,128]{2,1,0:T(8,128)(2,1)S(1)}, bf16[2,96,128]{2,1,0:T(8,128)(2,1)S(1)}, u32[]{:S(2)}, u32[]{:S(2)}) collective-permute-start(bf16[2,96,128]{2,1,0:T(8,128)(2,1)S(1)} %get-tuple-element.38), channel_id=1, source_target_pairs={{0,2},{1,3},{2,0},{3,1},{4,6},{5,7},{6,4},{7,5},{8,10},{9,11},{10,... | collective-permute-start | bytes 147464 | tf_op jit(solution)/shard_map/ppermute | solution.py:213
  39.6 0.4 collective-permute-start.13
  40.0 0.1 broadcast_multiply_fusion.1
  40.0 1.3 %collective-permute-done.11 = bf16[2,96,128]{2,1,0:T(8,128)(2,1)S(1)} collective-permute-done((bf16[2,96,128]{2,1,0:T(8,128)(2,1)S(1)}, bf16[2,96,128]{2,1,0:T(8,128)(2,1)S(1)}, u32[]{:S(2)}, u32[]{:S(2)}) %collective-permute-start.11) | collective-permute-done | bytes 49184 | tf_op jit(solution)/shard_map/ppermute | solution.py:213
  41.3 1.7 %collective-permute-done.12 = bf16[2,96,128]{2,1,0:T(8,128)(2,1)S(1)} collective-permute-done((bf16[2,96,128]{2,1,0:T(8,128)(2,1)S(1)}, bf16[2,96,128]{2,1,0:T(8,128)(2,1)S(1)}, u32[]{:S(2)}, u32[]{:S(2)}) %collective-permute-start.12) | collective-permute-done | bytes 49184 | tf_op jit(solution)/shard_map/ppermute | solution.py:213
  43.0 1.9 %collective-permute-done.13 = bf16[2,96,128]{2,1,0:T(8,128)(2,1)S(1)} collective-permute-done((bf16[2,96,128]{2,1,0:T(8,128)(2,1)S(1)}, bf16[2,96,128]{2,1,0:T(8,128)(2,1)S(1)}, u32[]{:S(2)}, u32[]{:S(2)}) %collective-permute-start.13) | collective-permute-done | bytes 49184 | tf_op jit(solution)/shard_map/ppermute | solution.py:213
  44.9 3.7 %collective-permute-start.14 = (bf16[96,128]{1,0:T(8,128)(2,1)S(1)}, bf16[96,128]{1,0:T(8,128)(2,1)S(1)}, u32[]{:S(2)}, u32[]{:S(2)}) collective-permute-start(bf16[96,128]{1,0:T(8,128)(2,1)S(1)} %fusion.8), channel_id=1, source_target_pairs={{0,8},{1,9},{2,10},{3,11},{4,12},{5,13},{6,14},{7,15},{8,0},{9,1},... | collective-permute-start | bytes 73736 | tf_op jit(solution)/shard_map/ppermute | solution.py:213
  48.6 0.1 broadcast_multiply_fusion
  49.4 1.0 %collective-permute-done.14 = bf16[96,128]{1,0:T(8,128)(2,1)S(1)} collective-permute-done((bf16[96,128]{1,0:T(8,128)(2,1)S(1)}, bf16[96,128]{1,0:T(8,128)(2,1)S(1)}, u32[]{:S(2)}, u32[]{:S(2)}) %collective-permute-start.14) | collective-permute-done | bytes 24608 | tf_op jit(solution)/shard_map/ppermute | solution.py:213
  50.4 0.7 %divide_add_fusion = (f32[96,128]{1,0:T(8,128)}, f32[96,128]{1,0:T(8,128)}, f32[96,128]{1,0:T(8,128)}) fusion(f32[96,128]{1,0:T(8,128)S(1)} %bitcast.44, f32[]{:T(128)} %bitcast.11, f32[]{:T(128)} %bitcast.9, f32[96,128]{1,0:T(8,128)S(1)} %bitcast.43, bf16[96,128]{1,0:T(8,128)(2,1)S(1)} %collective-permute-done.14, f32[2,96,128]{2,1,0:T(8,128)S(1)} %fusion.5, ...), kind=kLoop, calls=%fused_computation.25 | loop fusion | flops 147456 | bytes 368648 | tf_op jit(solution)/shard_map/add | solution.py:208
  (16 shorter events, 0.2 us)
Async XLA Ops:
  0.6 3.6 %copy-start.1 = (f32[128,96]{0,1:T(8,128)S(1)}, f32[128,96]{0,1:T(8,128)}, u32[]{:S(2)}) copy-start(f32[128,96]{0,1:T(8,128)} %param.8) | copy-start | bytes 147460
  0.6 3.6 %copy-start = (s32[128,12288]{1,0:T(8,128)S(1)}, s32[128,12288]{1,0:T(8,128)}, u32[]{:S(2)}) copy-start(s32[128,12288]{1,0:T(8,128)} %refs_0_.7) | copy-start | bytes 18874372
  2.5 14.3 %collective-permute-start = (bf16[64,4352]{1,0:T(8,128)(2,1)S(1)}, bf16[64,4352]{1,0:T(8,128)(2,1)S(1)}, u32[]{:S(2)}, u32[]{:S(2)}) collective-permute-start(bf16[64,4352]{1,0:T(8,128)(2,1)S(1)} %first_rows.1), channel_id=1, source_target_pairs={{0,32},{1,33},{2,34},{3,35},{4,36},{5,37},{6,38},{7,39},{8,40},{9,... | collective-permute-start | bytes 1671176 | tf_op jit(solution)/shard_map/ppermute | solution.py:213
  4.8 14.3 %collective-permute-start.3 = (bf16[64,4096]{1,0:T(8,128)(2,1)S(1)}, bf16[64,4096]{1,0:T(8,128)(2,1)S(1)}, u32[]{:S(2)}, u32[]{:S(2)}) collective-permute-start(bf16[64,4096]{1,0:T(8,128)(2,1)S(1)} %dequantize.5), channel_id=1, source_target_pairs={{0,16},{1,17},{2,18},{3,19},{4,20},{5,21},{6,22},{7,23},{8,24},{9,... | collective-permute-start | bytes 1572872 | tf_op jit(solution)/shard_map/ppermute | solution.py:213
  7.4 23.9 %copy-start.2 = (s32[1,1,16,96]{3,2,1,0:T(8,128)S(1)}, s32[1,1,16,96]{3,2,1,0:T(8,128)}, u32[]{:S(2)}) copy-start(s32[1,1,16,96]{3,2,1,0:T(8,128)} %param.9) | copy-start | bytes 18436
  7.4 24.3 %copy-start.3 = (f32[1,12288]{1,0:T(1,128)S(1)}, f32[1,12288]{1,0:T(1,128)}, u32[]{:S(2)}) copy-start(f32[1,12288]{1,0:T(1,128)} %param.11) | copy-start | bytes 147460
  7.4 14.6 %collective-permute-start.2 = (bf16[64,3840]{1,0:T(8,128)(2,1)S(1)}, bf16[64,3840]{1,0:T(8,128)(2,1)S(1)}, u32[]{:S(2)}, u32[]{:S(2)}) collective-permute-start(bf16[64,3840]{1,0:T(8,128)(2,1)S(1)} %dequantize.4), channel_id=1, source_target_pairs={{0,96},{1,97},{2,98},{3,99},{4,100},{5,101},{6,102},{7,103},{8,104... | collective-permute-start | bytes 1474568 | tf_op jit(solution)/shard_map/ppermute | solution.py:213
  11.4 28.6 %copy-start.4 = (f32[1,12288]{1,0:T(1,128)S(1)}, f32[1,12288]{1,0:T(1,128)}, u32[]{:S(2)}) copy-start(f32[1,12288]{1,0:T(1,128)} %param.12) | copy-start | bytes 147460
  11.4 37.2 %copy-start.5 = (f32[1,12288]{1,0:T(1,128)S(1)}, f32[1,12288]{1,0:T(1,128)}, u32[]{:S(2)}) copy-start(f32[1,12288]{1,0:T(1,128)} %param.10) | copy-start | bytes 147460
  16.9 8.0 %collective-permute-start.1 = (bf16[32,4352]{1,0:T(8,128)(2,1)S(1)}, bf16[32,4352]{1,0:T(8,128)(2,1)S(1)}, u32[]{:S(2)}, u32[]{:S(2)}) collective-permute-start(bf16[32,4352]{1,0:T(8,128)(2,1)S(1)} %add_convert_fusion), channel_id=1, source_target_pairs={{0,16},{1,17},{2,18},{3,19},{4,20},{5,21},{6,22},{7,23},{8,24},{9,... | collective-permute-start | bytes 835592 | tf_op jit(solution)/shard_map/ppermute | solution.py:213
  19.2 8.6 %collective-permute-start.6 = (bf16[32,4096]{1,0:T(8,128)(2,1)S(1)}, bf16[32,4096]{1,0:T(8,128)(2,1)S(1)}, u32[]{:S(2)}, u32[]{:S(2)}) collective-permute-start(bf16[32,4096]{1,0:T(8,128)(2,1)S(1)} %add_convert_fusion.1), channel_id=1, source_target_pairs={{0,96},{1,97},{2,98},{3,99},{4,100},{5,101},{6,102},{7,103},{8,104... | collective-permute-start | bytes 786440 | tf_op jit(solution)/shard_map/ppermute | solution.py:213
  22.1 6.3 %collective-permute-start.8 = (bf16[32,3840]{1,0:T(8,128)(2,1)S(1)}, bf16[32,3840]{1,0:T(8,128)(2,1)S(1)}, u32[]{:S(2)}, u32[]{:S(2)}) collective-permute-start(bf16[32,3840]{1,0:T(8,128)(2,1)S(1)} %add_convert_fusion.2), channel_id=1, source_target_pairs={{0,32},{1,33},{2,34},{3,35},{4,36},{5,37},{6,38},{7,39},{8,40},{9,... | collective-permute-start | bytes 737288 | tf_op jit(solution)/shard_map/ppermute | solution.py:213
  25.0 6.3 %collective-permute-start.4 = (bf16[16,4352]{1,0:T(8,128)(2,1)S(1)}, bf16[16,4352]{1,0:T(8,128)(2,1)S(1)}, u32[]{:S(2)}, u32[]{:S(2)}) collective-permute-start(bf16[16,4352]{1,0:T(8,128)(2,1)S(1)} %add_convert_fusion.3), channel_id=1, source_target_pairs={{0,96},{1,97},{2,98},{3,99},{4,100},{5,101},{6,102},{7,103},{8,104... | collective-permute-start | bytes 417800 | tf_op jit(solution)/shard_map/ppermute | solution.py:213
  27.9 5.6 %collective-permute-start.7 = (bf16[16,4096]{1,0:T(8,128)(2,1)S(1)}, bf16[16,4096]{1,0:T(8,128)(2,1)S(1)}, u32[]{:S(2)}, u32[]{:S(2)}) collective-permute-start(bf16[16,4096]{1,0:T(8,128)(2,1)S(1)} %add_convert_fusion.4), channel_id=1, source_target_pairs={{0,32},{1,33},{2,34},{3,35},{4,36},{5,37},{6,38},{7,39},{8,40},{9,... | collective-permute-start | bytes 393224 | tf_op jit(solution)/shard_map/ppermute | solution.py:213
  28.5 5.0 %collective-permute-start.9 = (bf16[16,3840]{1,0:T(8,128)(2,1)S(1)}, bf16[16,3840]{1,0:T(8,128)(2,1)S(1)}, u32[]{:S(2)}, u32[]{:S(2)}) collective-permute-start(bf16[16,3840]{1,0:T(8,128)(2,1)S(1)} %add_convert_fusion.5), channel_id=1, source_target_pairs={{0,16},{1,17},{2,18},{3,19},{4,20},{5,21},{6,22},{7,23},{8,24},{9,... | collective-permute-start | bytes 368648 | tf_op jit(solution)/shard_map/ppermute | solution.py:213
  31.6 2.6 %collective-permute-start.5 = (bf16[4,2,34,128]{3,2,1,0:T(8,128)(2,1)S(1)}, bf16[4,2,34,128]{3,2,1,0:T(8,128)(2,1)S(1)}, u32[]{:S(2)}, u32[]{:S(2)}) collective-permute-start(bf16[4,2,34,128]{3,2,1,0:T(8,128)(2,1)S(1)} %get-tuple-element.26), channel_id=1, source_target_pairs={{0,1},{1,0},{2,3},{3,2},{4,5},{5,4},{6,7},{7,6},{8,9},{9,8},{10,11... | collective-permute-start | bytes 208904 | tf_op jit(solution)/shard_map/ppermute | solution.py:213
  34.1 1.4 %collective-permute-start.10 = (bf16[4,2,62,128]{3,2,1,0:T(8,128)(2,1)S(1)}, bf16[4,2,62,128]{3,2,1,0:T(8,128)(2,1)S(1)}, u32[]{:S(2)}, u32[]{:S(2)}) collective-permute-start(bf16[4,2,62,128]{3,2,1,0:T(8,128)(2,1)S(1)} %get-tuple-element.32), channel_id=1, source_target_pairs={{0,1},{1,0},{2,3},{3,2},{4,5},{5,4},{6,7},{7,6},{8,9},{9,8},{10,11... | collective-permute-start | bytes 380936 | tf_op jit(solution)/shard_map/ppermute | solution.py:213
  35.6 5.7 %collective-permute-start.11 = (bf16[2,96,128]{2,1,0:T(8,128)(2,1)S(1)}, bf16[2,96,128]{2,1,0:T(8,128)(2,1)S(1)}, u32[]{:S(2)}, u32[]{:S(2)}) collective-permute-start(bf16[2,96,128]{2,1,0:T(8,128)(2,1)S(1)} %get-tuple-element.36), channel_id=1, source_target_pairs={{0,4},{1,5},{2,6},{3,7},{4,0},{5,1},{6,2},{7,3},{8,12},{9,13},{10,... | collective-permute-start | bytes 147464 | tf_op jit(solution)/shard_map/ppermute | solution.py:213
  38.9 4.1 %collective-permute-start.12 = (bf16[2,96,128]{2,1,0:T(8,128)(2,1)S(1)}, bf16[2,96,128]{2,1,0:T(8,128)(2,1)S(1)}, u32[]{:S(2)}, u32[]{:S(2)}) collective-permute-start(bf16[2,96,128]{2,1,0:T(8,128)(2,1)S(1)} %get-tuple-element.38), channel_id=1, source_target_pairs={{0,2},{1,3},{2,0},{3,1},{4,6},{5,7},{6,4},{7,5},{8,10},{9,11},{10,... | collective-permute-start | bytes 147464 | tf_op jit(solution)/shard_map/ppermute | solution.py:213
  39.6 5.3 %collective-permute-start.13 = (bf16[2,96,128]{2,1,0:T(8,128)(2,1)S(1)}, bf16[2,96,128]{2,1,0:T(8,128)(2,1)S(1)}, u32[]{:S(2)}, u32[]{:S(2)}) collective-permute-start(bf16[2,96,128]{2,1,0:T(8,128)(2,1)S(1)} %get-tuple-element.37), channel_id=1, source_target_pairs={{0,6},{1,7},{2,4},{3,5},{4,2},{5,3},{6,0},{7,1},{8,14},{9,15},{10,... | collective-permute-start | bytes 147464 | tf_op jit(solution)/shard_map/ppermute | solution.py:213
  44.9 5.5 %collective-permute-start.14 = (bf16[96,128]{1,0:T(8,128)(2,1)S(1)}, bf16[96,128]{1,0:T(8,128)(2,1)S(1)}, u32[]{:S(2)}, u32[]{:S(2)}) collective-permute-start(bf16[96,128]{1,0:T(8,128)(2,1)S(1)} %fusion.8), channel_id=1, source_target_pairs={{0,8},{1,9},{2,10},{3,11},{4,12},{5,13},{6,14},{7,15},{8,0},{9,1},... | collective-permute-start | bytes 73736 | tf_op jit(solution)/shard_map/ppermute | solution.py:213

commit v6 on v5

--- a/solution.py
+++ b/solution.py
@@ -162,7 +162,7 @@
     scale = numerators * (1.0 / 32.0)
     inverse = 32.0 / numerators
     start, blocks = pieces[0][0], sum(piece[1] for piece in pieces)
-    stride = rows.shape[0] // TILE
+    stride = rows.shape[0] // (TILE + 1)
     for n, piece in enumerate(pieces):
         arrays = parts[sum(counts[:n]) : sum(counts[: n + 1])]
         for k in range(piece[1]):
@@ -193,7 +193,7 @@
         out_shape=[jax.ShapeDtypeStruct(shape, jnp.bfloat16), jax.ShapeDtypeStruct(shape, jnp.float32)],
         in_specs=[vmem] * len(inputs),
         out_specs=[vmem, vmem],
-        scratch_shapes=[pltpu.VMEM((TILE * pl.cdiv(blocks, 8) * 8, LANES), jnp.float32)],
+        scratch_shapes=[pltpu.VMEM(((TILE + 1) * pl.cdiv(blocks, 8) * 8, LANES), jnp.float32)],
         compiler_params=pltpu.CompilerParams(vmem_limit_bytes=VMEM_LIMIT),
         name="finish",
     )(*inputs)

time: 51.7 us -> 51.7 us (level)
  no operation moved by 1% of the time
where the time goes in v6:
time: 51.7 us; the launch traced here: 51.1 us
  starting transfers between devices  24.4 us (47%)
  waiting for transfers between devices  18.3 us (35%)
  Pallas kernels  5.47 us (11%)
  between operations  1.56 us (3%)
  other arithmetic  1.3 us (3%)
    ppermute x15, starting transfers between devices, send(): return lax.ppermute(array.astype(jnp.bfloat16), axes, route)  24.4 us
    ppermute x15, waiting for transfers between devices, send(): return lax.ppermute(array.astype(jnp.bfloat16), axes, route)  18.3 us
    pallas_call x3, Pallas kernels, dequantize(): pl.pallas_call(lambda *refs: dequantize_kernel(parts, *refs), out_shape=[...  2.67 us
    pallas_call x1, Pallas kernels, first_rows(): pl.pallas_call(lambda *refs: first_kernel(piece, *refs), out_shape=jax.Sh...  1.89 us
  transfers between devices with their start and end apart: 15, of which 10 were waited for; matrix products, arithmetic and copies ran while one was open for 1% of the time, Pallas kernels for 7%

profile of v6, /device:TPU:0, one launch (start us, length us, event | category | flops | bytes accessed | tf_op | source)
XLA Modules:
  0.0 51.1 jit_solution(7873321612603763982)
XLA Ops:
  0.6 1.9 %first_rows.1 = bf16[64,4352]{1,0:T(8,128)(2,1)S(1)} custom-call(s32[128,12288]{1,0:T(8,128)} %refs_0_.7, f32[96,128]{1,0:T(8,128)} %bitcast.36), custom_call_target="tpu_custom_call" | custom-call | tf_op jit(solution)/shard_map/first_rows/pallas_call | solution.py:113
  2.5 1.7 %collective-permute-start = (bf16[64,4352]{1,0:T(8,128)(2,1)S(1)}, bf16[64,4352]{1,0:T(8,128)(2,1)S(1)}, u32[]{:S(2)}, u32[]{:S(2)}) collective-permute-start(bf16[64,4352]{1,0:T(8,128)(2,1)S(1)} %first_rows.1), channel_id=1, source_target_pairs={{0,32},{1,33},{2,34},{3,35},{4,36},{5,37},{6,38},{7,39},{8,40},{9,... | collective-permute-start | bytes 1671176 | tf_op jit(solution)/shard_map/ppermute | solution.py:213
  4.2 0.6 %dequantize.5 = bf16[64,4096]{1,0:T(8,128)(2,1)S(1)} custom-call(s32[128,12288]{1,0:T(8,128)S(1)} %copy-done, f32[96,128]{1,0:T(8,128)S(1)} %bitcast.37), custom_call_target="tpu_custom_call" | custom-call | tf_op jit(solution)/shard_map/dequantize/pallas_call | solution.py:148
  4.8 2.0 %collective-permute-start.3 = (bf16[64,4096]{1,0:T(8,128)(2,1)S(1)}, bf16[64,4096]{1,0:T(8,128)(2,1)S(1)}, u32[]{:S(2)}, u32[]{:S(2)}) collective-permute-start(bf16[64,4096]{1,0:T(8,128)(2,1)S(1)} %dequantize.5), channel_id=1, source_target_pairs={{0,16},{1,17},{2,18},{3,19},{4,20},{5,21},{6,22},{7,23},{8,24},{9,... | collective-permute-start | bytes 1572872 | tf_op jit(solution)/shard_map/ppermute | solution.py:213
  6.8 0.6 %dequantize.4 = bf16[64,3840]{1,0:T(8,128)(2,1)S(1)} custom-call(s32[128,12288]{1,0:T(8,128)S(1)} %copy-done, f32[96,128]{1,0:T(8,128)S(1)} %bitcast.38), custom_call_target="tpu_custom_call" | custom-call | tf_op jit(solution)/shard_map/dequantize/pallas_call | solution.py:148
  7.4 0.0 copy-start.2
  7.4 0.0 copy-start.3
  7.4 2.5 %collective-permute-start.2 = (bf16[64,3840]{1,0:T(8,128)(2,1)S(1)}, bf16[64,3840]{1,0:T(8,128)(2,1)S(1)}, u32[]{:S(2)}, u32[]{:S(2)}) collective-permute-start(bf16[64,3840]{1,0:T(8,128)(2,1)S(1)} %dequantize.4), channel_id=1, source_target_pairs={{0,96},{1,97},{2,98},{3,99},{4,100},{5,101},{6,102},{7,103},{8,104... | collective-permute-start | bytes 1474568 | tf_op jit(solution)/shard_map/ppermute | solution.py:213
  9.9 1.5 %dequantize.3 = (bf16[64,4352]{1,0:T(8,128)(2,1)S(1)}, bf16[64,4096]{1,0:T(8,128)(2,1)S(1)}, bf16[64,3840]{1,0:T(8,128)(2,1)S(1)}) custom-call(s32[128,12288]{1,0:T(8,128)S(1)} %copy-done, f32[96,128]{1,0:T(8,128)S(1)} %bitcast.39), custom_call_target="tpu_custom_call" | custom-call | tf_op jit(solution)/shard_map/dequantize/pallas_call | solution.py:148
  11.4 0.0 copy-start.4
  11.4 0.0 copy-start.5
  11.4 5.4 %collective-permute-done.refs_2_ = bf16[64,4352]{1,0:T(8,128)(2,1)S(1)} collective-permute-done((bf16[64,4352]{1,0:T(8,128)(2,1)S(1)}, bf16[64,4352]{1,0:T(8,128)(2,1)S(1)}, u32[]{:S(2)}, u32[]{:S(2)}) %collective-permute-start) | collective-permute-done | bytes 557088 | tf_op jit(solution)/shard_map/ppermute | solution.py:213
  16.8 0.1 add_convert_fusion
  16.9 2.2 %collective-permute-start.1 = (bf16[32,4352]{1,0:T(8,128)(2,1)S(1)}, bf16[32,4352]{1,0:T(8,128)(2,1)S(1)}, u32[]{:S(2)}, u32[]{:S(2)}) collective-permute-start(bf16[32,4352]{1,0:T(8,128)(2,1)S(1)} %add_convert_fusion), channel_id=1, source_target_pairs={{0,16},{1,17},{2,18},{3,19},{4,20},{5,21},{6,22},{7,23},{8,24},{9,... | collective-permute-start | bytes 835592 | tf_op jit(solution)/shard_map/ppermute | solution.py:213
  19.2 0.0 collective-permute-done.3.refs_2_
  19.2 0.1 add_convert_fusion.1
  19.2 2.8 %collective-permute-start.6 = (bf16[32,4096]{1,0:T(8,128)(2,1)S(1)}, bf16[32,4096]{1,0:T(8,128)(2,1)S(1)}, u32[]{:S(2)}, u32[]{:S(2)}) collective-permute-start(bf16[32,4096]{1,0:T(8,128)(2,1)S(1)} %add_convert_fusion.1), channel_id=1, source_target_pairs={{0,96},{1,97},{2,98},{3,99},{4,100},{5,101},{6,102},{7,103},{8,104... | collective-permute-start | bytes 786440 | tf_op jit(solution)/shard_map/ppermute | solution.py:213
  22.1 0.0 collective-permute-done.2.refs_6_
  22.1 0.1 add_convert_fusion.2
  22.1 0.3 collective-permute-start.8
  22.4 2.5 %collective-permute-done.1.refs_3_ = bf16[32,4352]{1,0:T(8,128)(2,1)S(1)} collective-permute-done((bf16[32,4352]{1,0:T(8,128)(2,1)S(1)}, bf16[32,4352]{1,0:T(8,128)(2,1)S(1)}, u32[]{:S(2)}, u32[]{:S(2)}) %collective-permute-start.1) | collective-permute-done | bytes 278560 | tf_op jit(solution)/shard_map/ppermute | solution.py:213
  24.9 0.1 add_convert_fusion.3
  25.0 2.8 %collective-permute-start.4 = (bf16[16,4352]{1,0:T(8,128)(2,1)S(1)}, bf16[16,4352]{1,0:T(8,128)(2,1)S(1)}, u32[]{:S(2)}, u32[]{:S(2)}) collective-permute-start(bf16[16,4352]{1,0:T(8,128)(2,1)S(1)} %add_convert_fusion.3), channel_id=1, source_target_pairs={{0,96},{1,97},{2,98},{3,99},{4,100},{5,101},{6,102},{7,103},{8,104... | collective-permute-start | bytes 417800 | tf_op jit(solution)/shard_map/ppermute | solution.py:213
  27.8 0.0 collective-permute-done.6.refs_3_
  27.8 0.1 add_convert_fusion.4
  27.9 0.3 collective-permute-start.7
  28.2 0.3 collective-permute-done.8.refs_7_
  28.5 1.5 %collective-permute-start.9 = (bf16[16,3840]{1,0:T(8,128)(2,1)S(1)}, bf16[16,3840]{1,0:T(8,128)(2,1)S(1)}, u32[]{:S(2)}, u32[]{:S(2)}) collective-permute-start(bf16[16,3840]{1,0:T(8,128)(2,1)S(1)} %add_convert_fusion.5), channel_id=1, source_target_pairs={{0,16},{1,17},{2,18},{3,19},{4,20},{5,21},{6,22},{7,23},{8,24},{9,... | collective-permute-start | bytes 368648 | tf_op jit(solution)/shard_map/ppermute | solution.py:213
  30.1 1.3 %collective-permute-done.4.refs_4_ = bf16[16,4352]{1,0:T(8,128)(2,1)S(1)} collective-permute-done((bf16[16,4352]{1,0:T(8,128)(2,1)S(1)}, bf16[16,4352]{1,0:T(8,128)(2,1)S(1)}, u32[]{:S(2)}, u32[]{:S(2)}) %collective-permute-start.4) | collective-permute-done | bytes 139296 | tf_op jit(solution)/shard_map/ppermute | solution.py:213
  31.3 0.3 finish.2
  31.6 0.1 collective-permute-start.5
  31.8 0.1 broadcast_multiply_fusion.2
  31.8 1.7 %collective-permute-done.9.refs_8_ = bf16[16,3840]{1,0:T(8,128)(2,1)S(1)} collective-permute-done((bf16[16,3840]{1,0:T(8,128)(2,1)S(1)}, bf16[16,3840]{1,0:T(8,128)(2,1)S(1)}, u32[]{:S(2)}, u32[]{:S(2)}) %collective-permute-start.9) | collective-permute-done | bytes 122912 | tf_op jit(solution)/shard_map/ppermute | solution.py:213
  33.5 0.6 %finish.3 = (bf16[4,2,62,128]{3,2,1,0:T(8,128)(2,1)S(1)}, f32[4,2,62,128]{3,2,1,0:T(8,128)S(1)}) custom-call(s32[16,96]{1,0:T(8,128)S(1)} %bitcast.41, bf16[64,4096]{1,0:T(8,128)(2,1)S(1)} %get-tuple-element.20.refs_1_, bf16[64,4096]{1,0:T(8,128)(2,1)S(1)} %collective-permute-done.3.refs_2_, bf16[32,4096]{1,0:T(8,128)(2,1)S(1)} %collective-permute-done.6.refs_3_, ...), custom_call_target="tpu_custom_call" | custom-call | tf_op jit(solution)/shard_map/finish/pallas_call | solution.py:191
  34.1 0.1 collective-permute-start.10
  34.2 0.0 collective-permute-done.5
  34.2 1.3 %collective-permute-done.10 = bf16[4,2,62,128]{3,2,1,0:T(8,128)(2,1)S(1)} collective-permute-done((bf16[4,2,62,128]{3,2,1,0:T(8,128)(2,1)S(1)}, bf16[4,2,62,128]{3,2,1,0:T(8,128)(2,1)S(1)}, u32[]{:S(2)}, u32[]{:S(2)}) %collective-permute-start.10) | collective-permute-done | bytes 127008 | tf_op jit(solution)/shard_map/ppermute | solution.py:213
  35.6 3.3 %collective-permute-start.11 = (bf16[2,96,128]{2,1,0:T(8,128)(2,1)S(1)}, bf16[2,96,128]{2,1,0:T(8,128)(2,1)S(1)}, u32[]{:S(2)}, u32[]{:S(2)}) collective-permute-start(bf16[2,96,128]{2,1,0:T(8,128)(2,1)S(1)} %get-tuple-element.36), channel_id=1, source_target_pairs={{0,4},{1,5},{2,6},{3,7},{4,0},{5,1},{6,2},{7,3},{8,12},{9,13},{10,... | collective-permute-start | bytes 147464 | tf_op jit(solution)/shard_map/ppermute | solution.py:213
  38.9 0.7 %collective-permute-start.12 = (bf16[2,96,128]{2,1,0:T(8,128)(2,1)S(1)}, bf16[2,96,128]{2,1,0:T(8,128)(2,1)S(1)}, u32[]{:S(2)}, u32[]{:S(2)}) collective-permute-start(bf16[2,96,128]{2,1,0:T(8,128)(2,1)S(1)} %get-tuple-element.38), channel_id=1, source_target_pairs={{0,2},{1,3},{2,0},{3,1},{4,6},{5,7},{6,4},{7,5},{8,10},{9,11},{10,... | collective-permute-start | bytes 147464 | tf_op jit(solution)/shard_map/ppermute | solution.py:213
  39.6 0.4 collective-permute-start.13
  40.0 0.1 broadcast_multiply_fusion.1
  40.0 1.3 %collective-permute-done.11 = bf16[2,96,128]{2,1,0:T(8,128)(2,1)S(1)} collective-permute-done((bf16[2,96,128]{2,1,0:T(8,128)(2,1)S(1)}, bf16[2,96,128]{2,1,0:T(8,128)(2,1)S(1)}, u32[]{:S(2)}, u32[]{:S(2)}) %collective-permute-start.11) | collective-permute-done | bytes 49184 | tf_op jit(solution)/shard_map/ppermute | solution.py:213
  41.3 1.7 %collective-permute-done.12 = bf16[2,96,128]{2,1,0:T(8,128)(2,1)S(1)} collective-permute-done((bf16[2,96,128]{2,1,0:T(8,128)(2,1)S(1)}, bf16[2,96,128]{2,1,0:T(8,128)(2,1)S(1)}, u32[]{:S(2)}, u32[]{:S(2)}) %collective-permute-start.12) | collective-permute-done | bytes 49184 | tf_op jit(solution)/shard_map/ppermute | solution.py:213
  43.0 1.9 %collective-permute-done.13 = bf16[2,96,128]{2,1,0:T(8,128)(2,1)S(1)} collective-permute-done((bf16[2,96,128]{2,1,0:T(8,128)(2,1)S(1)}, bf16[2,96,128]{2,1,0:T(8,128)(2,1)S(1)}, u32[]{:S(2)}, u32[]{:S(2)}) %collective-permute-start.13) | collective-permute-done | bytes 49184 | tf_op jit(solution)/shard_map/ppermute | solution.py:213
  44.9 3.7 %collective-permute-start.14 = (bf16[96,128]{1,0:T(8,128)(2,1)S(1)}, bf16[96,128]{1,0:T(8,128)(2,1)S(1)}, u32[]{:S(2)}, u32[]{:S(2)}) collective-permute-start(bf16[96,128]{1,0:T(8,128)(2,1)S(1)} %fusion.8), channel_id=1, source_target_pairs={{0,8},{1,9},{2,10},{3,11},{4,12},{5,13},{6,14},{7,15},{8,0},{9,1},... | collective-permute-start | bytes 73736 | tf_op jit(solution)/shard_map/ppermute | solution.py:213
  48.6 0.1 broadcast_multiply_fusion
  49.4 1.0 %collective-permute-done.14 = bf16[96,128]{1,0:T(8,128)(2,1)S(1)} collective-permute-done((bf16[96,128]{1,0:T(8,128)(2,1)S(1)}, bf16[96,128]{1,0:T(8,128)(2,1)S(1)}, u32[]{:S(2)}, u32[]{:S(2)}) %collective-permute-start.14) | collective-permute-done | bytes 24608 | tf_op jit(solution)/shard_map/ppermute | solution.py:213
  50.4 0.7 %divide_add_fusion = (f32[96,128]{1,0:T(8,128)}, f32[96,128]{1,0:T(8,128)}, f32[96,128]{1,0:T(8,128)}) fusion(f32[96,128]{1,0:T(8,128)S(1)} %bitcast.44, f32[]{:T(128)} %bitcast.11, f32[]{:T(128)} %bitcast.9, f32[96,128]{1,0:T(8,128)S(1)} %bitcast.43, bf16[96,128]{1,0:T(8,128)(2,1)S(1)} %collective-permute-done.14, f32[2,96,128]{2,1,0:T(8,128)S(1)} %fusion.5, ...), kind=kLoop, calls=%fused_computation.25 | loop fusion | flops 147456 | bytes 368648 | tf_op jit(solution)/shard_map/add | solution.py:208
  (16 shorter events, 0.2 us)
Async XLA Ops:
  0.6 3.6 %copy-start.1 = (f32[128,96]{0,1:T(8,128)S(1)}, f32[128,96]{0,1:T(8,128)}, u32[]{:S(2)}) copy-start(f32[128,96]{0,1:T(8,128)} %param.8) | copy-start | bytes 147460
  0.6 3.6 %copy-start = (s32[128,12288]{1,0:T(8,128)S(1)}, s32[128,12288]{1,0:T(8,128)}, u32[]{:S(2)}) copy-start(s32[128,12288]{1,0:T(8,128)} %refs_0_.7) | copy-start | bytes 18874372
  2.5 14.3 %collective-permute-start = (bf16[64,4352]{1,0:T(8,128)(2,1)S(1)}, bf16[64,4352]{1,0:T(8,128)(2,1)S(1)}, u32[]{:S(2)}, u32[]{:S(2)}) collective-permute-start(bf16[64,4352]{1,0:T(8,128)(2,1)S(1)} %first_rows.1), channel_id=1, source_target_pairs={{0,32},{1,33},{2,34},{3,35},{4,36},{5,37},{6,38},{7,39},{8,40},{9,... | collective-permute-start | bytes 1671176 | tf_op jit(solution)/shard_map/ppermute | solution.py:213
  4.8 14.3 %collective-permute-start.3 = (bf16[64,4096]{1,0:T(8,128)(2,1)S(1)}, bf16[64,4096]{1,0:T(8,128)(2,1)S(1)}, u32[]{:S(2)}, u32[]{:S(2)}) collective-permute-start(bf16[64,4096]{1,0:T(8,128)(2,1)S(1)} %dequantize.5), channel_id=1, source_target_pairs={{0,16},{1,17},{2,18},{3,19},{4,20},{5,21},{6,22},{7,23},{8,24},{9,... | collective-permute-start | bytes 1572872 | tf_op jit(solution)/shard_map/ppermute | solution.py:213
  7.4 23.9 %copy-start.2 = (s32[1,1,16,96]{3,2,1,0:T(8,128)S(1)}, s32[1,1,16,96]{3,2,1,0:T(8,128)}, u32[]{:S(2)}) copy-start(s32[1,1,16,96]{3,2,1,0:T(8,128)} %param.9) | copy-start | bytes 18436
  7.4 24.3 %copy-start.3 = (f32[1,12288]{1,0:T(1,128)S(1)}, f32[1,12288]{1,0:T(1,128)}, u32[]{:S(2)}) copy-start(f32[1,12288]{1,0:T(1,128)} %param.11) | copy-start | bytes 147460
  7.4 14.6 %collective-permute-start.2 = (bf16[64,3840]{1,0:T(8,128)(2,1)S(1)}, bf16[64,3840]{1,0:T(8,128)(2,1)S(1)}, u32[]{:S(2)}, u32[]{:S(2)}) collective-permute-start(bf16[64,3840]{1,0:T(8,128)(2,1)S(1)} %dequantize.4), channel_id=1, source_target_pairs={{0,96},{1,97},{2,98},{3,99},{4,100},{5,101},{6,102},{7,103},{8,104... | collective-permute-start | bytes 1474568 | tf_op jit(solution)/shard_map/ppermute | solution.py:213
  11.4 28.6 %copy-start.4 = (f32[1,12288]{1,0:T(1,128)S(1)}, f32[1,12288]{1,0:T(1,128)}, u32[]{:S(2)}) copy-start(f32[1,12288]{1,0:T(1,128)} %param.12) | copy-start | bytes 147460
  11.4 37.2 %copy-start.5 = (f32[1,12288]{1,0:T(1,128)S(1)}, f32[1,12288]{1,0:T(1,128)}, u32[]{:S(2)}) copy-start(f32[1,12288]{1,0:T(1,128)} %param.10) | copy-start | bytes 147460
  16.9 8.0 %collective-permute-start.1 = (bf16[32,4352]{1,0:T(8,128)(2,1)S(1)}, bf16[32,4352]{1,0:T(8,128)(2,1)S(1)}, u32[]{:S(2)}, u32[]{:S(2)}) collective-permute-start(bf16[32,4352]{1,0:T(8,128)(2,1)S(1)} %add_convert_fusion), channel_id=1, source_target_pairs={{0,16},{1,17},{2,18},{3,19},{4,20},{5,21},{6,22},{7,23},{8,24},{9,... | collective-permute-start | bytes 835592 | tf_op jit(solution)/shard_map/ppermute | solution.py:213
  19.2 8.6 %collective-permute-start.6 = (bf16[32,4096]{1,0:T(8,128)(2,1)S(1)}, bf16[32,4096]{1,0:T(8,128)(2,1)S(1)}, u32[]{:S(2)}, u32[]{:S(2)}) collective-permute-start(bf16[32,4096]{1,0:T(8,128)(2,1)S(1)} %add_convert_fusion.1), channel_id=1, source_target_pairs={{0,96},{1,97},{2,98},{3,99},{4,100},{5,101},{6,102},{7,103},{8,104... | collective-permute-start | bytes 786440 | tf_op jit(solution)/shard_map/ppermute | solution.py:213
  22.1 6.3 %collective-permute-start.8 = (bf16[32,3840]{1,0:T(8,128)(2,1)S(1)}, bf16[32,3840]{1,0:T(8,128)(2,1)S(1)}, u32[]{:S(2)}, u32[]{:S(2)}) collective-permute-start(bf16[32,3840]{1,0:T(8,128)(2,1)S(1)} %add_convert_fusion.2), channel_id=1, source_target_pairs={{0,32},{1,33},{2,34},{3,35},{4,36},{5,37},{6,38},{7,39},{8,40},{9,... | collective-permute-start | bytes 737288 | tf_op jit(solution)/shard_map/ppermute | solution.py:213
  25.0 6.3 %collective-permute-start.4 = (bf16[16,4352]{1,0:T(8,128)(2,1)S(1)}, bf16[16,4352]{1,0:T(8,128)(2,1)S(1)}, u32[]{:S(2)}, u32[]{:S(2)}) collective-permute-start(bf16[16,4352]{1,0:T(8,128)(2,1)S(1)} %add_convert_fusion.3), channel_id=1, source_target_pairs={{0,96},{1,97},{2,98},{3,99},{4,100},{5,101},{6,102},{7,103},{8,104... | collective-permute-start | bytes 417800 | tf_op jit(solution)/shard_map/ppermute | solution.py:213
  27.9 5.6 %collective-permute-start.7 = (bf16[16,4096]{1,0:T(8,128)(2,1)S(1)}, bf16[16,4096]{1,0:T(8,128)(2,1)S(1)}, u32[]{:S(2)}, u32[]{:S(2)}) collective-permute-start(bf16[16,4096]{1,0:T(8,128)(2,1)S(1)} %add_convert_fusion.4), channel_id=1, source_target_pairs={{0,32},{1,33},{2,34},{3,35},{4,36},{5,37},{6,38},{7,39},{8,40},{9,... | collective-permute-start | bytes 393224 | tf_op jit(solution)/shard_map/ppermute | solution.py:213
  28.5 5.0 %collective-permute-start.9 = (bf16[16,3840]{1,0:T(8,128)(2,1)S(1)}, bf16[16,3840]{1,0:T(8,128)(2,1)S(1)}, u32[]{:S(2)}, u32[]{:S(2)}) collective-permute-start(bf16[16,3840]{1,0:T(8,128)(2,1)S(1)} %add_convert_fusion.5), channel_id=1, source_target_pairs={{0,16},{1,17},{2,18},{3,19},{4,20},{5,21},{6,22},{7,23},{8,24},{9,... | collective-permute-start | bytes 368648 | tf_op jit(solution)/shard_map/ppermute | solution.py:213
  31.6 2.6 %collective-permute-start.5 = (bf16[4,2,34,128]{3,2,1,0:T(8,128)(2,1)S(1)}, bf16[4,2,34,128]{3,2,1,0:T(8,128)(2,1)S(1)}, u32[]{:S(2)}, u32[]{:S(2)}) collective-permute-start(bf16[4,2,34,128]{3,2,1,0:T(8,128)(2,1)S(1)} %get-tuple-element.26), channel_id=1, source_target_pairs={{0,1},{1,0},{2,3},{3,2},{4,5},{5,4},{6,7},{7,6},{8,9},{9,8},{10,11... | collective-permute-start | bytes 208904 | tf_op jit(solution)/shard_map/ppermute | solution.py:213
  34.1 1.4 %collective-permute-start.10 = (bf16[4,2,62,128]{3,2,1,0:T(8,128)(2,1)S(1)}, bf16[4,2,62,128]{3,2,1,0:T(8,128)(2,1)S(1)}, u32[]{:S(2)}, u32[]{:S(2)}) collective-permute-start(bf16[4,2,62,128]{3,2,1,0:T(8,128)(2,1)S(1)} %get-tuple-element.32), channel_id=1, source_target_pairs={{0,1},{1,0},{2,3},{3,2},{4,5},{5,4},{6,7},{7,6},{8,9},{9,8},{10,11... | collective-permute-start | bytes 380936 | tf_op jit(solution)/shard_map/ppermute | solution.py:213
  35.6 5.7 %collective-permute-start.11 = (bf16[2,96,128]{2,1,0:T(8,128)(2,1)S(1)}, bf16[2,96,128]{2,1,0:T(8,128)(2,1)S(1)}, u32[]{:S(2)}, u32[]{:S(2)}) collective-permute-start(bf16[2,96,128]{2,1,0:T(8,128)(2,1)S(1)} %get-tuple-element.36), channel_id=1, source_target_pairs={{0,4},{1,5},{2,6},{3,7},{4,0},{5,1},{6,2},{7,3},{8,12},{9,13},{10,... | collective-permute-start | bytes 147464 | tf_op jit(solution)/shard_map/ppermute | solution.py:213
  38.9 4.1 %collective-permute-start.12 = (bf16[2,96,128]{2,1,0:T(8,128)(2,1)S(1)}, bf16[2,96,128]{2,1,0:T(8,128)(2,1)S(1)}, u32[]{:S(2)}, u32[]{:S(2)}) collective-permute-start(bf16[2,96,128]{2,1,0:T(8,128)(2,1)S(1)} %get-tuple-element.38), channel_id=1, source_target_pairs={{0,2},{1,3},{2,0},{3,1},{4,6},{5,7},{6,4},{7,5},{8,10},{9,11},{10,... | collective-permute-start | bytes 147464 | tf_op jit(solution)/shard_map/ppermute | solution.py:213
  39.6 5.3 %collective-permute-start.13 = (bf16[2,96,128]{2,1,0:T(8,128)(2,1)S(1)}, bf16[2,96,128]{2,1,0:T(8,128)(2,1)S(1)}, u32[]{:S(2)}, u32[]{:S(2)}) collective-permute-start(bf16[2,96,128]{2,1,0:T(8,128)(2,1)S(1)} %get-tuple-element.37), channel_id=1, source_target_pairs={{0,6},{1,7},{2,4},{3,5},{4,2},{5,3},{6,0},{7,1},{8,14},{9,15},{10,... | collective-permute-start | bytes 147464 | tf_op jit(solution)/shard_map/ppermute | solution.py:213
  44.9 5.5 %collective-permute-start.14 = (bf16[96,128]{1,0:T(8,128)(2,1)S(1)}, bf16[96,128]{1,0:T(8,128)(2,1)S(1)}, u32[]{:S(2)}, u32[]{:S(2)}) collective-permute-start(bf16[96,128]{1,0:T(8,128)(2,1)S(1)} %fusion.8), channel_id=1, source_target_pairs={{0,8},{1,9},{2,10},{3,11},{4,12},{5,13},{6,14},{7,15},{8,0},{9,1},... | collective-permute-start | bytes 73736 | tf_op jit(solution)/shard_map/ppermute | solution.py:213

commit v7 on v6

--- a/solution.py
+++ b/solution.py
@@ -17,9 +17,9 @@
 COLUMNS = BLOCKS * LANES
 TILE = 16
 PIECES = (
-    (0, 34, "PZQ"),
-    (34, 32, "ZQP"),
-    (66, 30, "QPZ"),
+    (0, 32, "PZQ"),
+    (32, 33, "ZQP"),
+    (65, 31, "QPZ"),
 )
 SUMS = ((0, 1), (1, 1), (2, 1), (0, 2), (1, 2), (2, 2))
 EARLY = 1

time: 51.7 us -> 52.2 us (level)
  starting transfers between devices: 24.4 us -> 25 us
    ppermute x15, starting transfers between devices: 24.4 us -> 25 us  [send(): return lax.ppermute(array.astype(jnp.bfloat16), axes, route)]
  transfers between devices with their start and end apart: 15 -> 15, of which waited for: 10 -> 12; matrix products, arithmetic and copies ran while one was open for 1% -> 1% of each run, Pallas kernels for 7% -> 7%
where the time goes in v7:
time: 52.2 us; the launch traced here: 51.5 us
  starting transfers between devices  25 us (48%)
  waiting for transfers between devices  18.1 us (35%)
  Pallas kernels  5.56 us (11%)
  between operations  1.56 us (3%)
  other arithmetic  1.28 us (2%)
    ppermute x15, starting transfers between devices, send(): return lax.ppermute(array.astype(jnp.bfloat16), axes, route)  25 us
    ppermute x15, waiting for transfers between devices, send(): return lax.ppermute(array.astype(jnp.bfloat16), axes, route)  18.1 us
    pallas_call x3, Pallas kernels, dequantize(): pl.pallas_call(lambda *refs: dequantize_kernel(parts, *refs), out_shape=[...  2.69 us
    pallas_call x1, Pallas kernels, first_rows(): pl.pallas_call(lambda *refs: first_kernel(piece, *refs), out_shape=jax.Sh...  1.86 us
  transfers between devices with their start and end apart: 15, of which 12 were waited for; matrix products, arithmetic and copies ran while one was open for 1% of the time, Pallas kernels for 7%

profile of v7, /device:TPU:0, one launch (start us, length us, event | category | flops | bytes accessed | tf_op | source)
XLA Modules:
  0.0 51.5 jit_solution(17219659553077348029)
XLA Ops:
  0.6 1.9 %first_rows.1 = bf16[64,4096]{1,0:T(8,128)(2,1)S(1)} custom-call(s32[128,12288]{1,0:T(8,128)} %refs_0_.7, f32[96,128]{1,0:T(8,128)} %bitcast.36), custom_call_target="tpu_custom_call" | custom-call | tf_op jit(solution)/shard_map/first_rows/pallas_call | solution.py:113
  2.5 1.7 %collective-permute-start = (bf16[64,4096]{1,0:T(8,128)(2,1)S(1)}, bf16[64,4096]{1,0:T(8,128)(2,1)S(1)}, u32[]{:S(2)}, u32[]{:S(2)}) collective-permute-start(bf16[64,4096]{1,0:T(8,128)(2,1)S(1)} %first_rows.1), channel_id=1, source_target_pairs={{0,32},{1,33},{2,34},{3,35},{4,36},{5,37},{6,38},{7,39},{8,40},{9,... | collective-permute-start | bytes 1572872 | tf_op jit(solution)/shard_map/ppermute | solution.py:213
  4.2 0.6 %dequantize.5 = bf16[64,4224]{1,0:T(8,128)(2,1)S(1)} custom-call(s32[128,12288]{1,0:T(8,128)S(1)} %copy-done, f32[96,128]{1,0:T(8,128)S(1)} %bitcast.37), custom_call_target="tpu_custom_call" | custom-call | tf_op jit(solution)/shard_map/dequantize/pallas_call | solution.py:148
  4.8 2.0 %collective-permute-start.3 = (bf16[64,4224]{1,0:T(8,128)(2,1)S(1)}, bf16[64,4224]{1,0:T(8,128)(2,1)S(1)}, u32[]{:S(2)}, u32[]{:S(2)}) collective-permute-start(bf16[64,4224]{1,0:T(8,128)(2,1)S(1)} %dequantize.5), channel_id=1, source_target_pairs={{0,16},{1,17},{2,18},{3,19},{4,20},{5,21},{6,22},{7,23},{8,24},{9,... | collective-permute-start | bytes 1622024 | tf_op jit(solution)/shard_map/ppermute | solution.py:213
  6.8 0.6 %dequantize.4 = bf16[64,3968]{1,0:T(8,128)(2,1)S(1)} custom-call(s32[128,12288]{1,0:T(8,128)S(1)} %copy-done, f32[96,128]{1,0:T(8,128)S(1)} %bitcast.38), custom_call_target="tpu_custom_call" | custom-call | tf_op jit(solution)/shard_map/dequantize/pallas_call | solution.py:148
  7.4 0.0 copy-start.2
  7.4 0.0 copy-start.3
  7.4 2.5 %collective-permute-start.2 = (bf16[64,3968]{1,0:T(8,128)(2,1)S(1)}, bf16[64,3968]{1,0:T(8,128)(2,1)S(1)}, u32[]{:S(2)}, u32[]{:S(2)}) collective-permute-start(bf16[64,3968]{1,0:T(8,128)(2,1)S(1)} %dequantize.4), channel_id=1, source_target_pairs={{0,96},{1,97},{2,98},{3,99},{4,100},{5,101},{6,102},{7,103},{8,104... | collective-permute-start | bytes 1523720 | tf_op jit(solution)/shard_map/ppermute | solution.py:213
  9.9 1.5 %dequantize.3 = (bf16[64,4096]{1,0:T(8,128)(2,1)S(1)}, bf16[64,4224]{1,0:T(8,128)(2,1)S(1)}, bf16[64,3968]{1,0:T(8,128)(2,1)S(1)}) custom-call(s32[128,12288]{1,0:T(8,128)S(1)} %copy-done, f32[96,128]{1,0:T(8,128)S(1)} %bitcast.39), custom_call_target="tpu_custom_call" | custom-call | tf_op jit(solution)/shard_map/dequantize/pallas_call | solution.py:148
  11.4 0.0 copy-start.4
  11.4 0.0 copy-start.5
  11.4 4.7 %collective-permute-done.refs_2_ = bf16[64,4096]{1,0:T(8,128)(2,1)S(1)} collective-permute-done((bf16[64,4096]{1,0:T(8,128)(2,1)S(1)}, bf16[64,4096]{1,0:T(8,128)(2,1)S(1)}, u32[]{:S(2)}, u32[]{:S(2)}) %collective-permute-start) | collective-permute-done | bytes 524320 | tf_op jit(solution)/shard_map/ppermute | solution.py:213
  16.1 0.1 add_convert_fusion.1
  16.2 2.2 %collective-permute-start.1 = (bf16[32,4096]{1,0:T(8,128)(2,1)S(1)}, bf16[32,4096]{1,0:T(8,128)(2,1)S(1)}, u32[]{:S(2)}, u32[]{:S(2)}) collective-permute-start(bf16[32,4096]{1,0:T(8,128)(2,1)S(1)} %add_convert_fusion.1), channel_id=1, source_target_pairs={{0,16},{1,17},{2,18},{3,19},{4,20},{5,21},{6,22},{7,23},{8,24},{9,... | collective-permute-start | bytes 786440 | tf_op jit(solution)/shard_map/ppermute | solution.py:213
  18.4 0.9 %collective-permute-done.3.refs_2_ = bf16[64,4224]{1,0:T(8,128)(2,1)S(1)} collective-permute-done((bf16[64,4224]{1,0:T(8,128)(2,1)S(1)}, bf16[64,4224]{1,0:T(8,128)(2,1)S(1)}, u32[]{:S(2)}, u32[]{:S(2)}) %collective-permute-start.3) | collective-permute-done | bytes 540704 | tf_op jit(solution)/shard_map/ppermute | solution.py:213
  19.3 0.1 add_convert_fusion
  19.4 2.8 %collective-permute-start.6 = (bf16[32,4224]{1,0:T(8,128)(2,1)S(1)}, bf16[32,4224]{1,0:T(8,128)(2,1)S(1)}, u32[]{:S(2)}, u32[]{:S(2)}) collective-permute-start(bf16[32,4224]{1,0:T(8,128)(2,1)S(1)} %add_convert_fusion), channel_id=1, source_target_pairs={{0,96},{1,97},{2,98},{3,99},{4,100},{5,101},{6,102},{7,103},{8,104... | collective-permute-start | bytes 811016 | tf_op jit(solution)/shard_map/ppermute | solution.py:213
  22.1 0.1 add_convert_fusion.2
  22.2 0.3 collective-permute-start.8
  22.5 1.9 %collective-permute-done.1.refs_3_ = bf16[32,4096]{1,0:T(8,128)(2,1)S(1)} collective-permute-done((bf16[32,4096]{1,0:T(8,128)(2,1)S(1)}, bf16[32,4096]{1,0:T(8,128)(2,1)S(1)}, u32[]{:S(2)}, u32[]{:S(2)}) %collective-permute-start.1) | collective-permute-done | bytes 262176 | tf_op jit(solution)/shard_map/ppermute | solution.py:213
  24.4 0.1 add_convert_fusion.4
  24.5 2.8 %collective-permute-start.4 = (bf16[16,4096]{1,0:T(8,128)(2,1)S(1)}, bf16[16,4096]{1,0:T(8,128)(2,1)S(1)}, u32[]{:S(2)}, u32[]{:S(2)}) collective-permute-start(bf16[16,4096]{1,0:T(8,128)(2,1)S(1)} %add_convert_fusion.4), channel_id=1, source_target_pairs={{0,96},{1,97},{2,98},{3,99},{4,100},{5,101},{6,102},{7,103},{8,104... | collective-permute-start | bytes 393224 | tf_op jit(solution)/shard_map/ppermute | solution.py:213
  27.3 0.4 collective-permute-done.6.refs_3_
  27.6 0.1 add_convert_fusion.3
  27.7 0.9 %collective-permute-start.7 = (bf16[16,4224]{1,0:T(8,128)(2,1)S(1)}, bf16[16,4224]{1,0:T(8,128)(2,1)S(1)}, u32[]{:S(2)}, u32[]{:S(2)}) collective-permute-start(bf16[16,4224]{1,0:T(8,128)(2,1)S(1)} %add_convert_fusion.3), channel_id=1, source_target_pairs={{0,32},{1,33},{2,34},{3,35},{4,36},{5,37},{6,38},{7,39},{8,40},{9,... | collective-permute-start | bytes 405512 | tf_op jit(solution)/shard_map/ppermute | solution.py:213
  28.6 0.3 collective-permute-done.8.refs_7_
  28.9 0.1 add_convert_fusion.5
  29.0 1.7 %collective-permute-start.9 = (bf16[16,3968]{1,0:T(8,128)(2,1)S(1)}, bf16[16,3968]{1,0:T(8,128)(2,1)S(1)}, u32[]{:S(2)}, u32[]{:S(2)}) collective-permute-start(bf16[16,3968]{1,0:T(8,128)(2,1)S(1)} %add_convert_fusion.5), channel_id=1, source_target_pairs={{0,16},{1,17},{2,18},{3,19},{4,20},{5,21},{6,22},{7,23},{8,24},{9,... | collective-permute-start | bytes 380936 | tf_op jit(solution)/shard_map/ppermute | solution.py:213
  30.6 0.1 collective-permute-done.4.refs_4_
  30.7 0.3 finish.2
  31.1 0.1 collective-permute-start.5
  31.2 0.1 broadcast_multiply_fusion.2
  31.2 2.7 %collective-permute-done.9.refs_8_ = bf16[16,3968]{1,0:T(8,128)(2,1)S(1)} collective-permute-done((bf16[16,3968]{1,0:T(8,128)(2,1)S(1)}, bf16[16,3968]{1,0:T(8,128)(2,1)S(1)}, u32[]{:S(2)}, u32[]{:S(2)}) %collective-permute-start.9) | collective-permute-done | bytes 127008 | tf_op jit(solution)/shard_map/ppermute | solution.py:213
  34.0 0.0 collective-permute-done.7.refs_4_
  34.0 0.7 %finish.3 = (bf16[4,2,64,128]{3,2,1,0:T(8,128)(2,1)S(1)}, f32[4,2,64,128]{3,2,1,0:T(8,128)S(1)}) custom-call(s32[16,96]{1,0:T(8,128)S(1)} %bitcast.41, bf16[64,4224]{1,0:T(8,128)(2,1)S(1)} %get-tuple-element.20.refs_1_, bf16[64,4224]{1,0:T(8,128)(2,1)S(1)} %collective-permute-done.3.refs_2_, bf16[32,4224]{1,0:T(8,128)(2,1)S(1)} %collective-permute-done.6.refs_3_, ...), custom_call_target="tpu_custom_call" | custom-call | tf_op jit(solution)/shard_map/finish/pallas_call | solution.py:191
  34.6 0.1 collective-permute-start.10
  34.8 1.3 %collective-permute-done.10 = bf16[4,2,64,128]{3,2,1,0:T(8,128)(2,1)S(1)} collective-permute-done((bf16[4,2,64,128]{3,2,1,0:T(8,128)(2,1)S(1)}, bf16[4,2,64,128]{3,2,1,0:T(8,128)(2,1)S(1)}, u32[]{:S(2)}, u32[]{:S(2)}) %collective-permute-start.10) | collective-permute-done | bytes 131104 | tf_op jit(solution)/shard_map/ppermute | solution.py:213
  36.2 3.3 %collective-permute-start.11 = (bf16[2,96,128]{2,1,0:T(8,128)(2,1)S(1)}, bf16[2,96,128]{2,1,0:T(8,128)(2,1)S(1)}, u32[]{:S(2)}, u32[]{:S(2)}) collective-permute-start(bf16[2,96,128]{2,1,0:T(8,128)(2,1)S(1)} %get-tuple-element.36), channel_id=1, source_target_pairs={{0,4},{1,5},{2,6},{3,7},{4,0},{5,1},{6,2},{7,3},{8,12},{9,13},{10,... | collective-permute-start | bytes 147464 | tf_op jit(solution)/shard_map/ppermute | solution.py:213
  39.4 0.7 %collective-permute-start.12 = (bf16[2,96,128]{2,1,0:T(8,128)(2,1)S(1)}, bf16[2,96,128]{2,1,0:T(8,128)(2,1)S(1)}, u32[]{:S(2)}, u32[]{:S(2)}) collective-permute-start(bf16[2,96,128]{2,1,0:T(8,128)(2,1)S(1)} %get-tuple-element.38), channel_id=1, source_target_pairs={{0,2},{1,3},{2,0},{3,1},{4,6},{5,7},{6,4},{7,5},{8,10},{9,11},{10,... | collective-permute-start | bytes 147464 | tf_op jit(solution)/shard_map/ppermute | solution.py:213
  40.1 0.4 collective-permute-start.13
  40.5 0.1 broadcast_multiply_fusion.1
  40.5 1.3 %collective-permute-done.11 = bf16[2,96,128]{2,1,0:T(8,128)(2,1)S(1)} collective-permute-done((bf16[2,96,128]{2,1,0:T(8,128)(2,1)S(1)}, bf16[2,96,128]{2,1,0:T(8,128)(2,1)S(1)}, u32[]{:S(2)}, u32[]{:S(2)}) %collective-permute-start.11) | collective-permute-done | bytes 49184 | tf_op jit(solution)/shard_map/ppermute | solution.py:213
  41.8 1.7 %collective-permute-done.12 = bf16[2,96,128]{2,1,0:T(8,128)(2,1)S(1)} collective-permute-done((bf16[2,96,128]{2,1,0:T(8,128)(2,1)S(1)}, bf16[2,96,128]{2,1,0:T(8,128)(2,1)S(1)}, u32[]{:S(2)}, u32[]{:S(2)}) %collective-permute-start.12) | collective-permute-done | bytes 49184 | tf_op jit(solution)/shard_map/ppermute | solution.py:213
  43.5 1.9 %collective-permute-done.13 = bf16[2,96,128]{2,1,0:T(8,128)(2,1)S(1)} collective-permute-done((bf16[2,96,128]{2,1,0:T(8,128)(2,1)S(1)}, bf16[2,96,128]{2,1,0:T(8,128)(2,1)S(1)}, u32[]{:S(2)}, u32[]{:S(2)}) %collective-permute-start.13) | collective-permute-done | bytes 49184 | tf_op jit(solution)/shard_map/ppermute | solution.py:213
  45.4 3.6 %collective-permute-start.14 = (bf16[96,128]{1,0:T(8,128)(2,1)S(1)}, bf16[96,128]{1,0:T(8,128)(2,1)S(1)}, u32[]{:S(2)}, u32[]{:S(2)}) collective-permute-start(bf16[96,128]{1,0:T(8,128)(2,1)S(1)} %fusion.8), channel_id=1, source_target_pairs={{0,8},{1,9},{2,10},{3,11},{4,12},{5,13},{6,14},{7,15},{8,0},{9,1},... | collective-permute-start | bytes 73736 | tf_op jit(solution)/shard_map/ppermute | solution.py:213
  49.1 0.1 broadcast_multiply_fusion
  49.9 1.0 %collective-permute-done.14 = bf16[96,128]{1,0:T(8,128)(2,1)S(1)} collective-permute-done((bf16[96,128]{1,0:T(8,128)(2,1)S(1)}, bf16[96,128]{1,0:T(8,128)(2,1)S(1)}, u32[]{:S(2)}, u32[]{:S(2)}) %collective-permute-start.14) | collective-permute-done | bytes 24608 | tf_op jit(solution)/shard_map/ppermute | solution.py:213
  50.9 0.7 %divide_add_fusion = (f32[96,128]{1,0:T(8,128)}, f32[96,128]{1,0:T(8,128)}, f32[96,128]{1,0:T(8,128)}) fusion(f32[96,128]{1,0:T(8,128)S(1)} %bitcast.44, f32[]{:T(128)} %bitcast.11, f32[]{:T(128)} %bitcast.9, f32[96,128]{1,0:T(8,128)S(1)} %bitcast.43, bf16[96,128]{1,0:T(8,128)(2,1)S(1)} %collective-permute-done.14, f32[2,96,128]{2,1,0:T(8,128)S(1)} %fusion.5, ...), kind=kLoop, calls=%fused_computation.25 | loop fusion | flops 147456 | bytes 368648 | tf_op jit(solution)/shard_map/add | solution.py:208
  (16 shorter events, 0.1 us)
Async XLA Ops:
  0.6 3.5 %copy-start.1 = (f32[128,96]{0,1:T(8,128)S(1)}, f32[128,96]{0,1:T(8,128)}, u32[]{:S(2)}) copy-start(f32[128,96]{0,1:T(8,128)} %param.8) | copy-start | bytes 147460
  0.6 3.5 %copy-start = (s32[128,12288]{1,0:T(8,128)S(1)}, s32[128,12288]{1,0:T(8,128)}, u32[]{:S(2)}) copy-start(s32[128,12288]{1,0:T(8,128)} %refs_0_.7) | copy-start | bytes 18874372
  2.5 13.6 %collective-permute-start = (bf16[64,4096]{1,0:T(8,128)(2,1)S(1)}, bf16[64,4096]{1,0:T(8,128)(2,1)S(1)}, u32[]{:S(2)}, u32[]{:S(2)}) collective-permute-start(bf16[64,4096]{1,0:T(8,128)(2,1)S(1)} %first_rows.1), channel_id=1, source_target_pairs={{0,32},{1,33},{2,34},{3,35},{4,36},{5,37},{6,38},{7,39},{8,40},{9,... | collective-permute-start | bytes 1572872 | tf_op jit(solution)/shard_map/ppermute | solution.py:213
  4.8 14.5 %collective-permute-start.3 = (bf16[64,4224]{1,0:T(8,128)(2,1)S(1)}, bf16[64,4224]{1,0:T(8,128)(2,1)S(1)}, u32[]{:S(2)}, u32[]{:S(2)}) collective-permute-start(bf16[64,4224]{1,0:T(8,128)(2,1)S(1)} %dequantize.5), channel_id=1, source_target_pairs={{0,16},{1,17},{2,18},{3,19},{4,20},{5,21},{6,22},{7,23},{8,24},{9,... | collective-permute-start | bytes 1622024 | tf_op jit(solution)/shard_map/ppermute | solution.py:213
  7.4 23.3 %copy-start.2 = (s32[1,1,16,96]{3,2,1,0:T(8,128)S(1)}, s32[1,1,16,96]{3,2,1,0:T(8,128)}, u32[]{:S(2)}) copy-start(s32[1,1,16,96]{3,2,1,0:T(8,128)} %param.9) | copy-start | bytes 18436
  7.4 23.8 %copy-start.3 = (f32[1,12288]{1,0:T(1,128)S(1)}, f32[1,12288]{1,0:T(1,128)}, u32[]{:S(2)}) copy-start(f32[1,12288]{1,0:T(1,128)} %param.11) | copy-start | bytes 147460
  7.4 14.7 %collective-permute-start.2 = (bf16[64,3968]{1,0:T(8,128)(2,1)S(1)}, bf16[64,3968]{1,0:T(8,128)(2,1)S(1)}, u32[]{:S(2)}, u32[]{:S(2)}) collective-permute-start(bf16[64,3968]{1,0:T(8,128)(2,1)S(1)} %dequantize.4), channel_id=1, source_target_pairs={{0,96},{1,97},{2,98},{3,99},{4,100},{5,101},{6,102},{7,103},{8,104... | collective-permute-start | bytes 1523720 | tf_op jit(solution)/shard_map/ppermute | solution.py:213
  11.4 29.1 %copy-start.4 = (f32[1,12288]{1,0:T(1,128)S(1)}, f32[1,12288]{1,0:T(1,128)}, u32[]{:S(2)}) copy-start(f32[1,12288]{1,0:T(1,128)} %param.12) | copy-start | bytes 147460
  11.4 37.7 %copy-start.5 = (f32[1,12288]{1,0:T(1,128)S(1)}, f32[1,12288]{1,0:T(1,128)}, u32[]{:S(2)}) copy-start(f32[1,12288]{1,0:T(1,128)} %param.10) | copy-start | bytes 147460
  16.2 8.2 %collective-permute-start.1 = (bf16[32,4096]{1,0:T(8,128)(2,1)S(1)}, bf16[32,4096]{1,0:T(8,128)(2,1)S(1)}, u32[]{:S(2)}, u32[]{:S(2)}) collective-permute-start(bf16[32,4096]{1,0:T(8,128)(2,1)S(1)} %add_convert_fusion.1), channel_id=1, source_target_pairs={{0,16},{1,17},{2,18},{3,19},{4,20},{5,21},{6,22},{7,23},{8,24},{9,... | collective-permute-start | bytes 786440 | tf_op jit(solution)/shard_map/ppermute | solution.py:213
  19.4 8.3 %collective-permute-start.6 = (bf16[32,4224]{1,0:T(8,128)(2,1)S(1)}, bf16[32,4224]{1,0:T(8,128)(2,1)S(1)}, u32[]{:S(2)}, u32[]{:S(2)}) collective-permute-start(bf16[32,4224]{1,0:T(8,128)(2,1)S(1)} %add_convert_fusion), channel_id=1, source_target_pairs={{0,96},{1,97},{2,98},{3,99},{4,100},{5,101},{6,102},{7,103},{8,104... | collective-permute-start | bytes 811016 | tf_op jit(solution)/shard_map/ppermute | solution.py:213
  22.2 6.7 %collective-permute-start.8 = (bf16[32,3968]{1,0:T(8,128)(2,1)S(1)}, bf16[32,3968]{1,0:T(8,128)(2,1)S(1)}, u32[]{:S(2)}, u32[]{:S(2)}) collective-permute-start(bf16[32,3968]{1,0:T(8,128)(2,1)S(1)} %add_convert_fusion.2), channel_id=1, source_target_pairs={{0,32},{1,33},{2,34},{3,35},{4,36},{5,37},{6,38},{7,39},{8,40},{9,... | collective-permute-start | bytes 761864 | tf_op jit(solution)/shard_map/ppermute | solution.py:213
  24.5 6.3 %collective-permute-start.4 = (bf16[16,4096]{1,0:T(8,128)(2,1)S(1)}, bf16[16,4096]{1,0:T(8,128)(2,1)S(1)}, u32[]{:S(2)}, u32[]{:S(2)}) collective-permute-start(bf16[16,4096]{1,0:T(8,128)(2,1)S(1)} %add_convert_fusion.4), channel_id=1, source_target_pairs={{0,96},{1,97},{2,98},{3,99},{4,100},{5,101},{6,102},{7,103},{8,104... | collective-permute-start | bytes 393224 | tf_op jit(solution)/shard_map/ppermute | solution.py:213
  27.7 6.3 %collective-permute-start.7 = (bf16[16,4224]{1,0:T(8,128)(2,1)S(1)}, bf16[16,4224]{1,0:T(8,128)(2,1)S(1)}, u32[]{:S(2)}, u32[]{:S(2)}) collective-permute-start(bf16[16,4224]{1,0:T(8,128)(2,1)S(1)} %add_convert_fusion.3), channel_id=1, source_target_pairs={{0,32},{1,33},{2,34},{3,35},{4,36},{5,37},{6,38},{7,39},{8,40},{9,... | collective-permute-start | bytes 405512 | tf_op jit(solution)/shard_map/ppermute | solution.py:213
  29.0 5.0 %collective-permute-start.9 = (bf16[16,3968]{1,0:T(8,128)(2,1)S(1)}, bf16[16,3968]{1,0:T(8,128)(2,1)S(1)}, u32[]{:S(2)}, u32[]{:S(2)}) collective-permute-start(bf16[16,3968]{1,0:T(8,128)(2,1)S(1)} %add_convert_fusion.5), channel_id=1, source_target_pairs={{0,16},{1,17},{2,18},{3,19},{4,20},{5,21},{6,22},{7,23},{8,24},{9,... | collective-permute-start | bytes 380936 | tf_op jit(solution)/shard_map/ppermute | solution.py:213
  31.1 3.6 %collective-permute-start.5 = (bf16[4,2,32,128]{3,2,1,0:T(8,128)(2,1)S(1)}, bf16[4,2,32,128]{3,2,1,0:T(8,128)(2,1)S(1)}, u32[]{:S(2)}, u32[]{:S(2)}) collective-permute-start(bf16[4,2,32,128]{3,2,1,0:T(8,128)(2,1)S(1)} %get-tuple-element.26), channel_id=1, source_target_pairs={{0,1},{1,0},{2,3},{3,2},{4,5},{5,4},{6,7},{7,6},{8,9},{9,8},{10,11... | collective-permute-start | bytes 196616 | tf_op jit(solution)/shard_map/ppermute | solution.py:213
  34.6 1.4 %collective-permute-start.10 = (bf16[4,2,64,128]{3,2,1,0:T(8,128)(2,1)S(1)}, bf16[4,2,64,128]{3,2,1,0:T(8,128)(2,1)S(1)}, u32[]{:S(2)}, u32[]{:S(2)}) collective-permute-start(bf16[4,2,64,128]{3,2,1,0:T(8,128)(2,1)S(1)} %get-tuple-element.32), channel_id=1, source_target_pairs={{0,1},{1,0},{2,3},{3,2},{4,5},{5,4},{6,7},{7,6},{8,9},{9,8},{10,11... | collective-permute-start | bytes 393224 | tf_op jit(solution)/shard_map/ppermute | solution.py:213
  36.2 5.7 %collective-permute-start.11 = (bf16[2,96,128]{2,1,0:T(8,128)(2,1)S(1)}, bf16[2,96,128]{2,1,0:T(8,128)(2,1)S(1)}, u32[]{:S(2)}, u32[]{:S(2)}) collective-permute-start(bf16[2,96,128]{2,1,0:T(8,128)(2,1)S(1)} %get-tuple-element.36), channel_id=1, source_target_pairs={{0,4},{1,5},{2,6},{3,7},{4,0},{5,1},{6,2},{7,3},{8,12},{9,13},{10,... | collective-permute-start | bytes 147464 | tf_op jit(solution)/shard_map/ppermute | solution.py:213
  39.4 4.1 %collective-permute-start.12 = (bf16[2,96,128]{2,1,0:T(8,128)(2,1)S(1)}, bf16[2,96,128]{2,1,0:T(8,128)(2,1)S(1)}, u32[]{:S(2)}, u32[]{:S(2)}) collective-permute-start(bf16[2,96,128]{2,1,0:T(8,128)(2,1)S(1)} %get-tuple-element.38), channel_id=1, source_target_pairs={{0,2},{1,3},{2,0},{3,1},{4,6},{5,7},{6,4},{7,5},{8,10},{9,11},{10,... | collective-permute-start | bytes 147464 | tf_op jit(solution)/shard_map/ppermute | solution.py:213
  40.1 5.3 %collective-permute-start.13 = (bf16[2,96,128]{2,1,0:T(8,128)(2,1)S(1)}, bf16[2,96,128]{2,1,0:T(8,128)(2,1)S(1)}, u32[]{:S(2)}, u32[]{:S(2)}) collective-permute-start(bf16[2,96,128]{2,1,0:T(8,128)(2,1)S(1)} %get-tuple-element.37), channel_id=1, source_target_pairs={{0,6},{1,7},{2,4},{3,5},{4,2},{5,3},{6,0},{7,1},{8,14},{9,15},{10,... | collective-permute-start | bytes 147464 | tf_op jit(solution)/shard_map/ppermute | solution.py:213
  45.4 5.4 %collective-permute-start.14 = (bf16[96,128]{1,0:T(8,128)(2,1)S(1)}, bf16[96,128]{1,0:T(8,128)(2,1)S(1)}, u32[]{:S(2)}, u32[]{:S(2)}) collective-permute-start(bf16[96,128]{1,0:T(8,128)(2,1)S(1)} %fusion.8), channel_id=1, source_target_pairs={{0,8},{1,9},{2,10},{3,11},{4,12},{5,13},{6,14},{7,15},{8,0},{9,1},... | collective-permute-start | bytes 73736 | tf_op jit(solution)/shard_map/ppermute | solution.py:213

commit v8 on v6

--- a/solution.py
+++ b/solution.py
@@ -37,7 +37,7 @@
     return (label["Q"] << 2) | ((label["P"] ^ label["Q"]) << 1) | label["Z"]
 
 
-Y_FLIPS = (3, 1, 2, 0)
+Y_FLIPS = ((3, 1, 2, 0), (1, 2, 3, 0))
 
 
 def wide_at(wide, z_flip, y_flip, core):
@@ -175,9 +175,10 @@
             rows[pl.ds(at - start, TILE, stride=stride), :] = coded.astype(jnp.float32) * scale[:, at : at + 1]
     wide = lax.axis_index("wide")
     core = wide & 1
-    for slot, y_flip in enumerate(Y_FLIPS):
+    for slot, (first, second) in enumerate(zip(*Y_FLIPS)):
         for z_slot, z_flip in enumerate((1, 0)):
             for ref, owner in ((send_ref, 1 - core), (keep_ref, core)):
+                y_flip = first + owner * (second - first)
                 row = pl.multiple_of(wide_at(wide, z_flip, y_flip, owner) * stride, 8)
                 ref[slot, z_slot] = rows[pl.ds(row, blocks), :].astype(ref.dtype)
 
@@ -249,7 +250,7 @@
         requant, away = lax.optimization_barrier((requant, away))
         near.append(total(keep, send(away, "wide", [(b, b ^ 1) for b in range(16)])))
     near = jnp.concatenate(near, axis=2)
-    routes = [[(b, wide_at(b, 0, y_flip, b & 1)) for b in range(16)] for y_flip in Y_FLIPS[:3]]
+    routes = [[(b, wide_at(b, 0, Y_FLIPS[b & 1][slot], b & 1)) for b in range(16)] for slot in range(3)]
     chip = total(near[3], *[send(near[slot], "wide", route) for slot, route in enumerate(routes)])
     gradient = total(chip[1], send(chip[0], "wide", [(b, b ^ 8) for b in range(16)]))
     tall = (BLOCKS, LANES)

time: 51.7 us -> 51.7 us (level)
  no operation moved by 1% of the time
where the time goes in v8:
time: 51.7 us; the launch traced here: 51.1 us
  starting transfers between devices  24.4 us (47%)
  waiting for transfers between devices  18.3 us (35%)
  Pallas kernels  5.47 us (11%)
  between operations  1.56 us (3%)
  other arithmetic  1.3 us (3%)
    ppermute x15, starting transfers between devices, send(): return lax.ppermute(array.astype(jnp.bfloat16), axes, route)  24.4 us
    ppermute x15, waiting for transfers between devices, send(): return lax.ppermute(array.astype(jnp.bfloat16), axes, route)  18.3 us
    pallas_call x3, Pallas kernels, dequantize(): pl.pallas_call(lambda *refs: dequantize_kernel(parts, *refs), out_shape=[...  2.67 us
    pallas_call x1, Pallas kernels, first_rows(): pl.pallas_call(lambda *refs: first_kernel(piece, *refs), out_shape=jax.Sh...  1.89 us
  transfers between devices with their start and end apart: 15, of which 10 were waited for; matrix products, arithmetic and copies ran while one was open for 1% of the time, Pallas kernels for 7%

profile of v8, /device:TPU:0, one launch (start us, length us, event | category | flops | bytes accessed | tf_op | source)
XLA Modules:
  0.0 51.1 jit_solution(10490440520092890101)
XLA Ops:
  0.6 1.9 %first_rows.1 = bf16[64,4352]{1,0:T(8,128)(2,1)S(1)} custom-call(s32[128,12288]{1,0:T(8,128)} %refs_0_.7, f32[96,128]{1,0:T(8,128)} %bitcast.36), custom_call_target="tpu_custom_call" | custom-call | tf_op jit(solution)/shard_map/first_rows/pallas_call | solution.py:113
  2.5 1.7 %collective-permute-start = (bf16[64,4352]{1,0:T(8,128)(2,1)S(1)}, bf16[64,4352]{1,0:T(8,128)(2,1)S(1)}, u32[]{:S(2)}, u32[]{:S(2)}) collective-permute-start(bf16[64,4352]{1,0:T(8,128)(2,1)S(1)} %first_rows.1), channel_id=1, source_target_pairs={{0,32},{1,33},{2,34},{3,35},{4,36},{5,37},{6,38},{7,39},{8,40},{9,... | collective-permute-start | bytes 1671176 | tf_op jit(solution)/shard_map/ppermute | solution.py:214
  4.2 0.6 %dequantize.5 = bf16[64,4096]{1,0:T(8,128)(2,1)S(1)} custom-call(s32[128,12288]{1,0:T(8,128)S(1)} %copy-done, f32[96,128]{1,0:T(8,128)S(1)} %bitcast.37), custom_call_target="tpu_custom_call" | custom-call | tf_op jit(solution)/shard_map/dequantize/pallas_call | solution.py:148
  4.8 2.0 %collective-permute-start.3 = (bf16[64,4096]{1,0:T(8,128)(2,1)S(1)}, bf16[64,4096]{1,0:T(8,128)(2,1)S(1)}, u32[]{:S(2)}, u32[]{:S(2)}) collective-permute-start(bf16[64,4096]{1,0:T(8,128)(2,1)S(1)} %dequantize.5), channel_id=1, source_target_pairs={{0,16},{1,17},{2,18},{3,19},{4,20},{5,21},{6,22},{7,23},{8,24},{9,... | collective-permute-start | bytes 1572872 | tf_op jit(solution)/shard_map/ppermute | solution.py:214
  6.8 0.6 %dequantize.4 = bf16[64,3840]{1,0:T(8,128)(2,1)S(1)} custom-call(s32[128,12288]{1,0:T(8,128)S(1)} %copy-done, f32[96,128]{1,0:T(8,128)S(1)} %bitcast.38), custom_call_target="tpu_custom_call" | custom-call | tf_op jit(solution)/shard_map/dequantize/pallas_call | solution.py:148
  7.4 0.0 copy-start.2
  7.4 0.0 copy-start.3
  7.4 2.5 %collective-permute-start.2 = (bf16[64,3840]{1,0:T(8,128)(2,1)S(1)}, bf16[64,3840]{1,0:T(8,128)(2,1)S(1)}, u32[]{:S(2)}, u32[]{:S(2)}) collective-permute-start(bf16[64,3840]{1,0:T(8,128)(2,1)S(1)} %dequantize.4), channel_id=1, source_target_pairs={{0,96},{1,97},{2,98},{3,99},{4,100},{5,101},{6,102},{7,103},{8,104... | collective-permute-start | bytes 1474568 | tf_op jit(solution)/shard_map/ppermute | solution.py:214
  9.9 1.5 %dequantize.3 = (bf16[64,4352]{1,0:T(8,128)(2,1)S(1)}, bf16[64,4096]{1,0:T(8,128)(2,1)S(1)}, bf16[64,3840]{1,0:T(8,128)(2,1)S(1)}) custom-call(s32[128,12288]{1,0:T(8,128)S(1)} %copy-done, f32[96,128]{1,0:T(8,128)S(1)} %bitcast.39), custom_call_target="tpu_custom_call" | custom-call | tf_op jit(solution)/shard_map/dequantize/pallas_call | solution.py:148
  11.4 0.0 copy-start.4
  11.4 0.0 copy-start.5
  11.4 5.4 %collective-permute-done.refs_2_ = bf16[64,4352]{1,0:T(8,128)(2,1)S(1)} collective-permute-done((bf16[64,4352]{1,0:T(8,128)(2,1)S(1)}, bf16[64,4352]{1,0:T(8,128)(2,1)S(1)}, u32[]{:S(2)}, u32[]{:S(2)}) %collective-permute-start) | collective-permute-done | bytes 557088 | tf_op jit(solution)/shard_map/ppermute | solution.py:214
  16.8 0.1 add_convert_fusion
  16.9 2.2 %collective-permute-start.1 = (bf16[32,4352]{1,0:T(8,128)(2,1)S(1)}, bf16[32,4352]{1,0:T(8,128)(2,1)S(1)}, u32[]{:S(2)}, u32[]{:S(2)}) collective-permute-start(bf16[32,4352]{1,0:T(8,128)(2,1)S(1)} %add_convert_fusion), channel_id=1, source_target_pairs={{0,16},{1,17},{2,18},{3,19},{4,20},{5,21},{6,22},{7,23},{8,24},{9,... | collective-permute-start | bytes 835592 | tf_op jit(solution)/shard_map/ppermute | solution.py:214
  19.2 0.0 collective-permute-done.3.refs_2_
  19.2 0.1 add_convert_fusion.1
  19.2 2.8 %collective-permute-start.6 = (bf16[32,4096]{1,0:T(8,128)(2,1)S(1)}, bf16[32,4096]{1,0:T(8,128)(2,1)S(1)}, u32[]{:S(2)}, u32[]{:S(2)}) collective-permute-start(bf16[32,4096]{1,0:T(8,128)(2,1)S(1)} %add_convert_fusion.1), channel_id=1, source_target_pairs={{0,96},{1,97},{2,98},{3,99},{4,100},{5,101},{6,102},{7,103},{8,104... | collective-permute-start | bytes 786440 | tf_op jit(solution)/shard_map/ppermute | solution.py:214
  22.1 0.0 collective-permute-done.2.refs_6_
  22.1 0.1 add_convert_fusion.2
  22.1 0.3 collective-permute-start.8
  22.4 2.5 %collective-permute-done.1.refs_3_ = bf16[32,4352]{1,0:T(8,128)(2,1)S(1)} collective-permute-done((bf16[32,4352]{1,0:T(8,128)(2,1)S(1)}, bf16[32,4352]{1,0:T(8,128)(2,1)S(1)}, u32[]{:S(2)}, u32[]{:S(2)}) %collective-permute-start.1) | collective-permute-done | bytes 278560 | tf_op jit(solution)/shard_map/ppermute | solution.py:214
  24.9 0.1 add_convert_fusion.3
  25.0 2.8 %collective-permute-start.4 = (bf16[16,4352]{1,0:T(8,128)(2,1)S(1)}, bf16[16,4352]{1,0:T(8,128)(2,1)S(1)}, u32[]{:S(2)}, u32[]{:S(2)}) collective-permute-start(bf16[16,4352]{1,0:T(8,128)(2,1)S(1)} %add_convert_fusion.3), channel_id=1, source_target_pairs={{0,96},{1,97},{2,98},{3,99},{4,100},{5,101},{6,102},{7,103},{8,104... | collective-permute-start | bytes 417800 | tf_op jit(solution)/shard_map/ppermute | solution.py:214
  27.8 0.0 collective-permute-done.6.refs_3_
  27.8 0.1 add_convert_fusion.4
  27.9 0.3 collective-permute-start.7
  28.2 0.3 collective-permute-done.8.refs_7_
  28.5 1.5 %collective-permute-start.9 = (bf16[16,3840]{1,0:T(8,128)(2,1)S(1)}, bf16[16,3840]{1,0:T(8,128)(2,1)S(1)}, u32[]{:S(2)}, u32[]{:S(2)}) collective-permute-start(bf16[16,3840]{1,0:T(8,128)(2,1)S(1)} %add_convert_fusion.5), channel_id=1, source_target_pairs={{0,16},{1,17},{2,18},{3,19},{4,20},{5,21},{6,22},{7,23},{8,24},{9,... | collective-permute-start | bytes 368648 | tf_op jit(solution)/shard_map/ppermute | solution.py:214
  30.1 1.3 %collective-permute-done.4.refs_4_ = bf16[16,4352]{1,0:T(8,128)(2,1)S(1)} collective-permute-done((bf16[16,4352]{1,0:T(8,128)(2,1)S(1)}, bf16[16,4352]{1,0:T(8,128)(2,1)S(1)}, u32[]{:S(2)}, u32[]{:S(2)}) %collective-permute-start.4) | collective-permute-done | bytes 139296 | tf_op jit(solution)/shard_map/ppermute | solution.py:214
  31.3 0.3 finish.2
  31.6 0.1 collective-permute-start.5
  31.8 0.1 broadcast_multiply_fusion.2
  31.8 1.7 %collective-permute-done.9.refs_8_ = bf16[16,3840]{1,0:T(8,128)(2,1)S(1)} collective-permute-done((bf16[16,3840]{1,0:T(8,128)(2,1)S(1)}, bf16[16,3840]{1,0:T(8,128)(2,1)S(1)}, u32[]{:S(2)}, u32[]{:S(2)}) %collective-permute-start.9) | collective-permute-done | bytes 122912 | tf_op jit(solution)/shard_map/ppermute | solution.py:214
  33.5 0.6 %finish.3 = (bf16[4,2,62,128]{3,2,1,0:T(8,128)(2,1)S(1)}, f32[4,2,62,128]{3,2,1,0:T(8,128)S(1)}) custom-call(s32[16,96]{1,0:T(8,128)S(1)} %bitcast.41, bf16[64,4096]{1,0:T(8,128)(2,1)S(1)} %get-tuple-element.20.refs_1_, bf16[64,4096]{1,0:T(8,128)(2,1)S(1)} %collective-permute-done.3.refs_2_, bf16[32,4096]{1,0:T(8,128)(2,1)S(1)} %collective-permute-done.6.refs_3_, ...), custom_call_target="tpu_custom_call" | custom-call | tf_op jit(solution)/shard_map/finish/pallas_call | solution.py:192
  34.1 0.1 collective-permute-start.10
  34.2 0.0 collective-permute-done.5
  34.2 1.3 %collective-permute-done.10 = bf16[4,2,62,128]{3,2,1,0:T(8,128)(2,1)S(1)} collective-permute-done((bf16[4,2,62,128]{3,2,1,0:T(8,128)(2,1)S(1)}, bf16[4,2,62,128]{3,2,1,0:T(8,128)(2,1)S(1)}, u32[]{:S(2)}, u32[]{:S(2)}) %collective-permute-start.10) | collective-permute-done | bytes 127008 | tf_op jit(solution)/shard_map/ppermute | solution.py:214
  35.6 3.3 %collective-permute-start.11 = (bf16[2,96,128]{2,1,0:T(8,128)(2,1)S(1)}, bf16[2,96,128]{2,1,0:T(8,128)(2,1)S(1)}, u32[]{:S(2)}, u32[]{:S(2)}) collective-permute-start(bf16[2,96,128]{2,1,0:T(8,128)(2,1)S(1)} %get-tuple-element.36), channel_id=1, source_target_pairs={{0,4},{1,3},{2,6},{3,1},{4,0},{5,7},{6,2},{7,5},{8,12},{9,11},{10,... | collective-permute-start | bytes 147464 | tf_op jit(solution)/shard_map/ppermute | solution.py:214
  38.9 0.7 %collective-permute-start.12 = (bf16[2,96,128]{2,1,0:T(8,128)(2,1)S(1)}, bf16[2,96,128]{2,1,0:T(8,128)(2,1)S(1)}, u32[]{:S(2)}, u32[]{:S(2)}) collective-permute-start(bf16[2,96,128]{2,1,0:T(8,128)(2,1)S(1)} %get-tuple-element.38), channel_id=1, source_target_pairs={{0,2},{1,7},{2,0},{3,5},{4,6},{5,3},{6,4},{7,1},{8,10},{9,15},{10,... | collective-permute-start | bytes 147464 | tf_op jit(solution)/shard_map/ppermute | solution.py:214
  39.6 0.4 collective-permute-start.13
  40.0 0.1 broadcast_multiply_fusion.1
  40.0 1.7 %collective-permute-done.11 = bf16[2,96,128]{2,1,0:T(8,128)(2,1)S(1)} collective-permute-done((bf16[2,96,128]{2,1,0:T(8,128)(2,1)S(1)}, bf16[2,96,128]{2,1,0:T(8,128)(2,1)S(1)}, u32[]{:S(2)}, u32[]{:S(2)}) %collective-permute-start.11) | collective-permute-done | bytes 49184 | tf_op jit(solution)/shard_map/ppermute | solution.py:214
  41.7 1.3 %collective-permute-done.12 = bf16[2,96,128]{2,1,0:T(8,128)(2,1)S(1)} collective-permute-done((bf16[2,96,128]{2,1,0:T(8,128)(2,1)S(1)}, bf16[2,96,128]{2,1,0:T(8,128)(2,1)S(1)}, u32[]{:S(2)}, u32[]{:S(2)}) %collective-permute-start.12) | collective-permute-done | bytes 49184 | tf_op jit(solution)/shard_map/ppermute | solution.py:214
  43.0 1.9 %collective-permute-done.13 = bf16[2,96,128]{2,1,0:T(8,128)(2,1)S(1)} collective-permute-done((bf16[2,96,128]{2,1,0:T(8,128)(2,1)S(1)}, bf16[2,96,128]{2,1,0:T(8,128)(2,1)S(1)}, u32[]{:S(2)}, u32[]{:S(2)}) %collective-permute-start.13) | collective-permute-done | bytes 49184 | tf_op jit(solution)/shard_map/ppermute | solution.py:214
  44.9 3.7 %collective-permute-start.14 = (bf16[96,128]{1,0:T(8,128)(2,1)S(1)}, bf16[96,128]{1,0:T(8,128)(2,1)S(1)}, u32[]{:S(2)}, u32[]{:S(2)}) collective-permute-start(bf16[96,128]{1,0:T(8,128)(2,1)S(1)} %fusion.8), channel_id=1, source_target_pairs={{0,8},{1,9},{2,10},{3,11},{4,12},{5,13},{6,14},{7,15},{8,0},{9,1},... | collective-permute-start | bytes 73736 | tf_op jit(solution)/shard_map/ppermute | solution.py:214
  48.6 0.1 broadcast_multiply_fusion
  49.4 1.0 %collective-permute-done.14 = bf16[96,128]{1,0:T(8,128)(2,1)S(1)} collective-permute-done((bf16[96,128]{1,0:T(8,128)(2,1)S(1)}, bf16[96,128]{1,0:T(8,128)(2,1)S(1)}, u32[]{:S(2)}, u32[]{:S(2)}) %collective-permute-start.14) | collective-permute-done | bytes 24608 | tf_op jit(solution)/shard_map/ppermute | solution.py:214
  50.4 0.7 %divide_add_fusion = (f32[96,128]{1,0:T(8,128)}, f32[96,128]{1,0:T(8,128)}, f32[96,128]{1,0:T(8,128)}) fusion(f32[96,128]{1,0:T(8,128)S(1)} %bitcast.44, f32[]{:T(128)} %bitcast.11, f32[]{:T(128)} %bitcast.9, f32[96,128]{1,0:T(8,128)S(1)} %bitcast.43, bf16[96,128]{1,0:T(8,128)(2,1)S(1)} %collective-permute-done.14, f32[2,96,128]{2,1,0:T(8,128)S(1)} %fusion.5, ...), kind=kLoop, calls=%fused_computation.25 | loop fusion | flops 147456 | bytes 368648 | tf_op jit(solution)/shard_map/add | solution.py:209
  (16 shorter events, 0.2 us)
Async XLA Ops:
  0.6 3.6 %copy-start.1 = (f32[128,96]{0,1:T(8,128)S(1)}, f32[128,96]{0,1:T(8,128)}, u32[]{:S(2)}) copy-start(f32[128,96]{0,1:T(8,128)} %param.8) | copy-start | bytes 147460
  0.6 3.6 %copy-start = (s32[128,12288]{1,0:T(8,128)S(1)}, s32[128,12288]{1,0:T(8,128)}, u32[]{:S(2)}) copy-start(s32[128,12288]{1,0:T(8,128)} %refs_0_.7) | copy-start | bytes 18874372
  2.5 14.3 %collective-permute-start = (bf16[64,4352]{1,0:T(8,128)(2,1)S(1)}, bf16[64,4352]{1,0:T(8,128)(2,1)S(1)}, u32[]{:S(2)}, u32[]{:S(2)}) collective-permute-start(bf16[64,4352]{1,0:T(8,128)(2,1)S(1)} %first_rows.1), channel_id=1, source_target_pairs={{0,32},{1,33},{2,34},{3,35},{4,36},{5,37},{6,38},{7,39},{8,40},{9,... | collective-permute-start | bytes 1671176 | tf_op jit(solution)/shard_map/ppermute | solution.py:214
  4.8 14.3 %collective-permute-start.3 = (bf16[64,4096]{1,0:T(8,128)(2,1)S(1)}, bf16[64,4096]{1,0:T(8,128)(2,1)S(1)}, u32[]{:S(2)}, u32[]{:S(2)}) collective-permute-start(bf16[64,4096]{1,0:T(8,128)(2,1)S(1)} %dequantize.5), channel_id=1, source_target_pairs={{0,16},{1,17},{2,18},{3,19},{4,20},{5,21},{6,22},{7,23},{8,24},{9,... | collective-permute-start | bytes 1572872 | tf_op jit(solution)/shard_map/ppermute | solution.py:214
  7.4 23.9 %copy-start.2 = (s32[1,1,16,96]{3,2,1,0:T(8,128)S(1)}, s32[1,1,16,96]{3,2,1,0:T(8,128)}, u32[]{:S(2)}) copy-start(s32[1,1,16,96]{3,2,1,0:T(8,128)} %param.9) | copy-start | bytes 18436
  7.4 24.3 %copy-start.3 = (f32[1,12288]{1,0:T(1,128)S(1)}, f32[1,12288]{1,0:T(1,128)}, u32[]{:S(2)}) copy-start(f32[1,12288]{1,0:T(1,128)} %param.11) | copy-start | bytes 147460
  7.4 14.6 %collective-permute-start.2 = (bf16[64,3840]{1,0:T(8,128)(2,1)S(1)}, bf16[64,3840]{1,0:T(8,128)(2,1)S(1)}, u32[]{:S(2)}, u32[]{:S(2)}) collective-permute-start(bf16[64,3840]{1,0:T(8,128)(2,1)S(1)} %dequantize.4), channel_id=1, source_target_pairs={{0,96},{1,97},{2,98},{3,99},{4,100},{5,101},{6,102},{7,103},{8,104... | collective-permute-start | bytes 1474568 | tf_op jit(solution)/shard_map/ppermute | solution.py:214
  11.4 28.6 %copy-start.4 = (f32[1,12288]{1,0:T(1,128)S(1)}, f32[1,12288]{1,0:T(1,128)}, u32[]{:S(2)}) copy-start(f32[1,12288]{1,0:T(1,128)} %param.12) | copy-start | bytes 147460
  11.4 37.2 %copy-start.5 = (f32[1,12288]{1,0:T(1,128)S(1)}, f32[1,12288]{1,0:T(1,128)}, u32[]{:S(2)}) copy-start(f32[1,12288]{1,0:T(1,128)} %param.10) | copy-start | bytes 147460
  16.9 8.0 %collective-permute-start.1 = (bf16[32,4352]{1,0:T(8,128)(2,1)S(1)}, bf16[32,4352]{1,0:T(8,128)(2,1)S(1)}, u32[]{:S(2)}, u32[]{:S(2)}) collective-permute-start(bf16[32,4352]{1,0:T(8,128)(2,1)S(1)} %add_convert_fusion), channel_id=1, source_target_pairs={{0,16},{1,17},{2,18},{3,19},{4,20},{5,21},{6,22},{7,23},{8,24},{9,... | collective-permute-start | bytes 835592 | tf_op jit(solution)/shard_map/ppermute | solution.py:214
  19.2 8.6 %collective-permute-start.6 = (bf16[32,4096]{1,0:T(8,128)(2,1)S(1)}, bf16[32,4096]{1,0:T(8,128)(2,1)S(1)}, u32[]{:S(2)}, u32[]{:S(2)}) collective-permute-start(bf16[32,4096]{1,0:T(8,128)(2,1)S(1)} %add_convert_fusion.1), channel_id=1, source_target_pairs={{0,96},{1,97},{2,98},{3,99},{4,100},{5,101},{6,102},{7,103},{8,104... | collective-permute-start | bytes 786440 | tf_op jit(solution)/shard_map/ppermute | solution.py:214
  22.1 6.3 %collective-permute-start.8 = (bf16[32,3840]{1,0:T(8,128)(2,1)S(1)}, bf16[32,3840]{1,0:T(8,128)(2,1)S(1)}, u32[]{:S(2)}, u32[]{:S(2)}) collective-permute-start(bf16[32,3840]{1,0:T(8,128)(2,1)S(1)} %add_convert_fusion.2), channel_id=1, source_target_pairs={{0,32},{1,33},{2,34},{3,35},{4,36},{5,37},{6,38},{7,39},{8,40},{9,... | collective-permute-start | bytes 737288 | tf_op jit(solution)/shard_map/ppermute | solution.py:214
  25.0 6.3 %collective-permute-start.4 = (bf16[16,4352]{1,0:T(8,128)(2,1)S(1)}, bf16[16,4352]{1,0:T(8,128)(2,1)S(1)}, u32[]{:S(2)}, u32[]{:S(2)}) collective-permute-start(bf16[16,4352]{1,0:T(8,128)(2,1)S(1)} %add_convert_fusion.3), channel_id=1, source_target_pairs={{0,96},{1,97},{2,98},{3,99},{4,100},{5,101},{6,102},{7,103},{8,104... | collective-permute-start | bytes 417800 | tf_op jit(solution)/shard_map/ppermute | solution.py:214
  27.9 5.6 %collective-permute-start.7 = (bf16[16,4096]{1,0:T(8,128)(2,1)S(1)}, bf16[16,4096]{1,0:T(8,128)(2,1)S(1)}, u32[]{:S(2)}, u32[]{:S(2)}) collective-permute-start(bf16[16,4096]{1,0:T(8,128)(2,1)S(1)} %add_convert_fusion.4), channel_id=1, source_target_pairs={{0,32},{1,33},{2,34},{3,35},{4,36},{5,37},{6,38},{7,39},{8,40},{9,... | collective-permute-start | bytes 393224 | tf_op jit(solution)/shard_map/ppermute | solution.py:214
  28.5 5.0 %collective-permute-start.9 = (bf16[16,3840]{1,0:T(8,128)(2,1)S(1)}, bf16[16,3840]{1,0:T(8,128)(2,1)S(1)}, u32[]{:S(2)}, u32[]{:S(2)}) collective-permute-start(bf16[16,3840]{1,0:T(8,128)(2,1)S(1)} %add_convert_fusion.5), channel_id=1, source_target_pairs={{0,16},{1,17},{2,18},{3,19},{4,20},{5,21},{6,22},{7,23},{8,24},{9,... | collective-permute-start | bytes 368648 | tf_op jit(solution)/shard_map/ppermute | solution.py:214
  31.6 2.6 %collective-permute-start.5 = (bf16[4,2,34,128]{3,2,1,0:T(8,128)(2,1)S(1)}, bf16[4,2,34,128]{3,2,1,0:T(8,128)(2,1)S(1)}, u32[]{:S(2)}, u32[]{:S(2)}) collective-permute-start(bf16[4,2,34,128]{3,2,1,0:T(8,128)(2,1)S(1)} %get-tuple-element.26), channel_id=1, source_target_pairs={{0,1},{1,0},{2,3},{3,2},{4,5},{5,4},{6,7},{7,6},{8,9},{9,8},{10,11... | collective-permute-start | bytes 208904 | tf_op jit(solution)/shard_map/ppermute | solution.py:214
  34.1 1.4 %collective-permute-start.10 = (bf16[4,2,62,128]{3,2,1,0:T(8,128)(2,1)S(1)}, bf16[4,2,62,128]{3,2,1,0:T(8,128)(2,1)S(1)}, u32[]{:S(2)}, u32[]{:S(2)}) collective-permute-start(bf16[4,2,62,128]{3,2,1,0:T(8,128)(2,1)S(1)} %get-tuple-element.32), channel_id=1, source_target_pairs={{0,1},{1,0},{2,3},{3,2},{4,5},{5,4},{6,7},{7,6},{8,9},{9,8},{10,11... | collective-permute-start | bytes 380936 | tf_op jit(solution)/shard_map/ppermute | solution.py:214
  35.6 6.1 %collective-permute-start.11 = (bf16[2,96,128]{2,1,0:T(8,128)(2,1)S(1)}, bf16[2,96,128]{2,1,0:T(8,128)(2,1)S(1)}, u32[]{:S(2)}, u32[]{:S(2)}) collective-permute-start(bf16[2,96,128]{2,1,0:T(8,128)(2,1)S(1)} %get-tuple-element.36), channel_id=1, source_target_pairs={{0,4},{1,3},{2,6},{3,1},{4,0},{5,7},{6,2},{7,5},{8,12},{9,11},{10,... | collective-permute-start | bytes 147464 | tf_op jit(solution)/shard_map/ppermute | solution.py:214
  38.9 4.1 %collective-permute-start.12 = (bf16[2,96,128]{2,1,0:T(8,128)(2,1)S(1)}, bf16[2,96,128]{2,1,0:T(8,128)(2,1)S(1)}, u32[]{:S(2)}, u32[]{:S(2)}) collective-permute-start(bf16[2,96,128]{2,1,0:T(8,128)(2,1)S(1)} %get-tuple-element.38), channel_id=1, source_target_pairs={{0,2},{1,7},{2,0},{3,5},{4,6},{5,3},{6,4},{7,1},{8,10},{9,15},{10,... | collective-permute-start | bytes 147464 | tf_op jit(solution)/shard_map/ppermute | solution.py:214
  39.6 5.3 %collective-permute-start.13 = (bf16[2,96,128]{2,1,0:T(8,128)(2,1)S(1)}, bf16[2,96,128]{2,1,0:T(8,128)(2,1)S(1)}, u32[]{:S(2)}, u32[]{:S(2)}) collective-permute-start(bf16[2,96,128]{2,1,0:T(8,128)(2,1)S(1)} %get-tuple-element.37), channel_id=1, source_target_pairs={{0,6},{1,5},{2,4},{3,7},{4,2},{5,1},{6,0},{7,3},{8,14},{9,13},{10,... | collective-permute-start | bytes 147464 | tf_op jit(solution)/shard_map/ppermute | solution.py:214
  44.9 5.5 %collective-permute-start.14 = (bf16[96,128]{1,0:T(8,128)(2,1)S(1)}, bf16[96,128]{1,0:T(8,128)(2,1)S(1)}, u32[]{:S(2)}, u32[]{:S(2)}) collective-permute-start(bf16[96,128]{1,0:T(8,128)(2,1)S(1)} %fusion.8), channel_id=1, source_target_pairs={{0,8},{1,9},{2,10},{3,11},{4,12},{5,13},{6,14},{7,15},{8,0},{9,1},... | collective-permute-start | bytes 73736 | tf_op jit(solution)/shard_map/ppermute | solution.py:214

commit v9 on v8

--- a/solution.py
+++ b/solution.py
@@ -17,12 +17,13 @@
 COLUMNS = BLOCKS * LANES
 TILE = 16
 PIECES = (
-    (0, 34, "PZQ"),
-    (34, 32, "ZQP"),
-    (66, 30, "QPZ"),
+    (0, 28, "PZQ"),
+    (28, 26, "ZQP"),
+    (54, 24, "QPZ"),
+    (78, 18, "PQZ"),
 )
-SUMS = ((0, 1), (1, 1), (2, 1), (0, 2), (1, 2), (2, 2))
-EARLY = 1
+SUMS = ((0, 1), (1, 1), (2, 1), (3, 1), (0, 2), (1, 2), (2, 2), (3, 2))
+EARLY = 2
 FIRST = 0
 AXES = ("node", "wide")
 VMEM_LIMIT = 32 * 1024 * 1024

time: 51.7 us -> 52 us (level)
  starting transfers between devices: 24.4 us -> 26.5 us
  waiting for transfers between devices: 18.3 us -> 16.9 us
    ppermute x15 -> x18, starting transfers between devices: 24.4 us -> 26.5 us  [send(): return lax.ppermute(array.astype(jnp.bfloat16), axes, route)]
    ppermute x15 -> x18, waiting for transfers between devices: 18.3 us -> 16.9 us  [send(): return lax.ppermute(array.astype(jnp.bfloat16), axes, route)]
    pallas_call x3 -> x4, Pallas kernels: 2.67 us -> 2.93 us  [dequantize(): pl.pallas_call(lambda *refs: dequantize_kernel(parts, *refs), out_shape=[...]
  transfers between devices with their start and end apart: 15 -> 18, of which waited for: 10 -> 11; matrix products, arithmetic and copies ran while one was open for 1% -> 1% of each run, Pallas kernels for 7% -> 6%
where the time goes in v9:
time: 52 us; the launch traced here: 51.8 us
  starting transfers between devices  26.5 us (51%)
  waiting for transfers between devices  16.9 us (32%)
  Pallas kernels  5.49 us (11%)
  between operations  1.55 us (3%)
  other arithmetic  1.31 us (3%)
    ppermute x18, starting transfers between devices, send(): return lax.ppermute(array.astype(jnp.bfloat16), axes, route)  26.5 us
    ppermute x18, waiting for transfers between devices, send(): return lax.ppermute(array.astype(jnp.bfloat16), axes, route)  16.9 us
    pallas_call x4, Pallas kernels, dequantize(): pl.pallas_call(lambda *refs: dequantize_kernel(parts, *refs), out_shape=[...  2.93 us
    pallas_call x1, Pallas kernels, first_rows(): pl.pallas_call(lambda *refs: first_kernel(piece, *refs), out_shape=jax.Sh...  1.79 us
  transfers between devices with their start and end apart: 18, of which 11 were waited for; matrix products, arithmetic and copies ran while one was open for 1% of the time, Pallas kernels for 6%

profile of v9, /device:TPU:0, one launch (start us, length us, event | category | flops | bytes accessed | tf_op | source)
XLA Modules:
  0.0 51.8 jit_solution(8293028135498020037)
XLA Ops:
  0.6 1.8 %first_rows.1 = bf16[64,3584]{1,0:T(8,128)(2,1)S(1)} custom-call(s32[128,12288]{1,0:T(8,128)} %refs_0_.9, f32[96,128]{1,0:T(8,128)} %bitcast.36), custom_call_target="tpu_custom_call" | custom-call | tf_op jit(solution)/shard_map/first_rows/pallas_call | solution.py:114
  2.4 1.7 %collective-permute-start = (bf16[64,3584]{1,0:T(8,128)(2,1)S(1)}, bf16[64,3584]{1,0:T(8,128)(2,1)S(1)}, u32[]{:S(2)}, u32[]{:S(2)}) collective-permute-start(bf16[64,3584]{1,0:T(8,128)(2,1)S(1)} %first_rows.1), channel_id=1, source_target_pairs={{0,32},{1,33},{2,34},{3,35},{4,36},{5,37},{6,38},{7,39},{8,40},{9,... | collective-permute-start | bytes 1376264 | tf_op jit(solution)/shard_map/ppermute | solution.py:215
  4.1 0.5 %dequantize.7 = bf16[64,3328]{1,0:T(8,128)(2,1)S(1)} custom-call(s32[128,12288]{1,0:T(8,128)S(1)} %copy-done, f32[96,128]{1,0:T(8,128)S(1)} %bitcast.37), custom_call_target="tpu_custom_call" | custom-call | tf_op jit(solution)/shard_map/dequantize/pallas_call | solution.py:149
  4.6 2.0 %collective-permute-start.4 = (bf16[64,3328]{1,0:T(8,128)(2,1)S(1)}, bf16[64,3328]{1,0:T(8,128)(2,1)S(1)}, u32[]{:S(2)}, u32[]{:S(2)}) collective-permute-start(bf16[64,3328]{1,0:T(8,128)(2,1)S(1)} %dequantize.7), channel_id=1, source_target_pairs={{0,16},{1,17},{2,18},{3,19},{4,20},{5,21},{6,22},{7,23},{8,24},{9,... | collective-permute-start | bytes 1277960 | tf_op jit(solution)/shard_map/ppermute | solution.py:215
  6.6 0.5 dequantize.6
  7.1 2.7 %collective-permute-start.3 = (bf16[64,3072]{1,0:T(8,128)(2,1)S(1)}, bf16[64,3072]{1,0:T(8,128)(2,1)S(1)}, u32[]{:S(2)}, u32[]{:S(2)}) collective-permute-start(bf16[64,3072]{1,0:T(8,128)(2,1)S(1)} %dequantize.6), channel_id=1, source_target_pairs={{0,96},{1,97},{2,98},{3,99},{4,100},{5,101},{6,102},{7,103},{8,104... | collective-permute-start | bytes 1179656 | tf_op jit(solution)/shard_map/ppermute | solution.py:215
  9.8 0.4 dequantize.5
  10.2 0.0 copy-start.2
  10.2 0.0 copy-start.3
  10.3 0.3 collective-permute-start.2
  10.6 1.5 %dequantize.4 = (bf16[64,3584]{1,0:T(8,128)(2,1)S(1)}, bf16[64,3328]{1,0:T(8,128)(2,1)S(1)}, bf16[64,3072]{1,0:T(8,128)(2,1)S(1)}, bf16[64,2304]{1,0:T(8,128)(2,1)S(1)}) custom-call(s32[128,12288]{1,0:T(8,128)S(1)} %copy-done, f32[96,128]{1,0:T(8,128)S(1)} %bitcast.40), custom_call_target="tpu_custom_call" | custom-call | tf_op jit(solution)/shard_map/dequantize/pallas_call | solution.py:149
  12.0 0.0 copy-start.4
  12.1 0.0 copy-start.5
  12.1 3.9 %collective-permute-done.refs_2_ = bf16[64,3584]{1,0:T(8,128)(2,1)S(1)} collective-permute-done((bf16[64,3584]{1,0:T(8,128)(2,1)S(1)}, bf16[64,3584]{1,0:T(8,128)(2,1)S(1)}, u32[]{:S(2)}, u32[]{:S(2)}) %collective-permute-start) | collective-permute-done | bytes 458784 | tf_op jit(solution)/shard_map/ppermute | solution.py:215
  16.0 0.1 add_convert_fusion
  16.0 2.1 %collective-permute-start.1 = (bf16[32,3584]{1,0:T(8,128)(2,1)S(1)}, bf16[32,3584]{1,0:T(8,128)(2,1)S(1)}, u32[]{:S(2)}, u32[]{:S(2)}) collective-permute-start(bf16[32,3584]{1,0:T(8,128)(2,1)S(1)} %add_convert_fusion), channel_id=1, source_target_pairs={{0,16},{1,17},{2,18},{3,19},{4,20},{5,21},{6,22},{7,23},{8,24},{9,... | collective-permute-start | bytes 688136 | tf_op jit(solution)/shard_map/ppermute | solution.py:215
  18.1 0.0 collective-permute-done.4.refs_6_
  18.1 0.1 add_convert_fusion.1
  18.1 2.8 %collective-permute-start.6 = (bf16[32,3328]{1,0:T(8,128)(2,1)S(1)}, bf16[32,3328]{1,0:T(8,128)(2,1)S(1)}, u32[]{:S(2)}, u32[]{:S(2)}) collective-permute-start(bf16[32,3328]{1,0:T(8,128)(2,1)S(1)} %add_convert_fusion.1), channel_id=1, source_target_pairs={{0,96},{1,97},{2,98},{3,99},{4,100},{5,101},{6,102},{7,103},{8,104... | collective-permute-start | bytes 638984 | tf_op jit(solution)/shard_map/ppermute | solution.py:215
  21.0 0.3 collective-permute-start.9
  21.3 0.0 collective-permute-done.2.refs_6_
  21.4 3.6 %collective-permute-start.11 = (bf16[32,2304]{1,0:T(8,128)(2,1)S(1)}, bf16[32,2304]{1,0:T(8,128)(2,1)S(1)}, u32[]{:S(2)}, u32[]{:S(2)}) collective-permute-start(bf16[32,2304]{1,0:T(8,128)(2,1)S(1)} %add_convert_fusion.3), channel_id=1, source_target_pairs={{0,96},{1,97},{2,98},{3,99},{4,100},{5,101},{6,102},{7,103},{8,104... | collective-permute-start | bytes 442376 | tf_op jit(solution)/shard_map/ppermute | solution.py:215
  25.0 0.1 collective-permute-start.5
  25.1 1.6 %collective-permute-done.6.refs_7_ = bf16[32,3328]{1,0:T(8,128)(2,1)S(1)} collective-permute-done((bf16[32,3328]{1,0:T(8,128)(2,1)S(1)}, bf16[32,3328]{1,0:T(8,128)(2,1)S(1)}, u32[]{:S(2)}, u32[]{:S(2)}) %collective-permute-start.6) | collective-permute-done | bytes 213024 | tf_op jit(solution)/shard_map/ppermute | solution.py:215
  26.7 0.1 collective-permute-start.7
  26.9 1.1 %collective-permute-done.9.refs_3_ = bf16[32,3072]{1,0:T(8,128)(2,1)S(1)} collective-permute-done((bf16[32,3072]{1,0:T(8,128)(2,1)S(1)}, bf16[32,3072]{1,0:T(8,128)(2,1)S(1)}, u32[]{:S(2)}, u32[]{:S(2)}) %collective-permute-start.9) | collective-permute-done | bytes 196640 | tf_op jit(solution)/shard_map/ppermute | solution.py:215
  28.0 0.3 collective-permute-start.10
  28.3 1.4 %collective-permute-done.11.refs_7_ = bf16[32,2304]{1,0:T(8,128)(2,1)S(1)} collective-permute-done((bf16[32,2304]{1,0:T(8,128)(2,1)S(1)}, bf16[32,2304]{1,0:T(8,128)(2,1)S(1)}, u32[]{:S(2)}, u32[]{:S(2)}) %collective-permute-start.11) | collective-permute-done | bytes 147488 | tf_op jit(solution)/shard_map/ppermute | solution.py:215
  29.7 1.8 %collective-permute-start.12 = (bf16[16,2304]{1,0:T(8,128)(2,1)S(1)}, bf16[16,2304]{1,0:T(8,128)(2,1)S(1)}, u32[]{:S(2)}, u32[]{:S(2)}) collective-permute-start(bf16[16,2304]{1,0:T(8,128)(2,1)S(1)} %add_convert_fusion.7), channel_id=1, source_target_pairs={{0,16},{1,17},{2,18},{3,19},{4,20},{5,21},{6,22},{7,23},{8,24},{9,... | collective-permute-start | bytes 221192 | tf_op jit(solution)/shard_map/ppermute | solution.py:215
  31.5 0.4 finish.2
  32.0 2.2 %collective-permute-done.12.refs_8_ = bf16[16,2304]{1,0:T(8,128)(2,1)S(1)} collective-permute-done((bf16[16,2304]{1,0:T(8,128)(2,1)S(1)}, bf16[16,2304]{1,0:T(8,128)(2,1)S(1)}, u32[]{:S(2)}, u32[]{:S(2)}) %collective-permute-start.12) | collective-permute-done | bytes 73760 | tf_op jit(solution)/shard_map/ppermute | solution.py:215
  34.1 0.3 finish.3
  34.5 0.1 collective-permute-start.13
  34.6 0.1 broadcast_multiply_fusion.2
  34.7 0.6 %collective-permute-start.8 = (bf16[4,2,54,128]{3,2,1,0:T(8,128)(2,1)S(1)}, bf16[4,2,54,128]{3,2,1,0:T(8,128)(2,1)S(1)}, u32[]{:S(2)}, u32[]{:S(2)}) collective-permute-start(bf16[4,2,54,128]{3,2,1,0:T(8,128)(2,1)S(1)} %get-tuple-element.32), channel_id=1, source_target_pairs={{0,1},{1,0},{2,3},{3,2},{4,5},{5,4},{6,7},{7,6},{8,9},{9,8},{10,11... | collective-permute-start | bytes 331784 | tf_op jit(solution)/shard_map/ppermute | solution.py:215
  35.2 0.7 %collective-permute-done.13 = bf16[4,2,42,128]{3,2,1,0:T(8,128)(2,1)S(1)} collective-permute-done((bf16[4,2,42,128]{3,2,1,0:T(8,128)(2,1)S(1)}, bf16[4,2,42,128]{3,2,1,0:T(8,128)(2,1)S(1)}, u32[]{:S(2)}, u32[]{:S(2)}) %collective-permute-start.13) | collective-permute-done | bytes 86048 | tf_op jit(solution)/shard_map/ppermute | solution.py:215
  35.9 0.3 collective-permute-done.8
  36.3 3.3 %collective-permute-start.14 = (bf16[2,96,128]{2,1,0:T(8,128)(2,1)S(1)}, bf16[2,96,128]{2,1,0:T(8,128)(2,1)S(1)}, u32[]{:S(2)}, u32[]{:S(2)}) collective-permute-start(bf16[2,96,128]{2,1,0:T(8,128)(2,1)S(1)} %get-tuple-element.42), channel_id=1, source_target_pairs={{0,4},{1,3},{2,6},{3,1},{4,0},{5,7},{6,2},{7,5},{8,12},{9,11},{10,... | collective-permute-start | bytes 147464 | tf_op jit(solution)/shard_map/ppermute | solution.py:215
  39.6 0.7 %collective-permute-start.15 = (bf16[2,96,128]{2,1,0:T(8,128)(2,1)S(1)}, bf16[2,96,128]{2,1,0:T(8,128)(2,1)S(1)}, u32[]{:S(2)}, u32[]{:S(2)}) collective-permute-start(bf16[2,96,128]{2,1,0:T(8,128)(2,1)S(1)} %get-tuple-element.44), channel_id=1, source_target_pairs={{0,2},{1,7},{2,0},{3,5},{4,6},{5,3},{6,4},{7,1},{8,10},{9,15},{10,... | collective-permute-start | bytes 147464 | tf_op jit(solution)/shard_map/ppermute | solution.py:215
  40.2 0.4 collective-permute-start.16
  40.6 0.1 broadcast_multiply_fusion.1
  40.7 1.5 %collective-permute-done.14 = bf16[2,96,128]{2,1,0:T(8,128)(2,1)S(1)} collective-permute-done((bf16[2,96,128]{2,1,0:T(8,128)(2,1)S(1)}, bf16[2,96,128]{2,1,0:T(8,128)(2,1)S(1)}, u32[]{:S(2)}, u32[]{:S(2)}) %collective-permute-start.14) | collective-permute-done | bytes 49184 | tf_op jit(solution)/shard_map/ppermute | solution.py:215
  42.1 1.5 %collective-permute-done.15 = bf16[2,96,128]{2,1,0:T(8,128)(2,1)S(1)} collective-permute-done((bf16[2,96,128]{2,1,0:T(8,128)(2,1)S(1)}, bf16[2,96,128]{2,1,0:T(8,128)(2,1)S(1)}, u32[]{:S(2)}, u32[]{:S(2)}) %collective-permute-start.15) | collective-permute-done | bytes 49184 | tf_op jit(solution)/shard_map/ppermute | solution.py:215
  43.7 1.9 %collective-permute-done.16 = bf16[2,96,128]{2,1,0:T(8,128)(2,1)S(1)} collective-permute-done((bf16[2,96,128]{2,1,0:T(8,128)(2,1)S(1)}, bf16[2,96,128]{2,1,0:T(8,128)(2,1)S(1)}, u32[]{:S(2)}, u32[]{:S(2)}) %collective-permute-start.16) | collective-permute-done | bytes 49184 | tf_op jit(solution)/shard_map/ppermute | solution.py:215
  45.6 3.8 %collective-permute-start.17 = (bf16[96,128]{1,0:T(8,128)(2,1)S(1)}, bf16[96,128]{1,0:T(8,128)(2,1)S(1)}, u32[]{:S(2)}, u32[]{:S(2)}) collective-permute-start(bf16[96,128]{1,0:T(8,128)(2,1)S(1)} %fusion.8), channel_id=1, source_target_pairs={{0,8},{1,9},{2,10},{3,11},{4,12},{5,13},{6,14},{7,15},{8,0},{9,1},... | collective-permute-start | bytes 73736 | tf_op jit(solution)/shard_map/ppermute | solution.py:215
  49.4 0.1 broadcast_multiply_fusion
  50.2 1.0 %collective-permute-done.17 = bf16[96,128]{1,0:T(8,128)(2,1)S(1)} collective-permute-done((bf16[96,128]{1,0:T(8,128)(2,1)S(1)}, bf16[96,128]{1,0:T(8,128)(2,1)S(1)}, u32[]{:S(2)}, u32[]{:S(2)}) %collective-permute-start.17) | collective-permute-done | bytes 24608 | tf_op jit(solution)/shard_map/ppermute | solution.py:215
  51.2 0.7 %divide_add_fusion = (f32[96,128]{1,0:T(8,128)}, f32[96,128]{1,0:T(8,128)}, f32[96,128]{1,0:T(8,128)}) fusion(f32[96,128]{1,0:T(8,128)S(1)} %bitcast.45, f32[]{:T(128)} %bitcast.11, f32[]{:T(128)} %bitcast.9, f32[96,128]{1,0:T(8,128)S(1)} %bitcast.44, bf16[96,128]{1,0:T(8,128)(2,1)S(1)} %collective-permute-done.17, f32[2,96,128]{2,1,0:T(8,128)S(1)} %fusion.5, ...), kind=kLoop, calls=%fused_computation.27 | loop fusion | flops 147456 | bytes 368648 | tf_op jit(solution)/shard_map/add | solution.py:210
  (25 shorter events, 0.4 us)
Async XLA Ops:
  0.6 3.5 %copy-start.1 = (f32[128,96]{0,1:T(8,128)S(1)}, f32[128,96]{0,1:T(8,128)}, u32[]{:S(2)}) copy-start(f32[128,96]{0,1:T(8,128)} %param.8) | copy-start | bytes 147460
  0.6 3.5 %copy-start = (s32[128,12288]{1,0:T(8,128)S(1)}, s32[128,12288]{1,0:T(8,128)}, u32[]{:S(2)}) copy-start(s32[128,12288]{1,0:T(8,128)} %refs_0_.9) | copy-start | bytes 18874372
  2.4 13.5 %collective-permute-start = (bf16[64,3584]{1,0:T(8,128)(2,1)S(1)}, bf16[64,3584]{1,0:T(8,128)(2,1)S(1)}, u32[]{:S(2)}, u32[]{:S(2)}) collective-permute-start(bf16[64,3584]{1,0:T(8,128)(2,1)S(1)} %first_rows.1), channel_id=1, source_target_pairs={{0,32},{1,33},{2,34},{3,35},{4,36},{5,37},{6,38},{7,39},{8,40},{9,... | collective-permute-start | bytes 1376264 | tf_op jit(solution)/shard_map/ppermute | solution.py:215
  4.6 13.4 %collective-permute-start.4 = (bf16[64,3328]{1,0:T(8,128)(2,1)S(1)}, bf16[64,3328]{1,0:T(8,128)(2,1)S(1)}, u32[]{:S(2)}, u32[]{:S(2)}) collective-permute-start(bf16[64,3328]{1,0:T(8,128)(2,1)S(1)} %dequantize.7), channel_id=1, source_target_pairs={{0,16},{1,17},{2,18},{3,19},{4,20},{5,21},{6,22},{7,23},{8,24},{9,... | collective-permute-start | bytes 1277960 | tf_op jit(solution)/shard_map/ppermute | solution.py:215
  7.1 13.8 %collective-permute-start.3 = (bf16[64,3072]{1,0:T(8,128)(2,1)S(1)}, bf16[64,3072]{1,0:T(8,128)(2,1)S(1)}, u32[]{:S(2)}, u32[]{:S(2)}) collective-permute-start(bf16[64,3072]{1,0:T(8,128)(2,1)S(1)} %dequantize.6), channel_id=1, source_target_pairs={{0,96},{1,97},{2,98},{3,99},{4,100},{5,101},{6,102},{7,103},{8,104... | collective-permute-start | bytes 1179656 | tf_op jit(solution)/shard_map/ppermute | solution.py:215
  10.2 21.3 %copy-start.2 = (s32[1,1,16,96]{3,2,1,0:T(8,128)S(1)}, s32[1,1,16,96]{3,2,1,0:T(8,128)}, u32[]{:S(2)}) copy-start(s32[1,1,16,96]{3,2,1,0:T(8,128)} %param.9) | copy-start | bytes 18436
  10.2 24.3 %copy-start.3 = (f32[1,12288]{1,0:T(1,128)S(1)}, f32[1,12288]{1,0:T(1,128)}, u32[]{:S(2)}) copy-start(f32[1,12288]{1,0:T(1,128)} %param.11) | copy-start | bytes 147460
  10.3 11.1 %collective-permute-start.2 = (bf16[64,2304]{1,0:T(8,128)(2,1)S(1)}, bf16[64,2304]{1,0:T(8,128)(2,1)S(1)}, u32[]{:S(2)}, u32[]{:S(2)}) collective-permute-start(bf16[64,2304]{1,0:T(8,128)(2,1)S(1)} %dequantize.5), channel_id=1, source_target_pairs={{0,32},{1,33},{2,34},{3,35},{4,36},{5,37},{6,38},{7,39},{8,40},{9,... | collective-permute-start | bytes 884744 | tf_op jit(solution)/shard_map/ppermute | solution.py:215
  12.0 28.6 %copy-start.4 = (f32[1,12288]{1,0:T(1,128)S(1)}, f32[1,12288]{1,0:T(1,128)}, u32[]{:S(2)}) copy-start(f32[1,12288]{1,0:T(1,128)} %param.12) | copy-start | bytes 147460
  12.1 37.3 %copy-start.5 = (f32[1,12288]{1,0:T(1,128)S(1)}, f32[1,12288]{1,0:T(1,128)}, u32[]{:S(2)}) copy-start(f32[1,12288]{1,0:T(1,128)} %param.10) | copy-start | bytes 147460
  16.0 9.0 %collective-permute-start.1 = (bf16[32,3584]{1,0:T(8,128)(2,1)S(1)}, bf16[32,3584]{1,0:T(8,128)(2,1)S(1)}, u32[]{:S(2)}, u32[]{:S(2)}) collective-permute-start(bf16[32,3584]{1,0:T(8,128)(2,1)S(1)} %add_convert_fusion), channel_id=1, source_target_pairs={{0,16},{1,17},{2,18},{3,19},{4,20},{5,21},{6,22},{7,23},{8,24},{9,... | collective-permute-start | bytes 688136 | tf_op jit(solution)/shard_map/ppermute | solution.py:215
  18.1 8.5 %collective-permute-start.6 = (bf16[32,3328]{1,0:T(8,128)(2,1)S(1)}, bf16[32,3328]{1,0:T(8,128)(2,1)S(1)}, u32[]{:S(2)}, u32[]{:S(2)}) collective-permute-start(bf16[32,3328]{1,0:T(8,128)(2,1)S(1)} %add_convert_fusion.1), channel_id=1, source_target_pairs={{0,96},{1,97},{2,98},{3,99},{4,100},{5,101},{6,102},{7,103},{8,104... | collective-permute-start | bytes 638984 | tf_op jit(solution)/shard_map/ppermute | solution.py:215
  21.0 6.9 %collective-permute-start.9 = (bf16[32,3072]{1,0:T(8,128)(2,1)S(1)}, bf16[32,3072]{1,0:T(8,128)(2,1)S(1)}, u32[]{:S(2)}, u32[]{:S(2)}) collective-permute-start(bf16[32,3072]{1,0:T(8,128)(2,1)S(1)} %add_convert_fusion.2), channel_id=1, source_target_pairs={{0,32},{1,33},{2,34},{3,35},{4,36},{5,37},{6,38},{7,39},{8,40},{9,... | collective-permute-start | bytes 589832 | tf_op jit(solution)/shard_map/ppermute | solution.py:215
  21.4 8.3 %collective-permute-start.11 = (bf16[32,2304]{1,0:T(8,128)(2,1)S(1)}, bf16[32,2304]{1,0:T(8,128)(2,1)S(1)}, u32[]{:S(2)}, u32[]{:S(2)}) collective-permute-start(bf16[32,2304]{1,0:T(8,128)(2,1)S(1)} %add_convert_fusion.3), channel_id=1, source_target_pairs={{0,96},{1,97},{2,98},{3,99},{4,100},{5,101},{6,102},{7,103},{8,104... | collective-permute-start | bytes 442376 | tf_op jit(solution)/shard_map/ppermute | solution.py:215
  25.0 6.5 %collective-permute-start.5 = (bf16[16,3584]{1,0:T(8,128)(2,1)S(1)}, bf16[16,3584]{1,0:T(8,128)(2,1)S(1)}, u32[]{:S(2)}, u32[]{:S(2)}) collective-permute-start(bf16[16,3584]{1,0:T(8,128)(2,1)S(1)} %add_convert_fusion.4), channel_id=1, source_target_pairs={{0,96},{1,97},{2,98},{3,99},{4,100},{5,101},{6,102},{7,103},{8,104... | collective-permute-start | bytes 344072 | tf_op jit(solution)/shard_map/ppermute | solution.py:215
  26.7 4.8 %collective-permute-start.7 = (bf16[16,3328]{1,0:T(8,128)(2,1)S(1)}, bf16[16,3328]{1,0:T(8,128)(2,1)S(1)}, u32[]{:S(2)}, u32[]{:S(2)}) collective-permute-start(bf16[16,3328]{1,0:T(8,128)(2,1)S(1)} %add_convert_fusion.5), channel_id=1, source_target_pairs={{0,32},{1,33},{2,34},{3,35},{4,36},{5,37},{6,38},{7,39},{8,40},{9,... | collective-permute-start | bytes 319496 | tf_op jit(solution)/shard_map/ppermute | solution.py:215
  28.0 6.2 %collective-permute-start.10 = (bf16[16,3072]{1,0:T(8,128)(2,1)S(1)}, bf16[16,3072]{1,0:T(8,128)(2,1)S(1)}, u32[]{:S(2)}, u32[]{:S(2)}) collective-permute-start(bf16[16,3072]{1,0:T(8,128)(2,1)S(1)} %add_convert_fusion.6), channel_id=1, source_target_pairs={{0,16},{1,17},{2,18},{3,19},{4,20},{5,21},{6,22},{7,23},{8,24},{9,... | collective-permute-start | bytes 294920 | tf_op jit(solution)/shard_map/ppermute | solution.py:215
  29.7 4.4 %collective-permute-start.12 = (bf16[16,2304]{1,0:T(8,128)(2,1)S(1)}, bf16[16,2304]{1,0:T(8,128)(2,1)S(1)}, u32[]{:S(2)}, u32[]{:S(2)}) collective-permute-start(bf16[16,2304]{1,0:T(8,128)(2,1)S(1)} %add_convert_fusion.7), channel_id=1, source_target_pairs={{0,16},{1,17},{2,18},{3,19},{4,20},{5,21},{6,22},{7,23},{8,24},{9,... | collective-permute-start | bytes 221192 | tf_op jit(solution)/shard_map/ppermute | solution.py:215
  34.5 1.4 %collective-permute-start.13 = (bf16[4,2,42,128]{3,2,1,0:T(8,128)(2,1)S(1)}, bf16[4,2,42,128]{3,2,1,0:T(8,128)(2,1)S(1)}, u32[]{:S(2)}, u32[]{:S(2)}) collective-permute-start(bf16[4,2,42,128]{3,2,1,0:T(8,128)(2,1)S(1)} %get-tuple-element.38), channel_id=1, source_target_pairs={{0,1},{1,0},{2,3},{3,2},{4,5},{5,4},{6,7},{7,6},{8,9},{9,8},{10,11... | collective-permute-start | bytes 258056 | tf_op jit(solution)/shard_map/ppermute | solution.py:215
  34.7 1.5 %collective-permute-start.8 = (bf16[4,2,54,128]{3,2,1,0:T(8,128)(2,1)S(1)}, bf16[4,2,54,128]{3,2,1,0:T(8,128)(2,1)S(1)}, u32[]{:S(2)}, u32[]{:S(2)}) collective-permute-start(bf16[4,2,54,128]{3,2,1,0:T(8,128)(2,1)S(1)} %get-tuple-element.32), channel_id=1, source_target_pairs={{0,1},{1,0},{2,3},{3,2},{4,5},{5,4},{6,7},{7,6},{8,9},{9,8},{10,11... | collective-permute-start | bytes 331784 | tf_op jit(solution)/shard_map/ppermute | solution.py:215
  36.3 5.9 %collective-permute-start.14 = (bf16[2,96,128]{2,1,0:T(8,128)(2,1)S(1)}, bf16[2,96,128]{2,1,0:T(8,128)(2,1)S(1)}, u32[]{:S(2)}, u32[]{:S(2)}) collective-permute-start(bf16[2,96,128]{2,1,0:T(8,128)(2,1)S(1)} %get-tuple-element.42), channel_id=1, source_target_pairs={{0,4},{1,3},{2,6},{3,1},{4,0},{5,7},{6,2},{7,5},{8,12},{9,11},{10,... | collective-permute-start | bytes 147464 | tf_op jit(solution)/shard_map/ppermute | solution.py:215
  39.6 4.1 %collective-permute-start.15 = (bf16[2,96,128]{2,1,0:T(8,128)(2,1)S(1)}, bf16[2,96,128]{2,1,0:T(8,128)(2,1)S(1)}, u32[]{:S(2)}, u32[]{:S(2)}) collective-permute-start(bf16[2,96,128]{2,1,0:T(8,128)(2,1)S(1)} %get-tuple-element.44), channel_id=1, source_target_pairs={{0,2},{1,7},{2,0},{3,5},{4,6},{5,3},{6,4},{7,1},{8,10},{9,15},{10,... | collective-permute-start | bytes 147464 | tf_op jit(solution)/shard_map/ppermute | solution.py:215
  40.2 5.3 %collective-permute-start.16 = (bf16[2,96,128]{2,1,0:T(8,128)(2,1)S(1)}, bf16[2,96,128]{2,1,0:T(8,128)(2,1)S(1)}, u32[]{:S(2)}, u32[]{:S(2)}) collective-permute-start(bf16[2,96,128]{2,1,0:T(8,128)(2,1)S(1)} %get-tuple-element.43), channel_id=1, source_target_pairs={{0,6},{1,5},{2,4},{3,7},{4,2},{5,1},{6,0},{7,3},{8,14},{9,13},{10,... | collective-permute-start | bytes 147464 | tf_op jit(solution)/shard_map/ppermute | solution.py:215
  45.6 5.6 %collective-permute-start.17 = (bf16[96,128]{1,0:T(8,128)(2,1)S(1)}, bf16[96,128]{1,0:T(8,128)(2,1)S(1)}, u32[]{:S(2)}, u32[]{:S(2)}) collective-permute-start(bf16[96,128]{1,0:T(8,128)(2,1)S(1)} %fusion.8), channel_id=1, source_target_pairs={{0,8},{1,9},{2,10},{3,11},{4,12},{5,13},{6,14},{7,15},{8,0},{9,1},... | collective-permute-start | bytes 73736 | tf_op jit(solution)/shard_map/ppermute | solution.py:215
